TPU v7x, 256 devices: a whole 4x4x8 slice. The times are simulated.
256 devices in a mesh: tm: 32 (over x, y, core), coef: 8 (over z).
Axes of the slice: x: 4, y: 4, z: 8, core: 2. Of those that a mesh axis runs over, the one named last changes fastest.
Arguments:
- design_lith: bfloat16 [34816, 32768], P('coef', 'tm'), may hold values from -0.03125 to 0.03125
- design_core: bfloat16 [440, 32768], P('coef', 'tm'), may hold values from -0.25 to 0.25
- sample_phase: float32 [32768], P('tm'), may hold values from 0 to 1
- data_weight: float32 [32768], P('tm'), may hold values from 0.1 to 1
- counts: int32 [256], P('tm'), may hold values from 1 to 128, as said below
- knot_index: int32 [256], P('tm'), may hold values from 0 to 255, as said below
- lith_damping: float32 [34816], P('coef'), may hold values from 0.3 to 3
- core_damping: float32 [440], P('coef'), may hold values from 0.3 to 3
- lith_solution: float32 [64, 34816], P(None, 'coef'), may hold values from -6 to 6
- lith_residual: float32 [64, 34816], P(None, 'coef'), may hold values from -6 to 6
- lith_direction: float32 [64, 34816], P(None, 'coef'), may hold values from -6 to 6
- core_solution: float32 [64, 440, 256], P(None, 'coef', 'tm'), may hold values from -6 to 6
- core_residual: float32 [64, 440, 256], P(None, 'coef', 'tm'), may hold values from -6 to 6
- core_direction: float32 [64, 440, 256], P(None, 'coef', 'tm'), may hold values from -6 to 6
Outputs:
- new_lith_solution: float32 [64, 34816], P(None, 'coef')
- new_lith_residual: float32 [64, 34816], P(None, 'coef')
- new_lith_direction: float32 [64, 34816], P(None, 'coef')
- new_core_solution: float32 [64, 440, 256], P(None, 'coef', 'tm')
- new_core_residual: float32 [64, 440, 256], P(None, 'coef', 'tm')
- new_core_direction: float32 [64, 440, 256], P(None, 'coef', 'tm')
Inputs may be any that keep to these rules, and one draw needn't show every extreme that they name: `counts`: quiet samples of a segment occupy its first slots; the rest are padding; some segment is full; the last segment of each index of tm holds at least 32 quiet samples. `knot_index`: segment g lies in a knot interval from (g // 8) * 8 to that plus 8 - 1; the first segment lies in the first interval, and the last segment of each index of tm in the last interval of its range.
All inputs are finite; a program needn't handle non-finite values.
Results may differ from a plain program's by a relative error of at most 0.0003.
Values sent between devices are 32-bit elements; how exact they have to be, the bound alone decides.
No kernel may reach another device: no remote copies, remote signals or barrier semaphores. Data moves between devices by JAX's collectives and lax.ppermute only.
A program may use at most 64 MiB of HBM per device.

v0:
```python
import jax
import jax.numpy as jnp
from jax import lax
from jax.sharding import PartitionSpec as P

SEG_ROWS = 128


def shifted(x, axis, by):
    peers = lax.axis_size(axis)
    pairs = [(i, i + by) for i in range(peers) if 0 <= i + by < peers]
    return lax.ppermute(x, axis, pairs)


def spline_values(fraction):
    basis_now = [jnp.ones_like(fraction)]
    for degree in range(1, 6):
        basis_next = []
        for s in range(degree + 1):
            lower_term = basis_now[s - 1] if s >= 1 else jnp.zeros_like(fraction)
            upper_term = basis_now[s] if s < degree else jnp.zeros_like(fraction)
            basis_next.append(
                ((fraction + (degree - s)) * lower_term + (s + 1 - fraction) * upper_term) / degree
            )
        basis_now = basis_next
    return jnp.stack(basis_now)


def split_two(values):
    high_part = lax.optimization_barrier(values.astype(jnp.bfloat16))
    low_part = (values - high_part.astype(jnp.float32)).astype(jnp.bfloat16)
    return jnp.concatenate([high_part, low_part], axis=0)


def shards(
    design_lith,
    design_core,
    sample_phase,
    data_weight,
    counts,
    knot_index,
    lith_damping,
    core_damping,
    lith_solution,
    lith_residual,
    lith_direction,
    core_solution,
    core_residual,
    core_direction,
):
    members = lith_direction.shape[0]
    sample_rows = design_lith.shape[1]
    spline_count = core_direction.shape[2]
    highest = lax.Precision.HIGHEST
    tm_index = lax.axis_index("tm")
    spline_basis = spline_values(sample_phase)
    positions = jnp.arange(sample_rows, dtype=jnp.int32)
    live_mask = (positions % SEG_ROWS < jnp.repeat(counts, SEG_ROWS)).astype(jnp.float32)
    weight = data_weight * live_mask
    local_knot = jnp.repeat(knot_index - tm_index * spline_count, SEG_ROWS)
    columns = jnp.arange(spline_count + 5, dtype=jnp.int32)[:, None]
    spline_weights = jnp.zeros((spline_count + 5, sample_rows), jnp.float32)
    for k in range(6):
        spline_weights = spline_weights + jnp.where(
            columns == (local_knot + k)[None, :], spline_basis[k][None, :], 0.0
        )
    design_small = design_core.astype(jnp.float32)
    upper_rows = shifted(core_direction[:, :, :5], "tm", -1)
    extended = jnp.concatenate([core_direction, upper_rows], axis=2)
    combined = jnp.einsum("vjr,ri->vji", extended, spline_weights, precision=highest)
    core_part = jnp.sum(combined * design_small[None], axis=1)
    lith_terms = jnp.dot(split_two(lith_direction), design_lith, preferred_element_type=jnp.float32)
    partial_value = lith_terms[:members] + lith_terms[members:] + core_part
    predicted = lax.psum(partial_value, "coef")
    residual = weight[None] * predicted
    grad_terms = lax.dot_general(
        split_two(residual),
        design_lith,
        (((1,), (1,)), ((), ())),
        preferred_element_type=jnp.float32,
    )
    grad_local = grad_terms[:members] + grad_terms[members:]
    weighted = residual[:, None, :] * design_small[None]
    grad_extended = jnp.einsum("vji,ri->vjr", weighted, spline_weights, precision=highest)
    lower_rows = shifted(grad_extended[:, :, spline_count:], "tm", 1)
    core_grad = grad_extended[:, :, :spline_count] + jnp.pad(
        lower_rows, ((0, 0), (0, 0), (0, spline_count - 5))
    )
    core_image = core_grad + core_damping[None, :, None] * core_direction
    summed = lax.psum(grad_local, "tm")
    lith_image = summed + lith_damping[None] * lith_direction
    count_once = (tm_index == 0).astype(jnp.float32)
    norm_part = count_once * jnp.sum(lith_residual * lith_residual, axis=1) + jnp.sum(
        core_residual * core_residual, axis=(1, 2)
    )
    curvature_part = count_once * jnp.sum(lith_direction * lith_image, axis=1) + jnp.sum(
        core_direction * core_image, axis=(1, 2)
    )
    norm_before, curvature = lax.psum((norm_part, curvature_part), ("tm", "coef"))
    step_size = norm_before / curvature
    next_lith_res = lith_residual - step_size[:, None] * lith_image
    next_core_res = core_residual - step_size[:, None, None] * core_image
    after_part = count_once * jnp.sum(next_lith_res * next_lith_res, axis=1) + jnp.sum(
        next_core_res * next_core_res, axis=(1, 2)
    )
    norm_after = lax.psum(after_part, ("tm", "coef"))
    conjugacy = norm_after / norm_before
    next_lith_sol = lith_solution + step_size[:, None] * lith_direction
    next_lith_dir = next_lith_res + conjugacy[:, None] * lith_direction
    next_core_sol = core_solution + step_size[:, None, None] * core_direction
    next_core_dir = next_core_res + conjugacy[:, None, None] * core_direction
    return (
        next_lith_sol,
        next_lith_res,
        next_lith_dir,
        next_core_sol,
        next_core_res,
        next_core_dir,
    )


def solution(mesh):
    return jax.shard_map(
        shards,
        mesh=mesh,
        in_specs=(
            P("coef", "tm"),
            P("coef", "tm"),
            P("tm"),
            P("tm"),
            P("tm"),
            P("tm"),
            P("coef"),
            P("coef"),
            P(None, "coef"),
            P(None, "coef"),
            P(None, "coef"),
            P(None, "coef", "tm"),
            P(None, "coef", "tm"),
            P(None, "coef", "tm"),
        ),
        out_specs=(
            P(None, "coef"),
            P(None, "coef"),
            P(None, "coef"),
            P(None, "coef", "tm"),
            P(None, "coef", "tm"),
            P(None, "coef", "tm"),
        ),
        check_vma=False,
    )
```

profile of v0, /device:TPU:1, one launch (start us, length us, event | category | flops | bytes accessed | tf_op | source)
XLA Modules:
  0.0 398.1 jit_solution(6662585375029629300)
XLA Ops:
  7.2 0.0 copy-start
  7.2 0.0 all-reduce.5.cloned.1.call-start
  7.2 5.3 %collective-permute-start = (f32[64,55,5]{0,2,1:T(8,128)}, f32[64,55,5]{0,2,1:T(8,128)S(1)}, u32[]{:S(2)}, u32[]{:S(2)}) collective-permute-start(f32[64,55,5]{0,2,1:T(8,128)} %bitcast.19), channel_id=1, source_target_pairs={{8,0},{16,8},{24,16},{32,24},{40,32},{48,40},{56,48},{64,56},{72,6... | collective-permute-start | bytes 211208 | tf_op jit(solution)/shard_map/ppermute | solution.py:12
  12.5 0.7 broadcast_subtract_fusion
  13.2 0.1 bitcast_add_fusion.4
  13.3 0.1 broadcast_bitcast_fusion
  13.3 0.7 fusion.25
  14.0 1.3 convert_element_type.28
  15.4 0.1 subtract_convert_fusion
  15.5 0.0 copy-start.2
  15.5 5.0 %fusion.4 = f32[128,1024]{1,0:T(8,128)S(1)} fusion(bf16[4352,1024]{1,0:T(8,128)(2,1)} %param.14, bf16[64,4352]{1,0:T(8,128)(2,1)S(1)} %subtract_convert_fusion, bf16[64,4352]{1,0:T(8,128)(2,1)S(1)} %convert_element_type.28), kind=kOutput, calls=%fused_computation.6 | convolution fusion | flops 1143078912 | bytes 10551296 | tf_op jit(solution)/shard_map/dot_general | solution.py:72
  20.5 0.0 copy-start.7
  20.5 0.0 copy-start.3
  20.6 0.2 multiply_reduce_fusion.3
  20.7 0.7 copy-done.7
  21.5 0.0 collective-permute-done
  21.5 0.1 copy-done.3
  21.5 12.1 %multiply_reduce_fusion = f32[64,1024]{1,0:T(8,128)S(1)} fusion(f32[55,1024]{1,0:T(8,128)S(1)} %convert_element_type.31, f32[64,55,5]{0,2,1:T(8,128)S(1)} %collective-permute-done, f32[64,55,8]{0,2,1:T(8,128)S(1)} %copy-done.3, f32[1024]{0:T(1024)S(1)} %get-tuple-element.20, s32[1024]{0:T(1024)S(1)} %get-tuple-element.23, f32[1024]{0:T(1024)S(1)} %get-tuple-element.19, ...), kind=kOutput, calls=%fused_computation.2 | convolution fusion | flops 569714368 | bytes 719616 | tf_op jit(solution)/shard_map/vjr,ri->vji/dot_general | solution.py:70
  33.6 0.0 copy-start.5
  33.6 0.0 copy-start.9
  33.6 0.0 copy-start.11
  33.6 0.8 fusion.11
  34.4 0.0 all-reduce.5.cloned.1.call-update
  34.4 0.0 all-reduce.7.cloned.1.call-start
  34.5 0.1 copy-done.5
  34.5 0.1 multiply_reduce_fusion.6
  34.6 0.1 fusion.32
  34.7 68.5 %all-reduce.5.cloned.1.call-done = f32[64,1024]{1,0:T(8,128)} async-done(((f32[64,1024]{1,0:T(8,128)}), f32[64,1024]{1,0:T(8,128)}) %all-reduce.5.cloned.1.call-update) | async-done | bytes 262160 | tf_op jit(solution)/shard_map/psum | solution.py:74
  103.2 1.0 fusion.38
  104.2 6.5 %fusion.12 = f32[128,4352]{1,0:T(8,128)S(1)} fusion(bf16[4352,1024]{1,0:T(8,128)(2,1)} %param.14, bf16[64,1024]{1,0:T(8,128)(2,1)S(1)} %subtract_convert_fusion.1, bf16[64,1024]{1,0:T(8,128)(2,1)S(1)} %get-tuple-element.12), kind=kOutput, calls=%fused_computation.23 | convolution fusion | flops 1141374976 | bytes 11403264 | tf_op jit(solution)/shard_map/dot_general | solution.py:76
  110.8 1.1 slice_add_fusion
  111.9 0.0 all-reduce.7.cloned.1.call-update
  111.9 0.0 copy-start.10
  111.9 49.2 %fusion = f32[64,55,13]{0,2,1:T(8,128)S(1)} fusion(f32[64,1024]{1,0:T(8,128)S(1)} %get-tuple-element.13, f32[55,1024]{1,0:T(8,128)S(1)} %convert_element_type.31, f32[1024]{0:T(1024)S(1)} %get-tuple-element.20, s32[1024]{0:T(1024)S(1)} %get-tuple-element.23, f32[1024]{0:T(1024)S(1)} %get-tuple-element.19, s32[1024]{0:T(1024)S(1)} %get-tuple-element.24, ...), kind=kOutput, calls=%fused_computation | convolution fusion | flops 566129664 | bytes 719616 | tf_op jit(solution)/shard_map/vji,ri->vjr/dot_general | solution.py:84
  161.1 0.0 copy-start.4
  161.1 0.0 copy-start.8
  161.2 8.2 %collective-permute-start.1 = (f32[64,55,5]{0,2,1:T(8,128)S(1)}, f32[64,55,5]{0,2,1:T(8,128)S(1)}, u32[]{:S(2)}, u32[]{:S(2)}) collective-permute-start(f32[64,55,5]{0,2,1:T(8,128)S(1)} %slice.33), channel_id=1, source_target_pairs={{0,8},{8,16},{16,24},{24,32},{32,40},{40,48},{48,56},{56,64},{64,7... | collective-permute-start | bytes 211208 | tf_op jit(solution)/shard_map/ppermute | solution.py:12
  169.4 2.9 collective-permute-done.1
  172.3 0.7 copy-done.6
  172.9 0.2 multiply_reduce_fusion.5
  173.1 57.1 %all-reduce.7.cloned.1.call-done = f32[64,4352]{1,0:T(8,128)} async-done(((f32[64,4352]{1,0:T(8,128)}), f32[64,4352]{1,0:T(8,128)}) %all-reduce.7.cloned.1.call-update) | async-done | bytes 1114128 | tf_op jit(solution)/shard_map/psum | solution.py:90
  230.2 1.5 multiply_reduce_fusion.2
  231.7 76.9 %all-reduce.1 = (f32[64]{0:T(128)S(1)}, f32[64]{0:T(128)S(1)}) all-reduce(f32[64]{0:T(128)S(1)} %multiply_add_fusion.8, f32[64]{0:T(128)S(1)} %multiply_add_fusion.7), channel_id=1, replica_groups=mesh['tm'=32,'coef'=8] {'tm','coef'}, use_global_device_ids=true, to_apply=%region_2.3 | all-reduce | flops 128 | bytes 1024 | tf_op jit(solution)/shard_map/psum | solution.py:99
  308.6 2.2 multiply_reduce_fusion.4
  310.8 3.1 multiply_reduce_fusion.1
  313.8 73.3 %psum.39 = f32[64]{0:T(128)S(1)} all-reduce(f32[64]{0:T(128)S(1)} %multiply_add_fusion.6), channel_id=1, replica_groups=mesh['tm'=32,'coef'=8] {'tm','coef'}, use_global_device_ids=true, to_apply=%region_11.12 | all-reduce | flops 64 | bytes 512 | tf_op jit(solution)/shard_map/psum | solution.py:106
  387.1 1.8 multiply_add_fusion.3
  388.9 2.4 multiply_add_fusion
  (18 shorter events, 0.1 us)
Async XLA Ops:
  7.2 8.2 %copy-start = (f32[64,4352]{1,0:T(8,128)S(1)}, f32[64,4352]{1,0:T(8,128)}, u32[]{:S(2)}) copy-start(f32[64,4352]{1,0:T(8,128)} %param.24) | copy-start | bytes 3342340
  7.2 96.0 %all-reduce.5.cloned.1.call-start = ((), (), s32[]{:S(2)}) async-start(), calls=%async_computation | async-start | bytes 524288 | tf_op jit(solution)/shard_map/psum | solution.py:74
  7.2 14.2 %collective-permute-start = (f32[64,55,5]{0,2,1:T(8,128)}, f32[64,55,5]{0,2,1:T(8,128)S(1)}, u32[]{:S(2)}, u32[]{:S(2)}) collective-permute-start(f32[64,55,5]{0,2,1:T(8,128)} %bitcast.19), channel_id=1, source_target_pairs={{8,0},{16,8},{24,16},{32,24},{40,32},{48,40},{56,48},{64,56},{72,6... | collective-permute-start | bytes 211208 | tf_op jit(solution)/shard_map/ppermute | solution.py:12
  15.5 5.0 %copy-start.2 = (f32[64,4352]{1,0:T(8,128)S(1)}, f32[64,4352]{1,0:T(8,128)}, u32[]{:S(2)}) copy-start(f32[64,4352]{1,0:T(8,128)} %param.23) | copy-start | bytes 3342340
  20.5 0.9 copy-start.7
  20.5 1.0 copy-start.3
  33.6 0.9 copy-start.5
  33.6 1.0 copy-start.9
  33.6 1.0 copy-start.11
  34.4 195.8 %all-reduce.7.cloned.1.call-start = ((), (), s32[]{:S(2)}) async-start(), calls=%async_computation.1 | async-start | bytes 2228224 | tf_op jit(solution)/shard_map/psum | solution.py:90
  111.9 61.0 %copy-start.10 = (f32[55]{0:T(128)S(1)}, f32[55]{0:T(128)}, u32[]{:S(2)}) copy-start(f32[55]{0:T(128)} %param.21) | copy-start | bytes 664
  161.1 11.1 %copy-start.4 = (f32[64,55,13]{0,2,1:T(8,128)}, f32[64,55,13]{0,2,1:T(8,128)S(1)}, u32[]{:S(2)}) copy-start(f32[64,55,13]{0,2,1:T(8,128)S(1)} %fusion) | copy-start | bytes 549124
  161.1 69.1 %copy-start.8 = (f32[4352]{0:T(1024)S(1)}, f32[4352]{0:T(1024)}, u32[]{:S(2)}) copy-start(f32[4352]{0:T(1024)} %param.20) | copy-start | bytes 52228
  161.2 11.1 %collective-permute-start.1 = (f32[64,55,5]{0,2,1:T(8,128)S(1)}, f32[64,55,5]{0,2,1:T(8,128)S(1)}, u32[]{:S(2)}, u32[]{:S(2)}) collective-permute-start(f32[64,55,5]{0,2,1:T(8,128)S(1)} %slice.33), channel_id=1, source_target_pairs={{0,8},{8,16},{16,24},{24,32},{32,40},{40,48},{48,56},{56,64},{64,7... | collective-permute-start | bytes 211208 | tf_op jit(solution)/shard_map/ppermute | solution.py:12
  172.3 0.7 copy-start.6
  231.7 79.1 %copy-start.1 = (f32[64,4352]{1,0:T(8,128)S(1)}, f32[64,4352]{1,0:T(8,128)}, u32[]{:S(2)}) copy-start(f32[64,4352]{1,0:T(8,128)} %all-reduce.7.cloned.1.call-done) | copy-start | bytes 3342340
Sparse Core Ops, SparseCore 0:
  34.5 68.6 all-reduce.4
  112.0 118.1 all-reduce.6
where the time goes:
time: 399 us; the launch traced here: 398 us
  blocking collectives  150 us (38%)
  waiting for transfers between devices  129 us (32%)
  matrix products  72.8 us (18%)
  other arithmetic  17.1 us (4%)
  between operations  14.3 us (4%)
  starting transfers between devices  13.5 us (3%)
    psum x1, blocking collectives, shards(): lax.psum((norm_part, curvature_part), ('tm', 'coef'))  76.9 us
    psum x1, blocking collectives, shards(): norm_after = lax.psum(after_part, ('tm', 'coef'))  73.3 us
    psum x1, waiting for transfers between devices, shards(): predicted = lax.psum(partial_value, 'coef')  68.5 us
    psum x1, waiting for transfers between devices, shards(): summed = lax.psum(grad_local, 'tm')  57.1 us
    dot_general x1, matrix products, shards(): jnp.einsum('vji,ri->vjr', weighted, spline_weights, precision=highest)  49.2 us
    ppermute x2, starting transfers between devices, shifted(): return lax.ppermute(x, axis, pairs)  13.5 us
    dot_general x1, matrix products, shards(): jnp.einsum('vjr,ri->vji', extended, spline_weights, precision=highest)  12.1 us
  transfers between devices with their start and end apart: 4, of which 3 were waited for; matrix products, arithmetic and copies ran while one was open for 14% of the time, Pallas kernels for 0%

commit v1 on v0

v1 whole, which is shorter than its diff:
```python
import jax
import jax.numpy as jnp
from jax import lax
from jax.experimental import pallas as pl
from jax.experimental.pallas import tpu as pltpu
from jax.sharding import PartitionSpec as P

NL, NS, MEM, NJ, JP = 4352, 1024, 64, 55, 56
SEG = 128
WIDE = 1152
MIB = 1 << 20
F32, BF16 = jnp.float32, jnp.bfloat16
VM = pl.BlockSpec(memory_space=pltpu.VMEM)
SM = pl.BlockSpec(memory_space=pltpu.SMEM)
ANY = pl.BlockSpec(memory_space=pl.ANY)
FORWARD_CUTS = (0, 512, 1536, 2560, 3584, 4352)
BACK_CUTS = (0, 512, 1536, 2560, 3584, 4352)
TRANS_B = (((1,), (1,)), ((), ()))


def params(mib):
    return pltpu.CompilerParams(vmem_limit_bytes=mib * MIB)


def struct(shape, dtype=F32):
    return jax.ShapeDtypeStruct(shape, dtype)


def split(values):
    high = values.astype(BF16)
    return high, (values - high.astype(F32)).astype(BF16)


def row_blocks(a_hbm, a_buf, sems, cuts):
    copies = []
    for b in range(len(cuts) - 1):
        rows = pl.ds(cuts[b], cuts[b + 1] - cuts[b])
        copy = pltpu.make_async_copy(a_hbm.at[rows], a_buf.at[rows], sems.at[b])
        copy.start()
        copies.append(copy)
    return copies


def forward_kernel(dir_ref, a_hbm, out_ref, a_buf, lhs, acc, sems):
    copies = row_blocks(a_hbm, a_buf, sems, FORWARD_CUTS)
    high, low = split(dir_ref[...])
    lhs[0:MEM] = high
    lhs[MEM:] = low
    for b, copy in enumerate(copies):
        lo, hi = FORWARD_CUTS[b], FORWARD_CUTS[b + 1]
        copy.wait()
        part = jnp.dot(lhs[:, lo:hi], a_buf[lo:hi], preferred_element_type=F32)
        if b == 0:
            acc[...] = part
        else:
            acc[...] += part
    out_ref[...] = acc[0:MEM] + acc[MEM:]


def spline_values(u):
    now = [jnp.ones_like(u)]
    for d in range(1, 6):
        later = []
        for s in range(d + 1):
            term = 0.0
            if s >= 1:
                term = (u + float(d - s)) * now[s - 1]
            if s < d:
                term = term + (float(s + 1) - u) * now[s]
            later.append(term * (1.0 / d))
        now = later
    return now


def columns_to_rows(cols):
    lane = lax.broadcasted_iota(jnp.int32, (MEM, 128), 1)
    square = jnp.zeros((MEM, 128), F32)
    for k, col in enumerate(cols):
        square = jnp.where(lane == k, col, square)
    square = jnp.concatenate([square, jnp.zeros((128 - MEM, 128), F32)], axis=0)
    return jnp.transpose(square)[0:8]


def core_forward_kernel(
    lith_ref, dir_ref, res_ref, damp_ref, cdir_ref, halo_ref, cres_ref, design_ref, phase_ref,
    knot_ref, cdamp_ref, out_ref, ghi_ref, glo_ref, basis, design, ext,
):
    values = spline_values(phase_ref[...])
    row = lax.broadcasted_iota(jnp.int32, (16, SEG), 0)
    for g in range(8):
        first = lax.rem(knot_ref[g], 8)
        block = jnp.zeros((16, SEG), F32)
        for k in range(6):
            block = block + jnp.where(row == first + k, values[k][g : g + 1, :], 0.0)
        basis[:, g * SEG : (g + 1) * SEG] = block
    design[0:NJ] = design_ref[...].astype(F32)
    design[NJ:JP] = jnp.zeros((1, NS), F32)

    def build(j, carry):
        product = basis[...] * design[pl.ds(j, 1), :]
        high, low = split(product)
        rows = pl.ds(pl.multiple_of(j * 16, 16), 16)
        ghi_ref[rows, :] = high
        glo_ref[rows, :] = low
        return carry

    lax.fori_loop(0, JP, build, 0)
    ext[0:NJ, 0:8, :] = cdir_ref[...]
    ext[0:NJ, 8:16, :] = halo_ref[...]
    ext[NJ:JP] = jnp.zeros((1, 16, MEM), F32)
    high, low = split(jnp.transpose(ext[...].reshape(JP * 16, MEM)))
    both = jnp.concatenate([high, low], axis=0)
    wide = jnp.dot(both, ghi_ref[...], preferred_element_type=F32)
    value = wide[0:MEM] + wide[MEM:] + jnp.dot(high, glo_ref[...], preferred_element_type=F32)
    value = value + lith_ref[...]
    out_ref[...] = jnp.zeros_like(out_ref)
    out_ref[:, :, 0:NS] = value.reshape(8, 8, NS)
    norm = jnp.zeros((8, MEM), F32)
    damped = jnp.zeros((8, MEM), F32)
    for j in range(NJ):
        norm = norm + cres_ref[j] * cres_ref[j]
        damped = damped + cdamp_ref[j] * (cdir_ref[j] * cdir_ref[j])
    lith_norm = jnp.sum(res_ref[...] * res_ref[...], axis=1, keepdims=True)
    lith_damped = jnp.sum(dir_ref[...] * dir_ref[...] * damp_ref[...], axis=1, keepdims=True)
    rows = columns_to_rows([jnp.zeros_like(lith_norm)] * 2 + [lith_norm, lith_damped])
    out_ref[0, :, NS:] = rows
    out_ref[0, 0:1, NS : NS + MEM] = jnp.sum(norm, axis=0, keepdims=True)
    out_ref[0, 1:2, NS : NS + MEM] = jnp.sum(damped, axis=0, keepdims=True)


def core_back_kernel(
    field_ref, weight_ref, ghi_ref, glo_ref, count_ref, pair_ref, local_ref, halo_ref, tile_ref
):
    lane = lax.broadcasted_iota(jnp.int32, (1, SEG), 1)
    curve = jnp.zeros((MEM, SEG), F32)
    for g in range(8):
        cols = slice(g * SEG, (g + 1) * SEG)
        weight = jnp.where(lane < count_ref[g], weight_ref[g : g + 1, :], 0.0)
        field = field_ref[:, :, cols].reshape(MEM, SEG)
        residual = field * weight
        curve = curve + residual * field
        high, low = split(residual)
        pair_ref[0:MEM, cols] = high
        pair_ref[MEM:, cols] = low
    rows = columns_to_rows(
        [jnp.zeros((MEM, 1), F32), jnp.sum(curve, axis=1, keepdims=True)]
    )
    tile_ref[...] = field_ref[0, :, NS:] + rows
    wide = lax.dot_general(ghi_ref[...], pair_ref[...], TRANS_B, preferred_element_type=F32)
    low = lax.dot_general(
        glo_ref[...], pair_ref[0:MEM], TRANS_B, preferred_element_type=F32
    )
    grad = (wide[:, 0:MEM] + wide[:, MEM:] + low).reshape(JP, 16, MEM)
    local_ref[...] = grad[0:NJ, 0:8, :]
    halo_ref[...] = grad[0:NJ, 8:16, :]


def back_kernel(core_ref, pair_ref, a_hbm, own_ref, other_ref, a_buf, lhs, sems):
    copies = row_blocks(a_hbm, a_buf, sems, BACK_CUTS)
    half = MEM // 2
    mine = pl.multiple_of(core_ref[0] * half, half)
    theirs = pl.multiple_of((1 - core_ref[0]) * half, half)
    for k, start in enumerate((mine, theirs, MEM + mine, MEM + theirs)):
        lhs[k * half : (k + 1) * half] = pair_ref[pl.ds(pl.multiple_of(start, half), half), :]
    for out in (own_ref, other_ref):
        out[:, 3, :, NL - 3 * WIDE :] = jnp.zeros((4, 8, 4 * WIDE - NL), F32)
    for b, copy in enumerate(copies):
        lo, hi = BACK_CUTS[b], BACK_CUTS[b + 1]
        copy.wait()
        part = lax.dot_general(lhs[...], a_buf[lo:hi], TRANS_B, preferred_element_type=F32)
        part = part[0:MEM] + part[MEM:]
        edges = sorted({lo, hi} | {e for e in (WIDE, 2 * WIDE, 3 * WIDE) if lo < e < hi})
        for left, right in zip(edges, edges[1:]):
            y = left // WIDE
            place = slice(left - y * WIDE, right - y * WIDE)
            piece = part[:, left - lo : right - lo]
            own_ref[:, y, :, place] = piece[0:half].reshape(4, 8, right - left)
            other_ref[:, y, :, place] = piece[half:].reshape(4, 8, right - left)


def image_kernel(
    own_ref, got_ref, local_ref, halo_ref, cdir_ref, cres_ref, tile_ref, cdamp_ref, out_ref, image_ref
):
    out_ref[...] = own_ref[...] + got_ref[...]
    cross = jnp.zeros((8, MEM), F32)
    square = jnp.zeros((8, MEM), F32)
    for j in range(NJ):
        image = local_ref[j] + halo_ref[j] + cdamp_ref[j] * cdir_ref[j]
        image_ref[j] = image
        cross = cross + cres_ref[j] * image
        square = square + image * image
    out_ref[0, 3, :, NS:] = tile_ref[...]
    out_ref[0, 3, 2:3, NS : NS + MEM] = jnp.sum(cross, axis=0, keepdims=True)
    out_ref[0, 3, 3:4, NS : NS + MEM] = jnp.sum(square, axis=0, keepdims=True)


def turned(row):
    return jnp.transpose(jnp.broadcast_to(row, (128, 128)))


def update_kernel(
    core_ref, own_ref, got_ref, tile_ref, damp_ref, sol_ref, res_ref, dir_ref,
    cimage_ref, csol_ref, cres_ref, cdir_ref,
    new_sol_ref, new_res_ref, new_csol_ref, new_cres_ref, norm_ref, keep_ref, step_col, norm_col,
):
    rt = pl.program_id(0)

    @pl.when(rt == 0)
    def _():
        total = own_ref[0, 3, :, NS:] + got_ref[0, 3, :, NS:]
        before = total[0:1] + tile_ref[2:3]
        curvature = total[1:2] + tile_ref[3:4]
        live = lax.broadcasted_iota(jnp.int32, (1, 128), 1) < MEM
        step = before / jnp.where(live, curvature, 1.0)
        step_col[...] = turned(step)
        keep_ref[0:1] = before
        keep_ref[1:2] = total[0:1]
        keep_ref[2:3] = step * (step * total[3:4] - 2.0 * total[2:3])
        keep_ref[3:8] = jnp.zeros((5, 128), F32)
        step = step[:, 0:MEM]
        for j in range(NJ):
            new_csol_ref[j] = csol_ref[j] + step * cdir_ref[j]
            new_cres_ref[j] = cres_ref[j] - step * cimage_ref[j]

    x = lax.rem(rt, 4)
    step = step_col[pl.ds(pl.multiple_of(rt * 8, 8), 8), 0:1]

    def work(ref):
        image = jnp.concatenate([ref[x, y] for y in range(4)], axis=1)[:, 0:NL]
        direction = dir_ref[...]
        image = image + damp_ref[...] * direction
        new_sol_ref[...] = sol_ref[...] + step * direction
        new_res = res_ref[...] - step * image
        new_res_ref[...] = new_res
        norm = jnp.sum(new_res * new_res, axis=1, keepdims=True)
        norm_col[pl.ds(pl.multiple_of(rt * 8, 8), 8), :] = jnp.broadcast_to(norm, (8, 128))

    mine = rt // 4 == core_ref[0]
    pl.when(mine)(lambda: work(own_ref))
    pl.when(jnp.logical_not(mine))(lambda: work(got_ref))

    @pl.when(rt == 7)
    def _():
        column = jnp.concatenate([norm_col[0:MEM], jnp.zeros((128 - MEM, 128), F32)], axis=0)
        row = jnp.transpose(column)[0:1] + keep_ref[2:3]
        norm_ref[...] = jnp.broadcast_to(row[None], (8, 8, 128))


def direction_kernel(
    norm_ref, keep_ref, res_ref, dir_ref, cres_ref, cdir_ref, new_dir_ref, new_cdir_ref, col
):
    rt = pl.program_id(0)

    @pl.when(rt == 0)
    def _():
        after = norm_ref[0, 0:1]
        for k in range(1, 8):
            after = after + norm_ref[k, 0:1]
        live = lax.broadcasted_iota(jnp.int32, (1, 128), 1) < MEM
        ratio = (after + keep_ref[1:2]) / jnp.where(live, keep_ref[0:1], 1.0)
        col[...] = turned(ratio)
        ratio = ratio[:, 0:MEM]
        for j in range(NJ):
            new_cdir_ref[j] = cres_ref[j] + ratio * cdir_ref[j]

    scale = col[pl.ds(pl.multiple_of(rt * 8, 8), 8), 0:1]
    new_dir_ref[...] = res_ref[...] + scale * dir_ref[...]


def full(shape):
    return pl.BlockSpec(shape, lambda i: (0,) * len(shape))


def shards(
    design_lith, design_core, sample_phase, data_weight, counts, knot_index, lith_damping, core_damping,
    lith_solution, lith_residual, lith_direction, core_solution, core_residual, core_direction,
):
    tm = lax.axis_size("tm")
    core = lax.rem(lax.axis_index("tm"), 2).reshape(1)
    planes = [[t for t in range(tm) if t % 2 == c] for c in range(2)]
    swap = [(t, t ^ 1) for t in range(tm)]
    csol, cres, cdir = (
        jnp.transpose(v, (1, 2, 0)) for v in (core_solution, core_residual, core_direction)
    )
    phase = sample_phase.reshape(8, SEG)
    weight = data_weight.reshape(8, SEG)
    damp = lith_damping.reshape(1, NL)
    upper = lax.ppermute(cdir, "tm", [(t, t - 1) for t in range(1, tm)])

    lith = pl.pallas_call(
        forward_kernel,
        out_shape=struct((MEM, NS)),
        in_specs=[VM, ANY],
        out_specs=VM,
        scratch_shapes=[
            pltpu.VMEM((NL, NS), BF16),
            pltpu.VMEM((2 * MEM, NL), BF16),
            pltpu.VMEM((2 * MEM, NS), F32),
            pltpu.SemaphoreType.DMA((len(FORWARD_CUTS) - 1,)),
        ],
        compiler_params=params(20),
        cost_estimate=pl.CostEstimate(flops=4 * MEM * NL * NS, bytes_accessed=10 * MIB, transcendentals=0),
        name="forward",
    )(lith_direction, design_lith)

    partial, ghi, glo = pl.pallas_call(
        core_forward_kernel,
        out_shape=(struct((8, 8, WIDE)), struct((JP * 16, NS), BF16), struct((JP * 16, NS), BF16)),
        in_specs=[VM] * 9 + [SM] * 2,
        out_specs=(VM, VM, VM),
        scratch_shapes=[
            pltpu.VMEM((16, NS), F32),
            pltpu.VMEM((JP, NS), F32),
            pltpu.VMEM((JP, 16, MEM), F32),
        ],
        compiler_params=params(16),
        name="core_forward",
    )(
        lith, lith_direction, lith_residual, damp, cdir, upper, cres, design_core, phase,
        knot_index, core_damping,
    )

    parts = lax.all_to_all(partial, "coef", 0, 0)
    field = lax.all_to_all(
        jnp.broadcast_to(jnp.sum(parts, axis=0)[None], (8, 8, WIDE)), "coef", 0, 0
    )

    pair, local, halo, tile = pl.pallas_call(
        core_back_kernel,
        out_shape=(
            struct((2 * MEM, NS), BF16),
            struct((NJ, 8, MEM)),
            struct((NJ, 8, MEM)),
            struct((8, 128)),
        ),
        in_specs=[VM] * 4 + [SM],
        out_specs=(VM,) * 4,
        compiler_params=params(16),
        name="core_back",
    )(field, weight, ghi, glo, counts)
    lower = lax.ppermute(halo, "tm", [(t, t + 1) for t in range(tm - 1)])

    own, other = pl.pallas_call(
        back_kernel,
        out_shape=(struct((4, 4, 8, WIDE)), struct((4, 4, 8, WIDE))),
        in_specs=[SM, VM, ANY],
        out_specs=(VM, VM),
        scratch_shapes=[
            pltpu.VMEM((NL, NS), BF16),
            pltpu.VMEM((2 * MEM, NS), BF16),
            pltpu.SemaphoreType.DMA((len(BACK_CUTS) - 1,)),
        ],
        compiler_params=params(20),
        cost_estimate=pl.CostEstimate(flops=4 * MEM * NL * NS, bytes_accessed=10 * MIB, transcendentals=0),
        name="back",
    )(core, pair, design_lith)
    got = lax.ppermute(other, "tm", swap)

    terms, cimage = pl.pallas_call(
        image_kernel,
        out_shape=(struct((4, 4, 8, WIDE)), struct((NJ, 8, MEM))),
        in_specs=[VM] * 7 + [SM],
        out_specs=(VM, VM),
        compiler_params=params(12),
        name="image",
    )(own, got, local, lower, cdir, cres, tile, core_damping)

    pieces = lax.all_to_all(
        terms.reshape(16, 8, WIDE), "tm", 0, 0, axis_index_groups=planes
    )
    whole = lax.all_to_all(
        jnp.broadcast_to(jnp.sum(pieces, axis=0)[None], (16, 8, WIDE)),
        "tm", 0, 0, axis_index_groups=planes,
    ).reshape(4, 4, 8, WIDE)
    rest = lax.ppermute(whole, "tm", swap)

    lith_block = pl.BlockSpec((8, NL), lambda i: (i, 0))
    core_full = full((NJ, 8, MEM))
    chunk_full = full((4, 4, 8, WIDE))
    lith_struct = struct((MEM, NL))
    core_struct = struct((NJ, 8, MEM))
    z_tile = field[0, :, NS:]
    new_sol, new_res, new_csol, new_cres, norms, keep = pl.pallas_call(
        update_kernel,
        grid=(8,),
        out_shape=(
            lith_struct, lith_struct, core_struct, core_struct, struct((8, 8, 128)), struct((8, 128))
        ),
        in_specs=[SM, chunk_full, chunk_full, full((8, 128)), full((1, NL))]
        + [lith_block] * 3
        + [core_full] * 4,
        out_specs=(lith_block, lith_block, core_full, core_full, full((8, 8, 128)), full((8, 128))),
        scratch_shapes=[pltpu.VMEM((128, 128), F32), pltpu.VMEM((128, 128), F32)],
        compiler_params=params(16),
        name="update",
    )(
        core, whole, rest, z_tile, damp, lith_solution, lith_residual, lith_direction,
        cimage, csol, cres, cdir,
    )
    norms = lax.all_to_all(norms, "coef", 0, 0)
    new_dir, new_cdir = pl.pallas_call(
        direction_kernel,
        grid=(8,),
        out_shape=(lith_struct, core_struct),
        in_specs=[full((8, 8, 128)), full((8, 128)), lith_block, lith_block, core_full, core_full],
        out_specs=(lith_block, core_full),
        scratch_shapes=[pltpu.VMEM((128, 128), F32)],
        compiler_params=params(12),
        name="direction",
    )(norms, keep, new_res, lith_direction, new_cres, cdir)
    back = lambda v: jnp.transpose(v, (2, 0, 1))
    return new_sol, new_res, new_dir, back(new_csol), back(new_cres), back(new_cdir)


def solution(mesh):
    lith, core = P(None, "coef"), P(None, "coef", "tm")
    return jax.shard_map(
        shards,
        mesh=mesh,
        in_specs=(
            P("coef", "tm"), P("coef", "tm"), P("tm"), P("tm"), P("tm"), P("tm"), P("coef"), P("coef"),
            lith, lith, lith, core, core, core,
        ),
        out_specs=(lith, lith, lith, core, core, core),
        check_vma=False,
    )
```

time: 399 us -> 131 us (0.33)
  waiting for transfers between devices: 129 us -> 17.5 us
  blocking collectives: 150 us -> 58.4 us
  matrix products: 72.8 us -> 0 us
  Pallas kernels: 0 us -> 19.3 us
  other arithmetic: 17.1 us -> 1.17 us
  local copies, waits for them, and re-layouts: 1.65 us -> 17.5 us
  between operations: 14.3 us -> 0.85 us
    psum x2 -> x0, blocking collectives: 150 us -> none  [the longest x1 76.9 us: shards(): lax.psum((norm_part, curvature_part), ('tm', 'coef'))]
    psum x2 -> x0, waiting for transfers between devices: 126 us -> none  [the longest x1 68.5 us: shards(): predicted = lax.psum(partial_value, 'coef')]
    dot_general x4 -> x0, matrix products: 72.8 us -> none  [the longest x1 49.2 us: shards(): jnp.einsum('vji,ri->vjr', weighted, spline_weights, precision=highest)]
    all_to_all x0 -> x4, blocking collectives: none -> 58.4 us  [the longest x1 19.5 us: shards(): parts = lax.all_to_all(partial, 'coef', 0, 0)]
    pallas_call x0 -> x7, Pallas kernels: none -> 19.3 us  [the longest x1 4.46 us: shards(): pl.pallas_call(back_kernel, out_shape=(struct((4, 4, 8, WIDE)), struct((4...]
    unnamed x24 -> x42, local copies, waits for them, and re-layouts: 1.57 us -> 16 us
    all_to_all x0 -> x1, waiting for transfers between devices: none -> 13 us  [shards(): lax.all_to_all(jnp.broadcast_to(jnp.sum(parts, axis=0)[None], (8, 8, WIDE...]
    add x8 -> x0, other arithmetic: 6.12 us -> none  [the longest x1 2.41 us: shards(): next_lith_dir = next_lith_res + conjugacy[:, None] * lith_direction]
  transfers between devices with their start and end apart: 4 -> 5, of which waited for: 3 -> 3; matrix products, arithmetic and copies ran while one was open for 14% -> 1% of each run, Pallas kernels for 0% -> 2%
where the time goes in v1:
time: 131 us; the launch traced here: 130 us
  blocking collectives  58.4 us (45%)
  Pallas kernels  19.3 us (15%)
  local copies, waits for them, and re-layouts  17.5 us (13%)
  waiting for transfers between devices  17.5 us (13%)
  starting transfers between devices  15.7 us (12%)
    all_to_all x1, blocking collectives, shards(): parts = lax.all_to_all(partial, 'coef', 0, 0)  19.5 us
    all_to_all x1, blocking collectives, shards(): lax.all_to_all(terms.reshape(16, 8, WIDE), 'tm', 0, 0, axis_index_groups=...  16.9 us
    unnamed x42, local copies, waits for them, and re-layouts  16 us
    all_to_all x1, waiting for transfers between devices, shards(): lax.all_to_all(jnp.broadcast_to(jnp.sum(parts, axis=0)[None], (8, 8, WIDE...  13 us
    all_to_all x1, blocking collectives, shards(): lax.all_to_all(jnp.broadcast_to(jnp.sum(pieces, axis=0)[None], (16, 8, WI...  12.8 us
    all_to_all x1, blocking collectives, shards(): norms = lax.all_to_all(norms, 'coef', 0, 0)  9.23 us
    ppermute x1, starting transfers between devices, shards(): upper = lax.ppermute(cdir, 'tm', [(t, t - 1) for t in range(1, tm)])  5.15 us
    pallas_call x1, Pallas kernels, shards(): pl.pallas_call(back_kernel, out_shape=(struct((4, 4, 8, WIDE)), struct((4...  4.46 us
  transfers between devices with their start and end apart: 5, of which 3 were waited for; matrix products, arithmetic and copies ran while one was open for 1% of the time, Pallas kernels for 2%

profile of v1, /device:TPU:1, one launch (start us, length us, event | category | flops | bytes accessed | tf_op | source)
XLA Modules:
  0.0 130.4 jit_solution(11373621402381316991)
XLA Ops:
  0.6 5.2 %collective-permute-start = (f32[55,8,64]{2,1,0:T(8,128)}, f32[55,8,64]{2,1,0:T(8,128)S(1)}, u32[]{:S(2)}, u32[]{:S(2)}) collective-permute-start(f32[55,8,64]{2,1,0:T(8,128)} %bitcast.13), channel_id=1, source_target_pairs={{8,0},{16,8},{24,16},{32,24},{40,32},{48,40},{56,48},{64,56},{72,6... | collective-permute-start | bytes 337928 | tf_op jit(solution)/shard_map/ppermute | solution.py:288
  5.8 0.7 reshape.33.damp_ref
  6.5 0.0 copy-start
  6.5 3.5 %copy-done = bf16[4352,1024]{1,0:T(8,128)(2,1)S(1)} copy-done((bf16[4352,1024]{1,0:T(8,128)(2,1)S(1)}, bf16[4352,1024]{1,0:T(8,128)(2,1)}, u32[]{:S(2)}) %copy-start) | copy-done | bytes 8912920
  10.1 1.2 copy-done.2
  11.3 0.0 copy-start.15
  11.3 0.0 copy-start.16
  11.4 0.0 copy-start.18
  11.4 0.0 copy-start.20
  11.4 2.4 %forward.1.lith_ref = f32[64,1024]{1,0:T(8,128)S(1)} custom-call(f32[64,4352]{1,0:T(8,128)S(1)} %copy-done.2, bf16[4352,1024]{1,0:T(8,128)(2,1)S(1)} %copy-done), custom_call_target="tpu_custom_call" | custom-call | flops 1140850688 | bytes 10485760 | tf_op jit(solution)/shard_map/forward/pallas_call | solution.py:290
  13.8 0.0 collective-permute-done.halo_ref
  13.8 0.0 copy-done.3
  13.8 0.0 copy-done.4
  13.8 0.0 copy-done.5
  13.8 0.0 copy-done.6
  13.8 0.0 copy-done.15
  13.9 0.0 copy-done.16
  13.9 0.0 copy-done.18
  13.9 0.0 copy-done.20
  13.9 2.6 %core_forward.1 = (f32[8,8,1152]{2,1,0:T(8,128)S(1)}, bf16[896,1024]{1,0:T(8,128)(2,1)S(1)}, bf16[896,1024]{1,0:T(8,128)(2,1)S(1)}) custom-call(f32[64,1024]{1,0:T(8,128)S(1)} %forward.1.lith_ref, f32[64,4352]{1,0:T(8,128)S(1)} %copy-done.3, f32[64,4352]{1,0:T(8,128)S(1)} %copy-done.4, f32[1,4352]{1,0:T(1,128)S(1)} %reshape.33.damp_ref, ...), custom_call_target="tpu_custom_call" | custom-call | tf_op jit(solution)/shard_map/core_forward/pallas_call | solution.py:306
  16.5 1.3 copy-done.7
  17.7 1.2 copy-done.9
  18.9 19.5 %all_to_all.25 = f32[8,8,1152]{2,1,0:T(8,128)S(1)} all-to-all(f32[8,8,1152]{2,1,0:T(8,128)S(1)} %get-tuple-element.25), channel_id=1, replica_groups=mesh['tm'=32,'coef'=8] {'coef'}, dimensions={0} | all-to-all | bytes 589824 | tf_op jit(solution)/shard_map/all_to_all | solution.py:323
  38.5 0.7 broadcast_in_dim.4
  39.2 3.4 %all-to-all-start.1 = ((f32[8,8,1152]{2,1,0:T(8,128)}), f32[8,8,1152]{2,1,0:T(8,128)S(1)}, u32[]{:S(2)}, u32[]{:S(2)}) async-start(f32[8,8,1152]{2,1,0:T(8,128)} %broadcast_in_dim.4), calls=%async_computation.1 | async-start | bytes 589824 | tf_op jit(solution)/shard_map/all_to_all | solution.py:324
  42.6 13.0 %all-to-all-done.1.field_ref = f32[8,8,1152]{2,1,0:T(8,128)S(1)} async-done(((f32[8,8,1152]{2,1,0:T(8,128)}), f32[8,8,1152]{2,1,0:T(8,128)S(1)}, u32[]{:S(2)}, u32[]{:S(2)}) %all-to-all-start.1) | async-done | bytes 294944 | tf_op jit(solution)/shard_map/all_to_all | solution.py:324
  55.6 0.0 copy-done.17
  55.6 1.5 %copy-done.8 = bf16[896,1024]{1,0:T(8,128)(2,1)S(1)} copy-done((bf16[896,1024]{1,0:T(8,128)(2,1)S(1)}, bf16[896,1024]{1,0:T(8,128)(2,1)}, u32[]{:S(2)}) %copy-start.8) | copy-done | bytes 1835032
  57.1 1.5 %copy-done.10 = bf16[896,1024]{1,0:T(8,128)(2,1)S(1)} copy-done((bf16[896,1024]{1,0:T(8,128)(2,1)S(1)}, bf16[896,1024]{1,0:T(8,128)(2,1)}, u32[]{:S(2)}) %copy-start.10) | copy-done | bytes 1835032
  58.6 1.8 %core_back.1 = (bf16[128,1024]{1,0:T(8,128)(2,1)S(1)}, f32[55,8,64]{2,1,0:T(8,128)S(1)}, f32[55,8,64]{2,1,0:T(8,128)S(1)}, f32[8,128]{1,0:T(8,128)S(1)}) custom-call(f32[8,8,1152]{2,1,0:T(8,128)S(1)} %all-to-all-done.1.field_ref, f32[8,128]{1,0:T(8,128)S(1)} %bitcast.27, bf16[896,1024]{1,0:T(8,128)(2,1)S(1)} %copy-done.8, bf16[896,1024]{1,0:T(8,128)(2,1)S(1)} %copy-done.10, ...), custom_call_target="tpu_custom_call" | custom-call | tf_op jit(solution)/shard_map/core_back/pallas_call | solution.py:328
  60.4 0.0 copy-start.1
  60.4 3.5 %copy-done.1 = bf16[4352,1024]{1,0:T(8,128)(2,1)S(1)} copy-done((bf16[4352,1024]{1,0:T(8,128)(2,1)S(1)}, bf16[4352,1024]{1,0:T(8,128)(2,1)}, u32[]{:S(2)}) %copy-start.1) | copy-done | bytes 8912920
  63.9 4.5 %back.1 = (f32[4,4,8,1152]{3,2,1,0:T(8,128)S(1)}, f32[4,4,8,1152]{3,2,1,0:T(8,128)S(1)}) custom-call(s32[1]{0:T(128)} %bitcast.core_ref, bf16[128,1024]{1,0:T(8,128)(2,1)S(1)} %get-tuple-element.28.pair_ref, bf16[4352,1024]{1,0:T(8,128)(2,1)S(1)} %copy-done.1), custom_call_target="tpu_custom_call" | custom-call | flops 1140850688 | bytes 10485760 | tf_op jit(solution)/shard_map/back/pallas_call | solution.py:343
  68.4 0.6 collective-permute-start.1
  68.9 2.7 %collective-permute-start.2 = (f32[55,8,64]{2,1,0:T(8,128)S(1)}, f32[55,8,64]{2,1,0:T(8,128)S(1)}, u32[]{:S(2)}, u32[]{:S(2)}) collective-permute-start(f32[55,8,64]{2,1,0:T(8,128)S(1)} %get-tuple-element.32), channel_id=1, source_target_pairs={{0,8},{8,16},{16,24},{24,32},{32,40},{40,48},{48,56},{56,64},{64,7... | collective-permute-start | bytes 337928 | tf_op jit(solution)/shard_map/ppermute | solution.py:341
  71.6 2.9 %collective-permute-done.2.halo_ref = f32[55,8,64]{2,1,0:T(8,128)S(1)} collective-permute-done((f32[55,8,64]{2,1,0:T(8,128)S(1)}, f32[55,8,64]{2,1,0:T(8,128)S(1)}, u32[]{:S(2)}, u32[]{:S(2)}) %collective-permute-start.2) | collective-permute-done | bytes 112672 | tf_op jit(solution)/shard_map/ppermute | solution.py:341
  74.5 0.0 collective-permute-done.1.got_ref
  74.5 0.7 image.1
  75.2 16.9 %all_to_all.26 = f32[16,8,1152]{2,1,0:T(8,128)} all-to-all(f32[16,8,1152]{2,1,0:T(8,128)S(1)} %bitcast.23), channel_id=1, replica_groups={{0,16,32,48,64,80,96,112,128,144,160,176,192,208,224,240},{8,24,40,56,7..., dimensions={0} | all-to-all | bytes 1179648 | tf_op jit(solution)/shard_map/all_to_all | solution.py:368
  92.1 1.1 reduce_sum.19
  93.3 12.8 %all_to_all.27 = f32[16,8,1152]{2,1,0:T(8,128)S(1)} all-to-all(f32[16,8,1152]{2,1,0:T(8,128)S(1)} %broadcast_in_dim.5), channel_id=1, replica_groups={{0,16,32,48,64,80,96,112,128,144,160,176,192,208,224,240},{8,24,40,56,7..., dimensions={0} | all-to-all | bytes 1179648 | tf_op jit(solution)/shard_map/all_to_all | solution.py:371
  106.1 3.9 %collective-permute-start.3 = (f32[4,4,8,1152]{3,2,1,0:T(8,128)S(1)}, f32[4,4,8,1152]{3,2,1,0:T(8,128)S(1)}, u32[]{:S(2)}, u32[]{:S(2)}) collective-permute-start(f32[4,4,8,1152]{3,2,1,0:T(8,128)S(1)} %bitcast.18), channel_id=1, source_target_pairs={{0,8},{8,0},{16,24},{24,16},{32,40},{40,32},{48,56},{56,48},{64,72... | collective-permute-start | bytes 1769480 | tf_op jit(solution)/shard_map/ppermute | solution.py:375
  110.0 1.6 %collective-permute-done.3.got_ref = f32[4,4,8,1152]{3,2,1,0:T(8,128)S(1)} collective-permute-done((f32[4,4,8,1152]{3,2,1,0:T(8,128)S(1)}, f32[4,4,8,1152]{3,2,1,0:T(8,128)S(1)}, u32[]{:S(2)}, u32[]{:S(2)}) %collective-permute-start.3) | collective-permute-done | bytes 589856 | tf_op jit(solution)/shard_map/ppermute | solution.py:375
  111.6 4.2 %update.1 = (f32[64,4352]{1,0:T(8,128)}, f32[64,4352]{1,0:T(8,128)}, f32[55,8,64]{2,1,0:T(8,128)}, f32[55,8,64]{2,1,0:T(8,128)}, f32[8,8,128]{2,1,0:T(8,128)S(1)}, /*index=5*/f32[8,128]{1,0:T(8,128)S(1)}) custom-call(s32[1]{0:T(128)} %bitcast.core_ref, f32[4,4,8,1152]{3,2,1,0:T(8,128)S(1)} %bitcast.19, f32[4,4,8,1152]{3,2,1,0:T(8,128)S(1)} %collective-permute-done.3.got_ref, ...), custom_call_target="tpu_custom_call" | custom-call | tf_op jit(solution)/shard_map/update/pallas_call | solution.py:383
  115.8 9.2 %all_to_all.28.norm_ref = f32[8,8,128]{2,1,0:T(8,128)S(1)} all-to-all(f32[8,8,128]{2,1,0:T(8,128)S(1)} %get-tuple-element.38), channel_id=1, replica_groups=mesh['tm'=32,'coef'=8] {'coef'}, dimensions={0} | all-to-all | bytes 65536 | tf_op jit(solution)/shard_map/all_to_all | solution.py:400
  125.1 1.2 copy-done.12
  126.3 0.9 copy-done.14
  127.2 3.2 %direction.1 = (f32[64,4352]{1,0:T(8,128)}, f32[55,8,64]{2,1,0:T(8,128)}) custom-call(f32[8,8,128]{2,1,0:T(8,128)S(1)} %all_to_all.28.norm_ref, f32[8,128]{1,0:T(8,128)S(1)} %get-tuple-element.39.keep_ref, f32[64,4352]{1,0:T(8,128)S(1)} %copy-done.12, f32[64,4352]{1,0:T(8,128)S(1)} %copy-done.3, f32[55,8,64]{2,1,0:T(8,128)S(1)} %copy-done.14, ...), custom_call_target="tpu_custom_call" | custom-call | tf_op jit(solution)/shard_map/direction/pallas_call | solution.py:401
  (21 shorter events, 0.1 us)
Async XLA Ops:
  0.6 13.2 %collective-permute-start = (f32[55,8,64]{2,1,0:T(8,128)}, f32[55,8,64]{2,1,0:T(8,128)S(1)}, u32[]{:S(2)}, u32[]{:S(2)}) collective-permute-start(f32[55,8,64]{2,1,0:T(8,128)} %bitcast.13), channel_id=1, source_target_pairs={{8,0},{16,8},{24,16},{32,24},{40,32},{48,40},{56,48},{64,56},{72,6... | collective-permute-start | bytes 337928 | tf_op jit(solution)/shard_map/ppermute | solution.py:288
  6.5 3.5 %copy-start = (bf16[4352,1024]{1,0:T(8,128)(2,1)S(1)}, bf16[4352,1024]{1,0:T(8,128)(2,1)}, u32[]{:S(2)}) copy-start(bf16[4352,1024]{1,0:T(8,128)(2,1)} %a_hbm.3) | copy-start | bytes 26738692
  10.1 1.2 copy-start.2
  11.3 2.5 %copy-start.3 = (f32[64,4352]{1,0:T(8,128)S(1)}, f32[64,4352]{1,0:T(8,128)}, u32[]{:S(2)}) copy-start(f32[64,4352]{1,0:T(8,128)} %dir_ref.7) | copy-start | bytes 3342340
  11.3 2.5 %copy-start.4 = (f32[64,4352]{1,0:T(8,128)S(1)}, f32[64,4352]{1,0:T(8,128)}, u32[]{:S(2)}) copy-start(f32[64,4352]{1,0:T(8,128)} %res_ref.3) | copy-start | bytes 3342340
  11.3 2.5 %copy-start.5 = (f32[64,55,8]{0,2,1:T(8,128)S(1)}, f32[64,55,8]{0,2,1:T(8,128)}, u32[]{:S(2)}) copy-start(f32[64,55,8]{0,2,1:T(8,128)} %param.27) | copy-start | bytes 337924
  11.3 2.5 %copy-start.6 = (f32[64,55,8]{0,2,1:T(8,128)S(1)}, f32[64,55,8]{0,2,1:T(8,128)}, u32[]{:S(2)}) copy-start(f32[64,55,8]{0,2,1:T(8,128)} %param.26) | copy-start | bytes 337924
  11.3 2.5 %copy-start.15 = (bf16[55,1024]{1,0:T(8,128)(2,1)S(1)}, bf16[55,1024]{1,0:T(8,128)(2,1)}, u32[]{:S(2)}) copy-start(bf16[55,1024]{1,0:T(8,128)(2,1)} %design_ref.1) | copy-start | bytes 337924
  11.3 2.5 %copy-start.16 = (f32[1024]{0:T(1024)S(1)}, f32[1024]{0:T(1024)}, u32[]{:S(2)}) copy-start(f32[1024]{0:T(1024)} %param.16) | copy-start | bytes 12292
  11.4 2.5 %copy-start.18 = (f32[55]{0:T(128)S(1)}, f32[55]{0:T(128)}, u32[]{:S(2)}) copy-start(f32[55]{0:T(128)} %cdamp_ref.3) | copy-start | bytes 664
  11.4 2.5 %copy-start.20 = (s32[8]{0:T(128)S(1)}, s32[8]{0:T(128)}, u32[]{:S(2)}) copy-start(s32[8]{0:T(128)} %knot_ref.1) | copy-start | bytes 100
  16.5 1.3 copy-start.7
  17.7 1.2 copy-start.9
  18.9 36.7 %copy-start.17 = (f32[1024]{0:T(1024)S(1)}, f32[1024]{0:T(1024)}, u32[]{:S(2)}) copy-start(f32[1024]{0:T(1024)} %param.17) | copy-start | bytes 12292
  18.9 36.7 %copy-start.19 = (s32[8]{0:T(128)S(1)}, s32[8]{0:T(128)}, u32[]{:S(2)}) copy-start(s32[8]{0:T(128)} %count_ref.1) | copy-start | bytes 100
  39.2 16.4 %all-to-all-start.1 = ((f32[8,8,1152]{2,1,0:T(8,128)}), f32[8,8,1152]{2,1,0:T(8,128)S(1)}, u32[]{:S(2)}, u32[]{:S(2)}) async-start(f32[8,8,1152]{2,1,0:T(8,128)} %broadcast_in_dim.4), calls=%async_computation.1 | async-start | bytes 589824 | tf_op jit(solution)/shard_map/all_to_all | solution.py:324
  55.6 1.5 %copy-start.8 = (bf16[896,1024]{1,0:T(8,128)(2,1)S(1)}, bf16[896,1024]{1,0:T(8,128)(2,1)}, u32[]{:S(2)}) copy-start(bf16[896,1024]{1,0:T(8,128)(2,1)} %copy-done.7) | copy-start | bytes 5505028
  57.1 1.5 %copy-start.10 = (bf16[896,1024]{1,0:T(8,128)(2,1)S(1)}, bf16[896,1024]{1,0:T(8,128)(2,1)}, u32[]{:S(2)}) copy-start(bf16[896,1024]{1,0:T(8,128)(2,1)} %copy-done.9) | copy-start | bytes 5505028
  60.4 3.5 %copy-start.1 = (bf16[4352,1024]{1,0:T(8,128)(2,1)S(1)}, bf16[4352,1024]{1,0:T(8,128)(2,1)}, u32[]{:S(2)}) copy-start(bf16[4352,1024]{1,0:T(8,128)(2,1)} %a_hbm.3) | copy-start | bytes 26738692
  68.4 6.1 %collective-permute-start.1 = (f32[4,4,8,1152]{3,2,1,0:T(8,128)S(1)}, f32[4,4,8,1152]{3,2,1,0:T(8,128)S(1)}, u32[]{:S(2)}, u32[]{:S(2)}) collective-permute-start(f32[4,4,8,1152]{3,2,1,0:T(8,128)S(1)} %get-tuple-element.30), channel_id=1, source_target_pairs={{0,8},{8,0},{16,24},{24,16},{32,40},{40,32},{48,56},{56,48},{64,72... | collective-permute-start | bytes 1769480 | tf_op jit(solution)/shard_map/ppermute | solution.py:357
  68.9 5.6 %collective-permute-start.2 = (f32[55,8,64]{2,1,0:T(8,128)S(1)}, f32[55,8,64]{2,1,0:T(8,128)S(1)}, u32[]{:S(2)}, u32[]{:S(2)}) collective-permute-start(f32[55,8,64]{2,1,0:T(8,128)S(1)} %get-tuple-element.32), channel_id=1, source_target_pairs={{0,8},{8,16},{16,24},{24,32},{32,40},{40,48},{48,56},{56,64},{64,7... | collective-permute-start | bytes 337928 | tf_op jit(solution)/shard_map/ppermute | solution.py:341
  92.1 19.5 %copy-start.13 = (f32[64,55,8]{0,2,1:T(8,128)S(1)}, f32[64,55,8]{0,2,1:T(8,128)}, u32[]{:S(2)}) copy-start(f32[64,55,8]{0,2,1:T(8,128)} %param.25) | copy-start | bytes 337924
  93.2 18.4 %copy-start.11 = (f32[64,4352]{1,0:T(8,128)S(1)}, f32[64,4352]{1,0:T(8,128)}, u32[]{:S(2)}) copy-start(f32[64,4352]{1,0:T(8,128)} %sol_ref.1) | copy-start | bytes 3342340
  106.1 5.5 %collective-permute-start.3 = (f32[4,4,8,1152]{3,2,1,0:T(8,128)S(1)}, f32[4,4,8,1152]{3,2,1,0:T(8,128)S(1)}, u32[]{:S(2)}, u32[]{:S(2)}) collective-permute-start(f32[4,4,8,1152]{3,2,1,0:T(8,128)S(1)} %bitcast.18), channel_id=1, source_target_pairs={{0,8},{8,0},{16,24},{24,16},{32,40},{40,32},{48,56},{56,48},{64,72... | collective-permute-start | bytes 1769480 | tf_op jit(solution)/shard_map/ppermute | solution.py:375
  125.1 1.2 copy-start.12
  126.3 0.9 copy-start.14

commit v2 on v1

v2 whole, which is shorter than its diff:
```python
import jax
import jax.numpy as jnp
from jax import lax
from jax.experimental import pallas as pl
from jax.experimental.pallas import tpu as pltpu
from jax.sharding import PartitionSpec as P

NL, NS, MEM, NJ, JP = 4352, 1024, 64, 55, 56
SEG = 128
WIDE, SENT = 1152, 1280
MIB = 1 << 20
F32, BF16 = jnp.float32, jnp.bfloat16
VM = pl.BlockSpec(memory_space=pltpu.VMEM)
SM = pl.BlockSpec(memory_space=pltpu.SMEM)
HB = pl.BlockSpec(memory_space=pltpu.HBM)
FORWARD_CUTS = (0, 512, 1280, 2304, 3328, 4352)
TRANS_B = (((1,), (1,)), ((), ()))


def params(mib):
    return pltpu.CompilerParams(vmem_limit_bytes=mib * MIB)


def struct(shape, dtype=F32):
    return jax.ShapeDtypeStruct(shape, dtype)


def split(values):
    high = values.astype(BF16)
    return high, (values - high.astype(F32)).astype(BF16)


def spline_values(u):
    now = [jnp.ones_like(u)]
    for d in range(1, 6):
        later = []
        for s in range(d + 1):
            term = 0.0
            if s >= 1:
                term = (u + float(d - s)) * now[s - 1]
            if s < d:
                term = term + (float(s + 1) - u) * now[s]
            later.append(term * (1.0 / d))
        now = later
    return now


def forward_kernel(
    dir_hbm, a_hbm, design_hbm, phase_hbm, knot_hbm, out_ref, a_buf, ghi_ref, glo_ref,
    dir_buf, lhs, acc, design_buf, phase_buf, knot_buf, basis, design, small_sems, sems,
):
    small = [
        pltpu.make_async_copy(src, dst, small_sems.at[k])
        for k, (src, dst) in enumerate(
            ((phase_hbm, phase_buf), (knot_hbm, knot_buf), (design_hbm, design_buf), (dir_hbm, dir_buf))
        )
    ]
    for copy in small:
        copy.start()
    copies = []
    for b in range(len(FORWARD_CUTS) - 1):
        rows = pl.ds(FORWARD_CUTS[b], FORWARD_CUTS[b + 1] - FORWARD_CUTS[b])
        copy = pltpu.make_async_copy(a_hbm.at[rows], a_buf.at[rows], sems.at[b])
        copy.start()
        copies.append(copy)
    for copy in small[0:3]:
        copy.wait()
    values = spline_values(phase_buf[...])
    row = lax.broadcasted_iota(jnp.int32, (16, SEG), 0)
    for g in range(8):
        first = lax.rem(knot_buf[g], 8)
        block = jnp.zeros((16, SEG), F32)
        for k in range(6):
            block = block + jnp.where(row == first + k, values[k][g : g + 1, :], 0.0)
        basis[:, g * SEG : (g + 1) * SEG] = block
    design[0:NJ] = design_buf[...].astype(F32)
    design[NJ:JP] = jnp.zeros((1, NS), F32)

    def build(j, carry):
        high, low = split(basis[...] * design[pl.ds(j, 1), :])
        rows = pl.ds(pl.multiple_of(j * 16, 16), 16)
        ghi_ref[rows, :] = high
        glo_ref[rows, :] = low
        return carry

    lax.fori_loop(0, JP, build, 0)
    small[3].wait()
    for b, copy in enumerate(copies):
        lo, hi = FORWARD_CUTS[b], FORWARD_CUTS[b + 1]
        high, low = split(dir_buf[:, lo:hi])
        lhs[0:MEM, lo:hi] = high
        lhs[MEM:, lo:hi] = low
        copy.wait()
        part = jnp.dot(lhs[:, lo:hi], a_buf[lo:hi], preferred_element_type=F32)
        if b == 0:
            acc[...] = part
        else:
            acc[...] += part
    out_ref[...] = acc[0:MEM] + acc[MEM:]


def core_forward_kernel(lith_ref, cdir_ref, halo_ref, ghi_ref, glo_ref, out_ref, ext):
    ext[0:NJ, 0:8, :] = cdir_ref[...]
    ext[0:NJ, 8:16, :] = halo_ref[...]
    ext[NJ:JP] = jnp.zeros((1, 16, MEM), F32)
    high, low = split(jnp.transpose(ext[...].reshape(JP * 16, MEM)))
    both = jnp.concatenate([high, low], axis=0)
    wide = jnp.dot(both, ghi_ref[...], preferred_element_type=F32)
    value = wide[0:MEM] + wide[MEM:] + jnp.dot(high, glo_ref[...], preferred_element_type=F32)
    out_ref[...] = (value + lith_ref[...]).reshape(8, 8, NS)


def sum_kernel(parts_ref, out_ref):
    total = parts_ref[0]
    for k in range(1, parts_ref.shape[0]):
        total = total + parts_ref[k]
    for k in range(parts_ref.shape[0]):
        out_ref[k] = total


def core_back_kernel(
    field_ref, weight_ref, ghi_ref, glo_ref, count_ref, pair_ref, local_ref, halo_ref, curve_ref
):
    lane = lax.broadcasted_iota(jnp.int32, (1, SEG), 1)
    curve = jnp.zeros((MEM, SEG), F32)
    for g in range(8):
        cols = slice(g * SEG, (g + 1) * SEG)
        weight = jnp.where(lane < count_ref[g], weight_ref[g : g + 1, :], 0.0)
        field = field_ref[:, :, cols].reshape(MEM, SEG)
        residual = field * weight
        curve = curve + residual * field
        high, low = split(residual)
        pair_ref[0:MEM, cols] = high
        pair_ref[MEM:, cols] = low
    curve_ref[...] = curve
    wide = lax.dot_general(ghi_ref[...], pair_ref[...], TRANS_B, preferred_element_type=F32)
    low = lax.dot_general(
        glo_ref[...], pair_ref[0:MEM], TRANS_B, preferred_element_type=F32
    )
    grad = (wide[:, 0:MEM] + wide[:, MEM:] + low).reshape(JP, 16, MEM)
    local_ref[...] = grad[0:NJ, 0:8, :]
    halo_ref[...] = grad[0:NJ, 8:16, :]


def back_kernel(pair_ref, a_ref, own_ref, other_ref, lhs):
    half = MEM // 2
    core = lax.axis_index("core")
    mine = pl.multiple_of(core * half, half)
    theirs = pl.multiple_of((1 - core) * half, half)
    for k, start in enumerate((mine, theirs, MEM + mine, MEM + theirs)):
        lhs[k * half : (k + 1) * half] = pair_ref[pl.ds(pl.multiple_of(start, half), half), :]
    for y in range(4):
        cols = columns_of(y)
        count = cols.stop - cols.start
        part = lax.dot_general(lhs[...], a_ref[cols], TRANS_B, preferred_element_type=F32)
        part = part[0:MEM] + part[MEM:]
        own_ref[:, y, :, 0:count] = part[0:half].reshape(4, 8, count)
        other_ref[:, y, :, 0:count] = part[half:].reshape(4, 8, count)
    for out in (own_ref, other_ref):
        out[:, 3, :, NL - 3 * WIDE :] = jnp.zeros((4, 8, 4 * WIDE - NL), F32)


def add_kernel(a_ref, b_ref, out_ref):
    out_ref[...] = a_ref[...] + b_ref[...]


def turned(row):
    return jnp.transpose(jnp.broadcast_to(row, (128, 128)))


def columns_of(y):
    return slice(y * WIDE, min((y + 1) * WIDE, NL))


def out_copies(pairs, sems):
    copies = [
        pltpu.make_async_copy(src, dst, sems.at[k]) for k, (src, dst) in enumerate(pairs)
    ]
    for copy in copies:
        copy.start()
    return copies


def damp_rows(damp_ref, cols):
    rows = range(cols.start // SEG, cols.stop // SEG)
    return jnp.concatenate(
        [jnp.broadcast_to(damp_ref[t : t + 1, :], (8, SEG)) for t in rows], axis=1
    )


def folded(values):
    total = values[:, 0:SEG]
    for t in range(1, values.shape[1] // SEG):
        total = total + values[:, t * SEG : (t + 1) * SEG]
    return total


def member_row(columns):
    padded = jnp.concatenate([columns, jnp.zeros((128 - MEM, 128), F32)], axis=0)
    return jnp.sum(jnp.transpose(padded), axis=0, keepdims=True)[:, 0:MEM]


def image_kernel(
    parts_ref, local_ref, halo_ref, cdir_ref, cres_ref, curve_ref, dir_ref, res_ref, damp_ref, cdamp_ref,
    chunk_ref, cimage_ref, sums_ref, square,
):
    zero = jnp.zeros((8, MEM), F32)
    before, curve, cross, norm = zero, zero, zero, zero
    for j in range(NJ):
        residual = cres_ref[j]
        damped = cdamp_ref[j] * cdir_ref[j]
        core_image = local_ref[j] + halo_ref[j] + damped
        cimage_ref[j] = core_image
        before = before + residual * residual
        curve = curve + damped * cdir_ref[j]
        cross = cross + residual * core_image
        norm = norm + core_image * core_image
    total = parts_ref[0]
    for k in range(1, 16):
        total = total + parts_ref[k]
    chunk_ref[...] = total
    square[...] = jnp.zeros((2, MEM, 128), F32)
    plane = lax.axis_index("plane")
    core = lax.axis_index("core")
    rows = pl.ds(pl.multiple_of((core * 4 + plane // 4) * 8, 8), 8)

    def finish(y):
        cols = columns_of(y)
        count = cols.stop - cols.start
        value = chunk_ref[:, 0:count] + damp_rows(damp_ref, cols) * dir_ref[rows, cols]
        chunk_ref[:, 0:count] = value
        square[0, rows, :] = folded(value * res_ref[rows, cols])
        square[1, rows, :] = folded(value * value)

    for y in range(4):
        pl.when(lax.rem(plane, 4) == y)(lambda y=y: finish(y))
    lith_before = jnp.zeros((MEM, SEG), F32)
    lith_curve = jnp.zeros((MEM, SEG), F32)
    for t in range(NL // SEG):
        cols = slice(t * SEG, (t + 1) * SEG)
        lith_before = lith_before + res_ref[:, cols] * res_ref[:, cols]
        lith_curve = lith_curve + dir_ref[:, cols] * dir_ref[:, cols] * damp_ref[t : t + 1, :]
    once = jnp.where(jnp.logical_and(plane == 0, core == 0), 1.0, 0.0)
    first = jnp.where(lax.axis_index("coef") == 0, 1.0, 0.0)
    lith_curve = once * lith_curve + first * curve_ref[...]
    rows_of = [
        (before, once * lith_before), (curve, lith_curve), (cross, square[0]), (norm, square[1])
    ]
    tile = jnp.concatenate(
        [jnp.sum(c, axis=0, keepdims=True) + member_row(v) for c, v in rows_of]
        + [jnp.zeros((4, MEM), F32)],
        axis=0,
    )
    tile = jnp.concatenate([tile, jnp.zeros((8, 128 - MEM), F32)], axis=1)
    for k in range(8):
        sums_ref[k] = tile


def spread_kernel(sums_ref, chunk_ref, out_ref):
    tile = sums_ref[0]
    for k in range(1, 8):
        tile = tile + sums_ref[k]
    for k in range(16):
        out_ref[k, :, 0:WIDE] = chunk_ref[...]
        out_ref[k, :, WIDE:] = tile


def update_kernel(
    own_ref, got_ref, sol_ref, res_ref, dir_ref, cimage_ref, csol_ref, cres_ref, cdir_ref,
    sol_hbm, res_hbm, dir_hbm, csol_hbm, cres_hbm, cdir_hbm,
    sol_buf, res_buf, dir_buf, csol_buf, cres_buf, cdir_buf, step_col, ratio_col, core_sems, sems,
):
    core = lax.axis_index("core")
    tile = jnp.zeros((8, 128), F32)
    for x in range(4):
        for y in range(4):
            tile = tile + (own_ref[x, y, :, WIDE:] + got_ref[x, y, :, WIDE:])
    tile = tile[:, 0:MEM]
    before = tile[0:1]
    step = before / tile[1:2]
    ratio = (before + step * (step * tile[3:4] - 2.0 * tile[2:3])) / before
    blank = jnp.zeros((1, 128 - MEM), F32)
    step_col[...] = turned(jnp.concatenate([step, blank], axis=1))
    ratio_col[...] = turned(jnp.concatenate([ratio, blank], axis=1))
    waits = []
    for y in range(4):
        cols = columns_of(y)
        count = (cols.stop - cols.start) // SEG
        for k in range(8):
            ref, part = (own_ref, core) if k < 4 else (got_ref, 1 - core)
            rows = pl.ds(pl.multiple_of(part * 32 + (k % 4) * 8, 8), 8)
            scale = jnp.concatenate([step_col[rows, :]] * count, axis=1)
            other = jnp.concatenate([ratio_col[rows, :]] * count, axis=1)
            direction = dir_ref[rows, cols]
            sol_buf[rows, cols] = sol_ref[rows, cols] + scale * direction
            new_res = res_ref[rows, cols] - scale * ref[k % 4, y, :, 0 : count * SEG]
            res_buf[rows, cols] = new_res
            dir_buf[rows, cols] = new_res + other * direction
        waits += out_copies(
            [
                (buf.at[:, cols], hbm.at[:, cols])
                for buf, hbm in ((sol_buf, sol_hbm), (res_buf, res_hbm), (dir_buf, dir_hbm))
            ],
            sems.at[y],
        )
    for j in range(NJ):
        csol_buf[j] = csol_ref[j] + step * cdir_ref[j]
        new_res = cres_ref[j] - step * cimage_ref[j]
        cres_buf[j] = new_res
        cdir_buf[j] = new_res + ratio * cdir_ref[j]
    waits += out_copies(
        [(csol_buf, csol_hbm), (cres_buf, cres_hbm), (cdir_buf, cdir_hbm)], core_sems
    )
    for copy in waits:
        copy.wait()


def shards(
    design_lith, design_core, sample_phase, data_weight, counts, knot_index, lith_damping, core_damping,
    lith_solution, lith_residual, lith_direction, core_solution, core_residual, core_direction,
):
    segments = ("plane", "core")
    tm = lax.axis_size("plane") * 2
    swap = [(0, 1), (1, 0)]
    csol, cres, cdir = (
        jnp.transpose(v, (1, 2, 0)) for v in (core_solution, core_residual, core_direction)
    )
    phase = sample_phase.reshape(8, SEG)
    weight = data_weight.reshape(8, SEG)
    damp = lith_damping.reshape(NL // SEG, SEG)
    upper = lax.ppermute(cdir, segments, [(t, t - 1) for t in range(1, tm)])
    product_cost = pl.CostEstimate(
        flops=16 * MEM * NL * NS, bytes_accessed=12 * MIB, transcendentals=0
    )

    pin = lambda v: pltpu.with_memory_space_constraint(v, pltpu.HBM)
    lith, design, ghi, glo = pl.pallas_call(
        forward_kernel,
        out_shape=(
            struct((MEM, NS)),
            pltpu.VMEM((NL, NS), BF16),
            struct((JP * 16, NS), BF16),
            struct((JP * 16, NS), BF16),
        ),
        in_specs=[HB] * 5,
        out_specs=(VM,) * 4,
        scratch_shapes=[
            pltpu.VMEM((MEM, NL), F32),
            pltpu.VMEM((2 * MEM, NL), BF16),
            pltpu.VMEM((2 * MEM, NS), F32),
            pltpu.VMEM((NJ, NS), BF16),
            pltpu.VMEM((8, SEG), F32),
            pltpu.SMEM((8,), jnp.int32),
            pltpu.VMEM((16, NS), F32),
            pltpu.VMEM((JP, NS), F32),
            pltpu.SemaphoreType.DMA((4,)),
            pltpu.SemaphoreType.DMA((len(FORWARD_CUTS) - 1,)),
        ],
        compiler_params=params(24),
        cost_estimate=product_cost,
        name="forward",
    )(pin(lith_direction), pin(design_lith), pin(design_core), pin(phase), pin(knot_index))

    partial = pl.pallas_call(
        core_forward_kernel,
        out_shape=struct((8, 8, NS)),
        in_specs=[VM] * 5,
        out_specs=VM,
        scratch_shapes=[pltpu.VMEM((JP, 16, MEM), F32)],
        compiler_params=params(12),
        name="core_forward",
    )(lith, cdir, upper, ghi, glo)

    parts = lax.all_to_all(partial, "coef", 0, 0)
    total = pl.pallas_call(
        sum_kernel,
        out_shape=struct(parts.shape),
        in_specs=[VM],
        out_specs=VM,
        compiler_params=params(8),
        name="field_sum",
    )(parts)
    field = lax.all_to_all(total, "coef", 0, 0)

    pair, local, halo, curve = pl.pallas_call(
        core_back_kernel,
        out_shape=(
            struct((2 * MEM, NS), BF16),
            struct((NJ, 8, MEM)),
            struct((NJ, 8, MEM)),
            struct((MEM, SEG)),
        ),
        in_specs=[VM] * 4 + [SM],
        out_specs=(VM,) * 4,
        compiler_params=params(16),
        name="core_back",
    )(field, weight, ghi, glo, counts)
    lower = lax.ppermute(halo, segments, [(t, t + 1) for t in range(tm - 1)])

    chunks = struct((4, 4, 8, WIDE))
    core_struct = struct((NJ, 8, MEM))
    own, other = pl.pallas_call(
        back_kernel,
        out_shape=(chunks, chunks),
        in_specs=[VM, VM],
        out_specs=(VM, VM),
        scratch_shapes=[pltpu.VMEM((2 * MEM, NS), BF16)],
        compiler_params=params(12),
        cost_estimate=product_cost,
        name="back",
    )(pair, design)
    other, lower = lax.optimization_barrier((other, lower))
    got = lax.ppermute(other, "core", swap)
    terms = pl.pallas_call(
        add_kernel,
        out_shape=chunks,
        in_specs=[VM, VM],
        out_specs=VM,
        compiler_params=params(8),
        name="add_halves",
    )(own, got)

    pieces = lax.all_to_all(terms.reshape(16, 8, WIDE), "plane", 0, 0)
    chunk, cimage, sums = pl.pallas_call(
        image_kernel,
        out_shape=(struct((8, WIDE)), core_struct, struct((8, 8, 128))),
        in_specs=[VM] * 9 + [SM],
        out_specs=(VM, VM, VM),
        scratch_shapes=[pltpu.VMEM((2, MEM, 128), F32)],
        compiler_params=params(12),
        name="image",
    )(pieces, local, lower, cdir, cres, curve, lith_direction, lith_residual, damp, core_damping)
    sums = lax.all_to_all(sums, "coef", 0, 0)
    sent = pl.pallas_call(
        spread_kernel,
        out_shape=struct((16, 8, SENT)),
        in_specs=[VM, VM],
        out_specs=VM,
        compiler_params=params(8),
        name="spread",
    )(sums, chunk)
    whole = lax.all_to_all(sent, "plane", 0, 0).reshape(4, 4, 8, SENT)
    rest = lax.ppermute(whole, "core", swap)

    lith_struct = struct((MEM, NL))
    new_sol, new_res, new_dir, new_csol, new_cres, new_cdir = pl.pallas_call(
        update_kernel,
        out_shape=(lith_struct,) * 3 + (core_struct,) * 3,
        in_specs=[VM] * 9,
        out_specs=(HB,) * 6,
        scratch_shapes=[pltpu.VMEM((MEM, NL), F32)] * 3
        + [pltpu.VMEM((NJ, 8, MEM), F32)] * 3
        + [pltpu.VMEM((128, 128), F32)] * 2
        + [pltpu.SemaphoreType.DMA((3,)), pltpu.SemaphoreType.DMA((4, 3))],
        compiler_params=params(20),
        name="update",
    )(
        whole, rest, lith_solution, lith_residual, lith_direction, cimage, csol, cres, cdir,
    )
    back = lambda v: jnp.transpose(v, (2, 0, 1))
    return new_sol, new_res, new_dir, back(new_csol), back(new_cres), back(new_cdir)


def solution(mesh):
    parts = jax.sharding.Mesh(mesh.devices.reshape(-1, 2, mesh.devices.shape[1]), ("plane", "core", "coef"))
    segments = ("plane", "core")
    lith, core = P(None, "coef"), P(None, "coef", segments)
    return jax.shard_map(
        shards,
        mesh=parts,
        in_specs=(
            P("coef", segments), P("coef", segments), P(segments), P(segments), P(segments), P(segments),
            P("coef"), P("coef"), lith, lith, lith, core, core, core,
        ),
        out_specs=(lith, lith, lith, core, core, core),
        check_vma=False,
    )
```

time: 131 us -> 107 us (0.82)
  local copies, waits for them, and re-layouts: 17.5 us -> 0.05 us
  blocking collectives: 58.4 us -> 75.2 us
  waiting for transfers between devices: 17.5 us -> 3.72 us
  Pallas kernels: 19.3 us -> 14.4 us
  starting transfers between devices: 15.7 us -> 12.7 us
    all_to_all x3 -> x4, blocking collectives: 38.9 us -> 56.5 us  [the longest x1 19.5 us: shards(): pieces = lax.all_to_all(terms.reshape(16, 8, WIDE), 'plane', 0, 0)]
    unnamed x42 -> x20, local copies, waits for them, and re-layouts: 16 us -> 0.05 us
    all_to_all x1 -> x0, waiting for transfers between devices: 13 us -> none  [shards(): lax.all_to_all(jnp.broadcast_to(jnp.sum(parts, axis=0)[None], (8, 8, WIDE...]
    pallas_call x6 -> x8, Pallas kernels: 17.6 us -> 12.6 us  [the longest x1 5.26 us: shards(): pl.pallas_call(forward_kernel, out_shape=(struct((MEM, NS)), pltpu.VMEM((...]
    all_to_all x1 -> x0, starting transfers between devices: 3.42 us -> none  [shards(): lax.all_to_all(jnp.broadcast_to(jnp.sum(parts, axis=0)[None], (8, 8, WIDE...]
  transfers between devices with their start and end apart: 5 -> 4, of which waited for: 3 -> 2; matrix products, arithmetic and copies ran while one was open for 1% -> 0% of each run, Pallas kernels for 2% -> 8%
where the time goes in v2:
time: 107 us
  blocking collectives  75.2 us (70%)
  Pallas kernels  14.4 us (13%)
  starting transfers between devices  12.7 us (12%)
  waiting for transfers between devices  3.72 us (3%)
    all_to_all x1, blocking collectives, shards(): pieces = lax.all_to_all(terms.reshape(16, 8, WIDE), 'plane', 0, 0)  19.5 us
    all_to_all x1, blocking collectives, shards(): parts = lax.all_to_all(partial, 'coef', 0, 0)  18.7 us
    all_to_all x1, blocking collectives, shards(): field = lax.all_to_all(total, 'coef', 0, 0)  14.7 us
    all_to_all x1, blocking collectives, shards(): whole = lax.all_to_all(sent, 'plane', 0, 0).reshape(4, 4, 8, SENT)  12.9 us
    all_to_all x1, blocking collectives, shards(): sums = lax.all_to_all(sums, 'coef', 0, 0)  9.38 us
    pallas_call x1, Pallas kernels, shards(): pl.pallas_call(forward_kernel, out_shape=(struct((MEM, NS)), pltpu.VMEM((...  5.26 us
    ppermute x1, starting transfers between devices, shards(): upper = lax.ppermute(cdir, segments, [(t, t - 1) for t in range(1, tm)])  5.15 us
    ppermute x1, starting transfers between devices, shards(): rest = lax.ppermute(whole, 'core', swap)  3.95 us
  transfers between devices with their start and end apart: 4, of which 2 were waited for; matrix products, arithmetic and copies ran while one was open for 0% of the time, Pallas kernels for 8%

profile of v2, /device:TPU:1, one launch (start us, length us, event | category | flops | bytes accessed | tf_op | source)
XLA Modules:
  0.0 106.9 jit_solution(2151412150962897592)
XLA Ops:
  0.6 5.1 %collective-permute-start = (f32[55,8,64]{2,1,0:T(8,128)}, f32[55,8,64]{2,1,0:T(8,128)S(1)}, u32[]{:S(2)}, u32[]{:S(2)}) collective-permute-start(f32[55,8,64]{2,1,0:T(8,128)} %bitcast.14), channel_id=1, source_target_pairs={{8,0},{16,8},{24,16},{32,24},{40,32},{48,40},{56,48},{64,56},{72,6... | collective-permute-start | bytes 337928 | tf_op jit(solution)/shard_map/ppermute | solution.py:331
  5.8 0.0 copy-start.2
  5.8 5.3 %forward.1 = (f32[64,1024]{1,0:T(8,128)S(1)}, bf16[4352,1024]{1,0:T(8,128)(2,1)S(1)}, bf16[896,1024]{1,0:T(8,128)(2,1)S(1)}, bf16[896,1024]{1,0:T(8,128)(2,1)S(1)}) custom-call(f32[64,4352]{1,0:T(8,128)} %dir_ref.3, bf16[4352,1024]{1,0:T(8,128)(2,1)} %a_hbm.1, bf16[55,1024]{1,0:T(8,128)(2,1)} %design_hbm.1, f32[8,128]{1,0:T(8,128)} %bitcast.26, s32[8]{0:T(128)} %knot_hbm.1), custom_call_target="tpu_custom_call" | custom-call | flops 4563402752 | bytes 12582912 | tf_op jit(solution)/shard_map/forward/pallas_call | solution.py:337
  11.1 0.0 collective-permute-done.halo_ref
  11.1 0.0 copy-done.2
  11.1 0.8 core_forward.1
  11.9 0.0 copy-start.7
  11.9 0.0 copy-start.8
  11.9 18.7 %all_to_all.25.parts_ref = f32[8,8,1024]{2,1,0:T(8,128)S(1)} all-to-all(f32[8,8,1024]{2,1,0:T(8,128)S(1)} %core_forward.1), channel_id=1, replica_groups=mesh['plane'=16,'core'=2,'coef'=8] {'coef'}, dimensions={0} | all-to-all | bytes 524288 | tf_op jit(solution)/shard_map/all_to_all | solution.py:374
  30.6 14.7 %all_to_all.26.field_ref = f32[8,8,1024]{2,1,0:T(8,128)S(1)} all-to-all(f32[8,8,1024]{2,1,0:T(8,128)S(1)} %field_sum.1), channel_id=1, replica_groups=mesh['plane'=16,'core'=2,'coef'=8] {'coef'}, dimensions={0} | all-to-all | bytes 524288 | tf_op jit(solution)/shard_map/all_to_all | solution.py:383
  45.3 0.0 copy-done.7
  45.3 0.0 copy-done.8
  45.3 1.8 %core_back.1 = (bf16[128,1024]{1,0:T(8,128)(2,1)S(1)}, f32[55,8,64]{2,1,0:T(8,128)S(1)}, f32[55,8,64]{2,1,0:T(8,128)S(1)}, f32[64,128]{1,0:T(8,128)S(1)}) custom-call(f32[8,8,1024]{2,1,0:T(8,128)S(1)} %all_to_all.26.field_ref, f32[8,128]{1,0:T(8,128)S(1)} %bitcast.22, bf16[896,1024]{1,0:T(8,128)(2,1)S(1)} %get-tuple-element.28.ghi_ref, ...), custom_call_target="tpu_custom_call" | custom-call | tf_op jit(solution)/shard_map/core_back/pallas_call | solution.py:385
  47.1 3.5 %collective-permute-start.1 = (f32[55,8,64]{2,1,0:T(8,128)S(1)}, f32[55,8,64]{2,1,0:T(8,128)S(1)}, u32[]{:S(2)}, u32[]{:S(2)}) collective-permute-start(f32[55,8,64]{2,1,0:T(8,128)S(1)} %get-tuple-element.34), channel_id=1, source_target_pairs={{0,8},{8,16},{16,24},{24,32},{32,40},{40,48},{48,56},{56,64},{64,7... | collective-permute-start | bytes 337928 | tf_op jit(solution)/shard_map/ppermute | solution.py:398
  50.6 2.9 %back.1 = (f32[4,4,8,1152]{3,2,1,0:T(8,128)S(1)}, f32[4,4,8,1152]{3,2,1,0:T(8,128)S(1)}) custom-call(bf16[128,1024]{1,0:T(8,128)(2,1)S(1)} %get-tuple-element.30.pair_ref, bf16[4352,1024]{1,0:T(8,128)(2,1)S(1)} %get-tuple-element.31.a_ref), custom_call_target="tpu_custom_call" | custom-call | flops 4563402752 | bytes 12582912 | tf_op jit(solution)/shard_map/back/pallas_call | solution.py:402
  53.6 0.0 collective-permute-done.1.halo_ref
  53.6 0.1 collective-permute-start.2
  53.7 2.0 %collective-permute-done.2.b_ref = f32[4,4,8,1152]{3,2,1,0:T(8,128)S(1)} collective-permute-done((f32[4,4,8,1152]{3,2,1,0:T(8,128)S(1)}, f32[4,4,8,1152]{3,2,1,0:T(8,128)S(1)}, u32[]{:S(2)}, u32[]{:S(2)}) %collective-permute-start.2) | collective-permute-done | bytes 589856 | tf_op jit(solution)/shard_map/ppermute | solution.py:413
  55.7 0.0 copy-start
  55.7 0.0 copy-start.1
  55.7 0.0 copy-start.4
  55.7 0.0 copy-start.6
  55.7 0.0 copy-start.9
  55.7 0.1 add_halves.1
  55.8 19.5 %all_to_all.27.parts_ref = f32[16,8,1152]{2,1,0:T(8,128)S(1)} all-to-all(f32[16,8,1152]{2,1,0:T(8,128)S(1)} %bitcast.13), channel_id=1, replica_groups=mesh['plane'=16,'core'=2,'coef'=8] {'plane'}, dimensions={0} | all-to-all | bytes 1179648 | tf_op jit(solution)/shard_map/all_to_all | solution.py:423
  75.3 0.0 copy-done
  75.3 0.0 copy-done.1
  75.3 0.0 copy-done.4
  75.3 0.0 copy-done.6
  75.3 0.0 copy-done.9
  75.3 1.0 image.1
  76.4 0.0 copy-start.3
  76.4 0.0 copy-start.5
  76.4 9.4 %all_to_all.28.sums_ref = f32[8,8,128]{2,1,0:T(8,128)S(1)} all-to-all(f32[8,8,128]{2,1,0:T(8,128)S(1)} %get-tuple-element.39), channel_id=1, replica_groups=mesh['plane'=16,'core'=2,'coef'=8] {'coef'}, dimensions={0} | all-to-all | bytes 65536 | tf_op jit(solution)/shard_map/all_to_all | solution.py:433
  85.8 12.9 %all_to_all.29 = f32[16,8,1280]{2,1,0:T(8,128)S(1)} all-to-all(f32[16,8,1280]{2,1,0:T(8,128)S(1)} %spread.1), channel_id=1, replica_groups=mesh['plane'=16,'core'=2,'coef'=8] {'plane'}, dimensions={0} | all-to-all | bytes 1310720 | tf_op jit(solution)/shard_map/all_to_all | solution.py:442
  98.7 4.0 %collective-permute-start.3 = (f32[4,4,8,1280]{3,2,1,0:T(8,128)S(1)}, f32[4,4,8,1280]{3,2,1,0:T(8,128)S(1)}, u32[]{:S(2)}, u32[]{:S(2)}) collective-permute-start(f32[4,4,8,1280]{3,2,1,0:T(8,128)S(1)} %bitcast.11), channel_id=1, source_target_pairs={{0,8},{8,0},{1,9},{9,1},{2,10},{10,2},{3,11},{11,3},{4,12},{12,4},... | collective-permute-start | bytes 1966088 | tf_op jit(solution)/shard_map/ppermute | solution.py:443
  102.7 1.7 %collective-permute-done.3.got_ref = f32[4,4,8,1280]{3,2,1,0:T(8,128)S(1)} collective-permute-done((f32[4,4,8,1280]{3,2,1,0:T(8,128)S(1)}, f32[4,4,8,1280]{3,2,1,0:T(8,128)S(1)}, u32[]{:S(2)}, u32[]{:S(2)}) %collective-permute-start.3) | collective-permute-done | bytes 655392 | tf_op jit(solution)/shard_map/ppermute | solution.py:443
  104.4 0.0 copy-done.3
  104.4 0.0 copy-done.5
  104.4 2.5 %update.1 = (f32[64,4352]{1,0:T(8,128)}, f32[64,4352]{1,0:T(8,128)}, f32[64,4352]{1,0:T(8,128)}, f32[55,8,64]{2,1,0:T(8,128)}, f32[55,8,64]{2,1,0:T(8,128)}, /*index=5*/f32[55,8,64]{2,1,0:T(8,128)}) custom-call(f32[4,4,8,1280]{3,2,1,0:T(8,128)S(1)} %bitcast.12, f32[4,4,8,1280]{3,2,1,0:T(8,128)S(1)} %collective-permute-done.3.got_ref, ...), custom_call_target="tpu_custom_call" | custom-call | tf_op jit(solution)/shard_map/update/pallas_call | solution.py:446
  (2 shorter events, 0.1 us)
Async XLA Ops:
  0.6 10.4 %collective-permute-start = (f32[55,8,64]{2,1,0:T(8,128)}, f32[55,8,64]{2,1,0:T(8,128)S(1)}, u32[]{:S(2)}, u32[]{:S(2)}) collective-permute-start(f32[55,8,64]{2,1,0:T(8,128)} %bitcast.14), channel_id=1, source_target_pairs={{8,0},{16,8},{24,16},{32,24},{40,32},{48,40},{56,48},{64,56},{72,6... | collective-permute-start | bytes 337928 | tf_op jit(solution)/shard_map/ppermute | solution.py:331
  5.8 5.3 %copy-start.2 = (f32[64,55,8]{0,2,1:T(8,128)S(1)}, f32[64,55,8]{0,2,1:T(8,128)}, u32[]{:S(2)}) copy-start(f32[64,55,8]{0,2,1:T(8,128)} %param.27) | copy-start | bytes 337924
  11.9 33.5 %copy-start.7 = (f32[1024]{0:T(1024)S(1)}, f32[1024]{0:T(1024)}, u32[]{:S(2)}) copy-start(f32[1024]{0:T(1024)} %param.17) | copy-start | bytes 12292
  11.9 33.4 %copy-start.8 = (s32[8]{0:T(128)S(1)}, s32[8]{0:T(128)}, u32[]{:S(2)}) copy-start(s32[8]{0:T(128)} %count_ref.1) | copy-start | bytes 100
  47.1 6.5 %collective-permute-start.1 = (f32[55,8,64]{2,1,0:T(8,128)S(1)}, f32[55,8,64]{2,1,0:T(8,128)S(1)}, u32[]{:S(2)}, u32[]{:S(2)}) collective-permute-start(f32[55,8,64]{2,1,0:T(8,128)S(1)} %get-tuple-element.34), channel_id=1, source_target_pairs={{0,8},{8,16},{16,24},{24,32},{32,40},{40,48},{48,56},{56,64},{64,7... | collective-permute-start | bytes 337928 | tf_op jit(solution)/shard_map/ppermute | solution.py:398
  53.6 2.1 %collective-permute-start.2 = (f32[4,4,8,1152]{3,2,1,0:T(8,128)S(1)}, f32[4,4,8,1152]{3,2,1,0:T(8,128)S(1)}, u32[]{:S(2)}, u32[]{:S(2)}) collective-permute-start(f32[4,4,8,1152]{3,2,1,0:T(8,128)S(1)} %get-tuple-element.35), channel_id=1, source_target_pairs={{0,8},{8,0},{1,9},{9,1},{2,10},{10,2},{3,11},{11,3},{4,12},{12,4},... | collective-permute-start | bytes 1769480 | tf_op jit(solution)/shard_map/ppermute | solution.py:413
  55.7 19.6 %copy-start = (f32[64,4352]{1,0:T(8,128)S(1)}, f32[64,4352]{1,0:T(8,128)}, u32[]{:S(2)}) copy-start(f32[64,4352]{1,0:T(8,128)} %dir_ref.3) | copy-start | bytes 3342340
  55.7 19.6 %copy-start.1 = (f32[64,4352]{1,0:T(8,128)S(1)}, f32[64,4352]{1,0:T(8,128)}, u32[]{:S(2)}) copy-start(f32[64,4352]{1,0:T(8,128)} %res_ref.3) | copy-start | bytes 3342340
  55.7 19.6 %copy-start.4 = (f32[64,55,8]{0,2,1:T(8,128)S(1)}, f32[64,55,8]{0,2,1:T(8,128)}, u32[]{:S(2)}) copy-start(f32[64,55,8]{0,2,1:T(8,128)} %param.26) | copy-start | bytes 337924
  55.7 19.6 %copy-start.6 = (f32[4352]{0:T(1024)S(1)}, f32[4352]{0:T(1024)}, u32[]{:S(2)}) copy-start(f32[4352]{0:T(1024)} %param.20) | copy-start | bytes 52228
  55.7 19.6 %copy-start.9 = (f32[55]{0:T(128)S(1)}, f32[55]{0:T(128)}, u32[]{:S(2)}) copy-start(f32[55]{0:T(128)} %cdamp_ref.1) | copy-start | bytes 664
  76.4 28.0 %copy-start.3 = (f32[64,4352]{1,0:T(8,128)S(1)}, f32[64,4352]{1,0:T(8,128)}, u32[]{:S(2)}) copy-start(f32[64,4352]{1,0:T(8,128)} %sol_ref.1) | copy-start | bytes 3342340
  76.4 28.0 %copy-start.5 = (f32[64,55,8]{0,2,1:T(8,128)S(1)}, f32[64,55,8]{0,2,1:T(8,128)}, u32[]{:S(2)}) copy-start(f32[64,55,8]{0,2,1:T(8,128)} %param.25) | copy-start | bytes 337924
  98.7 5.7 %collective-permute-start.3 = (f32[4,4,8,1280]{3,2,1,0:T(8,128)S(1)}, f32[4,4,8,1280]{3,2,1,0:T(8,128)S(1)}, u32[]{:S(2)}, u32[]{:S(2)}) collective-permute-start(f32[4,4,8,1280]{3,2,1,0:T(8,128)S(1)} %bitcast.11), channel_id=1, source_target_pairs={{0,8},{8,0},{1,9},{9,1},{2,10},{10,2},{3,11},{11,3},{4,12},{12,4},... | collective-permute-start | bytes 1966088 | tf_op jit(solution)/shard_map/ppermute | solution.py:443

commit v3 on v2

--- a/solution.py
+++ b/solution.py
@@ -101,7 +101,8 @@
 
 def core_forward_kernel(lith_ref, cdir_ref, halo_ref, ghi_ref, glo_ref, out_ref, ext):
     ext[0:NJ, 0:8, :] = cdir_ref[...]
-    ext[0:NJ, 8:16, :] = halo_ref[...]
+    last = jnp.logical_and(lax.axis_index("plane") == 15, lax.axis_index("core") == 1)
+    ext[0:NJ, 8:16, :] = halo_ref[...] * jnp.where(last, 0.0, 1.0)
     ext[NJ:JP] = jnp.zeros((1, 16, MEM), F32)
     high, low = split(jnp.transpose(ext[...].reshape(JP * 16, MEM)))
     both = jnp.concatenate([high, low], axis=0)
@@ -139,7 +140,7 @@
     )
     grad = (wide[:, 0:MEM] + wide[:, MEM:] + low).reshape(JP, 16, MEM)
     local_ref[...] = grad[0:NJ, 0:8, :]
-    halo_ref[...] = grad[0:NJ, 8:16, :]
+    halo_ref[...] = jnp.concatenate([grad[0 : JP // 2, 8:16, :], grad[JP // 2 :, 8:16, :]], axis=2)
 
 
 def back_kernel(pair_ref, a_ref, own_ref, other_ref, lhs):
@@ -160,8 +161,25 @@
         out[:, 3, :, NL - 3 * WIDE :] = jnp.zeros((4, 8, 4 * WIDE - NL), F32)
 
 
-def add_kernel(a_ref, b_ref, out_ref):
+def add_kernel(
+    a_ref, b_ref, tile_ref, local_ref, halo_ref, cdir_ref, cres_ref, cdamp_ref, out_ref, tile_out_ref, cimage_ref
+):
     out_ref[...] = a_ref[...] + b_ref[...]
+    cross = jnp.zeros((8, MEM), F32)
+    norm = jnp.zeros((8, MEM), F32)
+    first = jnp.logical_and(lax.axis_index("plane") == 0, lax.axis_index("core") == 0)
+    later = jnp.where(first, 0.0, 1.0)
+    for j in range(NJ):
+        packed = halo_ref[j % (JP // 2)]
+        halo = packed[:, 0:MEM] if j < JP // 2 else packed[:, MEM:]
+        core_image = local_ref[j] + later * halo + cdamp_ref[j] * cdir_ref[j]
+        cimage_ref[j] = core_image
+        cross = cross + cres_ref[j] * core_image
+        norm = norm + core_image * core_image
+    zero = jnp.zeros((1, MEM), F32)
+    tile_out_ref[...] = tile_ref[...] + tile_of(
+        [zero, zero, jnp.sum(cross, axis=0, keepdims=True), jnp.sum(norm, axis=0, keepdims=True)]
+    )
 
 
 def turned(row):
@@ -200,81 +218,83 @@
     return jnp.sum(jnp.transpose(padded), axis=0, keepdims=True)[:, 0:MEM]
 
 
-def image_kernel(
-    parts_ref, local_ref, halo_ref, cdir_ref, cres_ref, curve_ref, dir_ref, res_ref, damp_ref, cdamp_ref,
-    chunk_ref, cimage_ref, sums_ref, square,
-):
-    zero = jnp.zeros((8, MEM), F32)
-    before, curve, cross, norm = zero, zero, zero, zero
+def tile_of(rows):
+    tile = jnp.concatenate(rows + [jnp.zeros((8 - len(rows), MEM), F32)], axis=0)
+    return jnp.concatenate([tile, jnp.zeros((8, 128 - MEM), F32)], axis=1)
+
+
+def known_sums_kernel(cdir_ref, cres_ref, dir_ref, res_ref, damp_ref, cdamp_ref, tile_ref):
+    before = jnp.zeros((8, MEM), F32)
+    curve = jnp.zeros((8, MEM), F32)
     for j in range(NJ):
-        residual = cres_ref[j]
-        damped = cdamp_ref[j] * cdir_ref[j]
-        core_image = local_ref[j] + halo_ref[j] + damped
-        cimage_ref[j] = core_image
-        before = before + residual * residual
-        curve = curve + damped * cdir_ref[j]
-        cross = cross + residual * core_image
-        norm = norm + core_image * core_image
-    total = parts_ref[0]
-    for k in range(1, 16):
-        total = total + parts_ref[k]
-    chunk_ref[...] = total
-    square[...] = jnp.zeros((2, MEM, 128), F32)
-    plane = lax.axis_index("plane")
-    core = lax.axis_index("core")
-    rows = pl.ds(pl.multiple_of((core * 4 + plane // 4) * 8, 8), 8)
-
-    def finish(y):
-        cols = columns_of(y)
-        count = cols.stop - cols.start
-        value = chunk_ref[:, 0:count] + damp_rows(damp_ref, cols) * dir_ref[rows, cols]
-        chunk_ref[:, 0:count] = value
-        square[0, rows, :] = folded(value * res_ref[rows, cols])
-        square[1, rows, :] = folded(value * value)
-
-    for y in range(4):
-        pl.when(lax.rem(plane, 4) == y)(lambda y=y: finish(y))
+        before = before + cres_ref[j] * cres_ref[j]
+        curve = curve + cdamp_ref[j] * (cdir_ref[j] * cdir_ref[j])
     lith_before = jnp.zeros((MEM, SEG), F32)
     lith_curve = jnp.zeros((MEM, SEG), F32)
     for t in range(NL // SEG):
         cols = slice(t * SEG, (t + 1) * SEG)
         lith_before = lith_before + res_ref[:, cols] * res_ref[:, cols]
         lith_curve = lith_curve + dir_ref[:, cols] * dir_ref[:, cols] * damp_ref[t : t + 1, :]
-    once = jnp.where(jnp.logical_and(plane == 0, core == 0), 1.0, 0.0)
+    once = jnp.logical_and(lax.axis_index("plane") == 0, lax.axis_index("core") == 0)
+    once = jnp.where(once, 1.0, 0.0)
+    tile_ref[...] = tile_of(
+        [
+            jnp.sum(c, axis=0, keepdims=True) + once * member_row(v)
+            for c, v in ((before, lith_before), (curve, lith_curve))
+        ]
+    )
+
+
+def image_kernel(parts_ref, curve_ref, dir_ref, res_ref, damp_ref, tile_ref, out_ref, image, square):
+    total = parts_ref[0]
+    for k in range(1, 16):
+        total = total + parts_ref[k]
+    image[...] = total
+    square[...] = jnp.zeros((2, MEM, 128), F32)
+    plane = lax.axis_index("plane")
+    rows = pl.ds(pl.multiple_of((lax.axis_index("core") * 4 + plane // 4) * 8, 8), 8)
+
+    def finish(y):
+        cols = columns_of(y)
+        count = cols.stop - cols.start
+        value = image[:, 0:count] + damp_rows(damp_ref, cols) * dir_ref[rows, cols]
+        image[:, 0:count] = value
+        square[0, rows, :] = folded(value * res_ref[rows, cols])
+        square[1, rows, :] = folded(value * value)
+
+    for y in range(4):
+        pl.when(lax.rem(plane, 4) == y)(lambda y=y: finish(y))
     first = jnp.where(lax.axis_index("coef") == 0, 1.0, 0.0)
-    lith_curve = once * lith_curve + first * curve_ref[...]
-    rows_of = [
-        (before, once * lith_before), (curve, lith_curve), (cross, square[0]), (norm, square[1])
-    ]
-    tile = jnp.concatenate(
-        [jnp.sum(c, axis=0, keepdims=True) + member_row(v) for c, v in rows_of]
-        + [jnp.zeros((4, MEM), F32)],
-        axis=0,
-    )
-    tile = jnp.concatenate([tile, jnp.zeros((8, 128 - MEM), F32)], axis=1)
-    for k in range(8):
-        sums_ref[k] = tile
-
-
-def spread_kernel(sums_ref, chunk_ref, out_ref):
-    tile = sums_ref[0]
-    for k in range(1, 8):
-        tile = tile + sums_ref[k]
+    tile = tile_ref[...] + tile_of(
+        [
+            jnp.zeros((1, MEM), F32),
+            first * member_row(curve_ref[...]),
+            member_row(square[0]),
+            member_row(square[1]),
+        ]
+    )
     for k in range(16):
-        out_ref[k, :, 0:WIDE] = chunk_ref[...]
+        out_ref[k, :, 0:WIDE] = image[...]
         out_ref[k, :, WIDE:] = tile
 
 
+def plane_sum_kernel(whole_ref, out_ref):
+    tile = whole_ref[0]
+    for k in range(1, 16):
+        tile = tile + whole_ref[k]
+    for k in range(16):
+        out_ref[k] = tile
+
+
 def update_kernel(
-    own_ref, got_ref, sol_ref, res_ref, dir_ref, cimage_ref, csol_ref, cres_ref, cdir_ref,
+    own_ref, got_ref, sums_ref, sol_ref, res_ref, dir_ref, cimage_ref, csol_ref, cres_ref, cdir_ref,
     sol_hbm, res_hbm, dir_hbm, csol_hbm, cres_hbm, cdir_hbm,
     sol_buf, res_buf, dir_buf, csol_buf, cres_buf, cdir_buf, step_col, ratio_col, core_sems, sems,
 ):
     core = lax.axis_index("core")
-    tile = jnp.zeros((8, 128), F32)
-    for x in range(4):
-        for y in range(4):
-            tile = tile + (own_ref[x, y, :, WIDE:] + got_ref[x, y, :, WIDE:])
+    tile = sums_ref[0]
+    for k in range(1, 16):
+        tile = tile + sums_ref[k]
     tile = tile[:, 0:MEM]
     before = tile[0:1]
     step = before / tile[1:2]
@@ -328,7 +348,7 @@
     phase = sample_phase.reshape(8, SEG)
     weight = data_weight.reshape(8, SEG)
     damp = lith_damping.reshape(NL // SEG, SEG)
-    upper = lax.ppermute(cdir, segments, [(t, t - 1) for t in range(1, tm)])
+    upper = lax.ppermute(cdir, segments, [(t, (t - 1) % tm) for t in range(tm)])
     product_cost = pl.CostEstimate(
         flops=16 * MEM * NL * NS, bytes_accessed=12 * MIB, transcendentals=0
     )
@@ -387,7 +407,7 @@
         out_shape=(
             struct((2 * MEM, NS), BF16),
             struct((NJ, 8, MEM)),
-            struct((NJ, 8, MEM)),
+            struct((JP // 2, 8, 2 * MEM)),
             struct((MEM, SEG)),
         ),
         in_specs=[VM] * 4 + [SM],
@@ -395,7 +415,7 @@
         compiler_params=params(16),
         name="core_back",
     )(field, weight, ghi, glo, counts)
-    lower = lax.ppermute(halo, segments, [(t, t + 1) for t in range(tm - 1)])
+    lower = lax.ppermute(halo, segments, [(t, (t + 1) % tm) for t in range(tm)])
 
     chunks = struct((4, 4, 8, WIDE))
     core_struct = struct((NJ, 8, MEM))
@@ -409,44 +429,54 @@
         cost_estimate=product_cost,
         name="back",
     )(pair, design)
-    other, lower = lax.optimization_barrier((other, lower))
     got = lax.ppermute(other, "core", swap)
-    terms = pl.pallas_call(
-        add_kernel,
-        out_shape=chunks,
-        in_specs=[VM, VM],
+    known = pl.pallas_call(
+        known_sums_kernel,
+        out_shape=struct((8, 128)),
+        in_specs=[VM] * 5 + [SM],
         out_specs=VM,
         compiler_params=params(8),
+        name="known_sums",
+    )(cdir, cres, lith_direction, lith_residual, damp, core_damping)
+
+    terms, known, cimage = pl.pallas_call(
+        add_kernel,
+        out_shape=(chunks, struct((8, 128)), core_struct),
+        in_specs=[VM] * 7 + [SM],
+        out_specs=(VM,) * 3,
+        compiler_params=params(8),
         name="add_halves",
-    )(own, got)
+    )(own, got, known, local, lower, cdir, cres, core_damping)
 
     pieces = lax.all_to_all(terms.reshape(16, 8, WIDE), "plane", 0, 0)
-    chunk, cimage, sums = pl.pallas_call(
+    sent = pl.pallas_call(
         image_kernel,
-        out_shape=(struct((8, WIDE)), core_struct, struct((8, 8, 128))),
-        in_specs=[VM] * 9 + [SM],
-        out_specs=(VM, VM, VM),
-        scratch_shapes=[pltpu.VMEM((2, MEM, 128), F32)],
+        out_shape=struct((16, 8, SENT)),
+        in_specs=[VM] * 6,
+        out_specs=VM,
+        scratch_shapes=[pltpu.VMEM((8, WIDE), F32), pltpu.VMEM((2, MEM, 128), F32)],
         compiler_params=params(12),
         name="image",
-    )(pieces, local, lower, cdir, cres, curve, lith_direction, lith_residual, damp, core_damping)
-    sums = lax.all_to_all(sums, "coef", 0, 0)
-    sent = pl.pallas_call(
-        spread_kernel,
-        out_shape=struct((16, 8, SENT)),
-        in_specs=[VM, VM],
-        out_specs=VM,
+    )(pieces, curve, lith_direction, lith_residual, damp, known)
+    whole = lax.all_to_all(sent, "plane", 0, 0)
+    rest = lax.ppermute(whole, "core", swap).reshape(4, 4, 8, SENT)
+    sums = pl.pallas_call(
+        plane_sum_kernel,
+        grid=(1,),
+        out_shape=struct((16, 8, 128)),
+        in_specs=[pl.BlockSpec((16, 8, 128), lambda i: (0, 0, WIDE // 128))],
+        out_specs=pl.BlockSpec((16, 8, 128), lambda i: (0, 0, 0)),
         compiler_params=params(8),
-        name="spread",
-    )(sums, chunk)
-    whole = lax.all_to_all(sent, "plane", 0, 0).reshape(4, 4, 8, SENT)
-    rest = lax.ppermute(whole, "core", swap)
+        name="plane_sum",
+    )(whole)
+    sums = lax.all_to_all(sums, ("core", "coef"), 0, 0)
+    whole = whole.reshape(4, 4, 8, SENT)
 
     lith_struct = struct((MEM, NL))
     new_sol, new_res, new_dir, new_csol, new_cres, new_cdir = pl.pallas_call(
         update_kernel,
         out_shape=(lith_struct,) * 3 + (core_struct,) * 3,
-        in_specs=[VM] * 9,
+        in_specs=[VM] * 10,
         out_specs=(HB,) * 6,
         scratch_shapes=[pltpu.VMEM((MEM, NL), F32)] * 3
         + [pltpu.VMEM((NJ, 8, MEM), F32)] * 3
@@ -455,7 +485,7 @@
         compiler_params=params(20),
         name="update",
     )(
-        whole, rest, lith_solution, lith_residual, lith_direction, cimage, csol, cres, cdir,
+        whole, rest, sums, lith_solution, lith_residual, lith_direction, cimage, csol, cres, cdir,
     )
     back = lambda v: jnp.transpose(v, (2, 0, 1))
     return new_sol, new_res, new_dir, back(new_csol), back(new_cres), back(new_cdir)

time: 107 us -> 99.6 us (0.931)
  blocking collectives: 75.2 us -> 67.3 us
  waiting for transfers between devices: 3.72 us -> 0.92 us
  starting transfers between devices: 12.7 us -> 15.1 us
    ppermute x1, starting transfers between devices: 0.09 us -> 7.3 us  [shards(): got = lax.ppermute(other, 'core', swap)]
    ppermute x3, starting transfers between devices: 12.6 us -> 7.85 us  [the longest x1 3.95 us: shards(): rest = lax.ppermute(whole, 'core', swap).reshape(4, 4, 8, SENT)]
    all_to_all x1, blocking collectives: 18.7 us -> 15.6 us  [shards(): parts = lax.all_to_all(partial, 'coef', 0, 0)]
    all_to_all x1, blocking collectives: 14.7 us -> 11.7 us  [shards(): field = lax.all_to_all(total, 'coef', 0, 0)]
    all_to_all x1, blocking collectives: 19.5 us -> 17.3 us  [shards(): pieces = lax.all_to_all(terms.reshape(16, 8, WIDE), 'plane', 0, 0)]
    ppermute x1, waiting for transfers between devices: 1.99 us -> 0.01 us  [shards(): got = lax.ppermute(other, 'core', swap)]
  transfers between devices with their start and end apart: 4 -> 4, of which waited for: 2 -> 1; matrix products, arithmetic and copies ran while one was open for 0% -> 0% of each run, Pallas kernels for 8% -> 6%
where the time goes in v3:
time: 99.6 us; the launch traced here: 99.3 us
  blocking collectives  67.3 us (68%)
  starting transfers between devices  15.1 us (15%)
  Pallas kernels  15.1 us (15%)
    all_to_all x1, blocking collectives, shards(): pieces = lax.all_to_all(terms.reshape(16, 8, WIDE), 'plane', 0, 0)  17.3 us
    all_to_all x1, blocking collectives, shards(): parts = lax.all_to_all(partial, 'coef', 0, 0)  15.6 us
    all_to_all x1, blocking collectives, shards(): whole = lax.all_to_all(sent, 'plane', 0, 0)  13.1 us
    all_to_all x1, blocking collectives, shards(): field = lax.all_to_all(total, 'coef', 0, 0)  11.7 us
    all_to_all x1, blocking collectives, shards(): sums = lax.all_to_all(sums, ('core', 'coef'), 0, 0)  9.62 us
    ppermute x1, starting transfers between devices, shards(): got = lax.ppermute(other, 'core', swap)  7.3 us
    pallas_call x1, Pallas kernels, shards(): pl.pallas_call(forward_kernel, out_shape=(struct((MEM, NS)), pltpu.VMEM((...  5.31 us
    ppermute x1, starting transfers between devices, shards(): rest = lax.ppermute(whole, 'core', swap).reshape(4, 4, 8, SENT)  3.95 us
  transfers between devices with their start and end apart: 4, of which 1 were waited for; matrix products, arithmetic and copies ran while one was open for 0% of the time, Pallas kernels for 6%

profile of v3, /device:TPU:1, one launch (start us, length us, event | category | flops | bytes accessed | tf_op | source)
XLA Modules:
  0.0 99.3 jit_solution(9584753737258753978)
XLA Ops:
  0.6 3.3 %collective-permute-start = (f32[55,8,64]{2,1,0:T(8,128)}, f32[55,8,64]{2,1,0:T(8,128)S(1)}, u32[]{:S(2)}, u32[]{:S(2)}) collective-permute-start(f32[55,8,64]{2,1,0:T(8,128)} %bitcast.13), channel_id=1, source_target_pairs={{0,248},{8,0},{16,8},{24,16},{32,24},{40,32},{48,40},{56,48},{64,5... | collective-permute-start | bytes 337928 | tf_op jit(solution)/shard_map/ppermute | solution.py:351
  4.0 0.0 copy-start.2
  4.0 5.3 %forward.1 = (f32[64,1024]{1,0:T(8,128)S(1)}, bf16[4352,1024]{1,0:T(8,128)(2,1)S(1)}, bf16[896,1024]{1,0:T(8,128)(2,1)S(1)}, bf16[896,1024]{1,0:T(8,128)(2,1)S(1)}) custom-call(f32[64,4352]{1,0:T(8,128)} %dir_ref.5, bf16[4352,1024]{1,0:T(8,128)(2,1)} %a_hbm.1, bf16[55,1024]{1,0:T(8,128)(2,1)} %design_hbm.1, f32[8,128]{1,0:T(8,128)} %bitcast.30, s32[8]{0:T(128)} %knot_hbm.1), custom_call_target="tpu_custom_call" | custom-call | flops 4563402752 | bytes 12582912 | tf_op jit(solution)/shard_map/forward/pallas_call | solution.py:357
  9.3 0.0 collective-permute-done.halo_ref
  9.3 0.0 copy-done.2
  9.3 0.8 core_forward.1
  10.1 0.0 copy-start.7
  10.1 0.0 copy-start.9
  10.1 15.6 %all_to_all.25.parts_ref = f32[8,8,1024]{2,1,0:T(8,128)S(1)} all-to-all(f32[8,8,1024]{2,1,0:T(8,128)S(1)} %core_forward.1), channel_id=1, replica_groups=mesh['plane'=16,'core'=2,'coef'=8] {'coef'}, dimensions={0} | all-to-all | bytes 524288 | tf_op jit(solution)/shard_map/all_to_all | solution.py:394
  25.7 11.7 %all_to_all.26.field_ref = f32[8,8,1024]{2,1,0:T(8,128)S(1)} all-to-all(f32[8,8,1024]{2,1,0:T(8,128)S(1)} %field_sum.1), channel_id=1, replica_groups=mesh['plane'=16,'core'=2,'coef'=8] {'coef'}, dimensions={0} | all-to-all | bytes 524288 | tf_op jit(solution)/shard_map/all_to_all | solution.py:403
  37.5 0.0 copy-done.7
  37.5 0.0 copy-done.9
  37.5 1.8 %core_back.1 = (bf16[128,1024]{1,0:T(8,128)(2,1)S(1)}, f32[55,8,64]{2,1,0:T(8,128)S(1)}, f32[28,8,128]{2,1,0:T(8,128)S(1)}, f32[64,128]{1,0:T(8,128)S(1)}) custom-call(f32[8,8,1024]{2,1,0:T(8,128)S(1)} %all_to_all.26.field_ref, f32[8,128]{1,0:T(8,128)S(1)} %bitcast.26, bf16[896,1024]{1,0:T(8,128)(2,1)S(1)} %get-tuple-element.26.ghi_ref, ...), custom_call_target="tpu_custom_call" | custom-call | tf_op jit(solution)/shard_map/core_back/pallas_call | solution.py:405
  39.3 0.0 copy-start
  39.3 0.0 copy-start.1
  39.3 0.0 copy-start.3
  39.3 0.0 copy-start.6
  39.3 0.0 copy-start.8
  39.4 2.9 %back.1 = (f32[4,4,8,1152]{3,2,1,0:T(8,128)S(1)}, f32[4,4,8,1152]{3,2,1,0:T(8,128)S(1)}) custom-call(bf16[128,1024]{1,0:T(8,128)(2,1)S(1)} %get-tuple-element.28.pair_ref, bf16[4352,1024]{1,0:T(8,128)(2,1)S(1)} %get-tuple-element.29.a_ref), custom_call_target="tpu_custom_call" | custom-call | flops 4563402752 | bytes 12582912 | tf_op jit(solution)/shard_map/back/pallas_call | solution.py:422
  42.3 7.3 %collective-permute-start.1 = (f32[4,4,8,1152]{3,2,1,0:T(8,128)S(1)}, f32[4,4,8,1152]{3,2,1,0:T(8,128)S(1)}, u32[]{:S(2)}, u32[]{:S(2)}) collective-permute-start(f32[4,4,8,1152]{3,2,1,0:T(8,128)S(1)} %get-tuple-element.31), channel_id=1, source_target_pairs={{0,8},{8,0},{1,9},{9,1},{2,10},{10,2},{3,11},{11,3},{4,12},{12,4},... | collective-permute-start | bytes 1769480 | tf_op jit(solution)/shard_map/ppermute | solution.py:432
  49.6 0.6 collective-permute-start.2
  50.2 0.0 copy-done
  50.2 0.0 copy-done.1
  50.2 0.0 copy-done.3
  50.2 0.0 copy-done.6
  50.2 0.0 copy-done.8
  50.2 0.9 known_sums.1.tile_ref
  51.0 0.9 collective-permute-done.2.halo_ref
  52.0 0.0 collective-permute-done.1.b_ref
  52.0 0.7 add_halves.1
  52.7 17.3 %all_to_all.27.parts_ref = f32[16,8,1152]{2,1,0:T(8,128)S(1)} all-to-all(f32[16,8,1152]{2,1,0:T(8,128)S(1)} %bitcast.22), channel_id=1, replica_groups=mesh['plane'=16,'core'=2,'coef'=8] {'plane'}, dimensions={0} | all-to-all | bytes 1179648 | tf_op jit(solution)/shard_map/all_to_all | solution.py:451
  70.0 0.2 image.1
  70.2 0.0 copy-start.4
  70.2 0.0 copy-start.5
  70.2 13.1 %all_to_all.28.whole_ref = f32[16,8,1280]{2,1,0:T(8,128)S(1)} all-to-all(f32[16,8,1280]{2,1,0:T(8,128)S(1)} %image.1), channel_id=1, replica_groups=mesh['plane'=16,'core'=2,'coef'=8] {'plane'}, dimensions={0} | all-to-all | bytes 1310720 | tf_op jit(solution)/shard_map/all_to_all | solution.py:461
  83.3 4.0 %collective-permute-start.3 = (f32[16,8,1280]{2,1,0:T(8,128)S(1)}, f32[16,8,1280]{2,1,0:T(8,128)S(1)}, u32[]{:S(2)}, u32[]{:S(2)}) collective-permute-start(f32[16,8,1280]{2,1,0:T(8,128)S(1)} %all_to_all.28.whole_ref), channel_id=1, source_target_pairs={{0,8},{8,0},{1,9},{9,1},{2,10},{10,2},{3,11},{11,3},{4,12},{12,4},... | collective-permute-start | bytes 1966088 | tf_op jit(solution)/shard_map/ppermute | solution.py:462
  87.3 9.6 %all_to_all.29.sums_ref = f32[16,8,128]{2,1,0:T(8,128)S(1)} all-to-all(f32[16,8,128]{2,1,0:T(8,128)S(1)} %plane_sum.1), channel_id=1, replica_groups=mesh['plane'=16,'core'=2,'coef'=8] {'core','coef'}, dimensions={0} | all-to-all | bytes 131072 | tf_op jit(solution)/shard_map/all_to_all | solution.py:472
  96.9 0.0 collective-permute-done.3
  96.9 0.0 copy-done.4
  96.9 0.0 copy-done.5
  96.9 2.4 %update.1 = (f32[64,4352]{1,0:T(8,128)}, f32[64,4352]{1,0:T(8,128)}, f32[64,4352]{1,0:T(8,128)}, f32[55,8,64]{2,1,0:T(8,128)}, f32[55,8,64]{2,1,0:T(8,128)}, /*index=5*/f32[55,8,64]{2,1,0:T(8,128)}) custom-call(f32[4,4,8,1280]{3,2,1,0:T(8,128)S(1)} %bitcast.12, f32[4,4,8,1280]{3,2,1,0:T(8,128)S(1)} %bitcast.21, f32[16,8,128]{2,1,0:T(8,128)S(1)} %all_to_all.29.sums_ref, ...), custom_call_target="tpu_custom_call" | custom-call | tf_op jit(solution)/shard_map/update/pallas_call | solution.py:476
  (2 shorter events, 0.0 us)
Async XLA Ops:
  0.6 8.6 %collective-permute-start = (f32[55,8,64]{2,1,0:T(8,128)}, f32[55,8,64]{2,1,0:T(8,128)S(1)}, u32[]{:S(2)}, u32[]{:S(2)}) collective-permute-start(f32[55,8,64]{2,1,0:T(8,128)} %bitcast.13), channel_id=1, source_target_pairs={{0,248},{8,0},{16,8},{24,16},{32,24},{40,32},{48,40},{56,48},{64,5... | collective-permute-start | bytes 337928 | tf_op jit(solution)/shard_map/ppermute | solution.py:351
  4.0 5.3 %copy-start.2 = (f32[64,55,8]{0,2,1:T(8,128)S(1)}, f32[64,55,8]{0,2,1:T(8,128)}, u32[]{:S(2)}) copy-start(f32[64,55,8]{0,2,1:T(8,128)} %param.27) | copy-start | bytes 337924
  10.1 27.4 %copy-start.7 = (f32[1024]{0:T(1024)S(1)}, f32[1024]{0:T(1024)}, u32[]{:S(2)}) copy-start(f32[1024]{0:T(1024)} %param.17) | copy-start | bytes 12292
  10.1 27.4 %copy-start.9 = (s32[8]{0:T(128)S(1)}, s32[8]{0:T(128)}, u32[]{:S(2)}) copy-start(s32[8]{0:T(128)} %count_ref.1) | copy-start | bytes 100
  39.3 10.9 %copy-start = (f32[64,4352]{1,0:T(8,128)S(1)}, f32[64,4352]{1,0:T(8,128)}, u32[]{:S(2)}) copy-start(f32[64,4352]{1,0:T(8,128)} %dir_ref.5) | copy-start | bytes 3342340
  39.3 10.8 %copy-start.1 = (f32[64,4352]{1,0:T(8,128)S(1)}, f32[64,4352]{1,0:T(8,128)}, u32[]{:S(2)}) copy-start(f32[64,4352]{1,0:T(8,128)} %res_ref.5) | copy-start | bytes 3342340
  39.3 10.8 %copy-start.3 = (f32[64,55,8]{0,2,1:T(8,128)S(1)}, f32[64,55,8]{0,2,1:T(8,128)}, u32[]{:S(2)}) copy-start(f32[64,55,8]{0,2,1:T(8,128)} %param.26) | copy-start | bytes 337924
  39.3 10.8 %copy-start.6 = (f32[4352]{0:T(1024)S(1)}, f32[4352]{0:T(1024)}, u32[]{:S(2)}) copy-start(f32[4352]{0:T(1024)} %param.20) | copy-start | bytes 52228
  39.3 10.8 %copy-start.8 = (f32[55]{0:T(128)S(1)}, f32[55]{0:T(128)}, u32[]{:S(2)}) copy-start(f32[55]{0:T(128)} %cdamp_ref.3) | copy-start | bytes 664
  42.3 9.7 %collective-permute-start.1 = (f32[4,4,8,1152]{3,2,1,0:T(8,128)S(1)}, f32[4,4,8,1152]{3,2,1,0:T(8,128)S(1)}, u32[]{:S(2)}, u32[]{:S(2)}) collective-permute-start(f32[4,4,8,1152]{3,2,1,0:T(8,128)S(1)} %get-tuple-element.31), channel_id=1, source_target_pairs={{0,8},{8,0},{1,9},{9,1},{2,10},{10,2},{3,11},{11,3},{4,12},{12,4},... | collective-permute-start | bytes 1769480 | tf_op jit(solution)/shard_map/ppermute | solution.py:432
  49.6 2.4 %collective-permute-start.2 = (f32[28,8,128]{2,1,0:T(8,128)S(1)}, f32[28,8,128]{2,1,0:T(8,128)S(1)}, u32[]{:S(2)}, u32[]{:S(2)}) collective-permute-start(f32[28,8,128]{2,1,0:T(8,128)S(1)} %get-tuple-element.33), channel_id=1, source_target_pairs={{0,8},{8,16},{16,24},{24,32},{32,40},{40,48},{48,56},{56,64},{64,7... | collective-permute-start | bytes 344072 | tf_op jit(solution)/shard_map/ppermute | solution.py:418
  70.2 26.7 %copy-start.4 = (f32[64,4352]{1,0:T(8,128)S(1)}, f32[64,4352]{1,0:T(8,128)}, u32[]{:S(2)}) copy-start(f32[64,4352]{1,0:T(8,128)} %sol_ref.1) | copy-start | bytes 3342340
  70.2 26.7 %copy-start.5 = (f32[64,55,8]{0,2,1:T(8,128)S(1)}, f32[64,55,8]{0,2,1:T(8,128)}, u32[]{:S(2)}) copy-start(f32[64,55,8]{0,2,1:T(8,128)} %param.25) | copy-start | bytes 337924
  83.3 13.6 %collective-permute-start.3 = (f32[16,8,1280]{2,1,0:T(8,128)S(1)}, f32[16,8,1280]{2,1,0:T(8,128)S(1)}, u32[]{:S(2)}, u32[]{:S(2)}) collective-permute-start(f32[16,8,1280]{2,1,0:T(8,128)S(1)} %all_to_all.28.whole_ref), channel_id=1, source_target_pairs={{0,8},{8,0},{1,9},{9,1},{2,10},{10,2},{3,11},{11,3},{4,12},{12,4},... | collective-permute-start | bytes 1966088 | tf_op jit(solution)/shard_map/ppermute | solution.py:462

commit v4 on v3

--- a/solution.py
+++ b/solution.py
@@ -6,8 +6,9 @@
 from jax.sharding import PartitionSpec as P
 
 NL, NS, MEM, NJ, JP = 4352, 1024, 64, 55, 56
+GROWS = JP * 8
 SEG = 128
-WIDE, SENT = 1152, 1280
+WIDE, FULL, HALF, HALO = 1152, 1024, 64, 144
 MIB = 1 << 20
 F32, BF16 = jnp.float32, jnp.bfloat16
 VM = pl.BlockSpec(memory_space=pltpu.VMEM)
@@ -45,14 +46,26 @@
     return now
 
 
+def core_product(ext, ghi_ref, glo_ref, first):
+    high, low = split(jnp.transpose(ext[...].reshape(GROWS, MEM)))
+    both = jnp.concatenate([high, low], axis=0)
+    rows = slice(first, first + GROWS)
+    wide = jnp.dot(both, ghi_ref[rows, :], preferred_element_type=F32)
+    low = jnp.dot(high, glo_ref[rows, :], preferred_element_type=F32)
+    return wide[0:MEM] + wide[MEM:] + low
+
+
 def forward_kernel(
-    dir_hbm, a_hbm, design_hbm, phase_hbm, knot_hbm, out_ref, a_buf, ghi_ref, glo_ref,
-    dir_buf, lhs, acc, design_buf, phase_buf, knot_buf, basis, design, small_sems, sems,
+    dir_hbm, a_hbm, design_hbm, phase_hbm, knot_hbm, cdir_hbm, out_ref, a_buf, ghi_ref, glo_ref,
+    dir_buf, lhs, acc, design_buf, phase_buf, knot_buf, ext, basis, design, small_sems, sems,
 ):
     small = [
         pltpu.make_async_copy(src, dst, small_sems.at[k])
         for k, (src, dst) in enumerate(
-            ((phase_hbm, phase_buf), (knot_hbm, knot_buf), (design_hbm, design_buf), (dir_hbm, dir_buf))
+            (
+                (phase_hbm, phase_buf), (knot_hbm, knot_buf), (design_hbm, design_buf),
+                (cdir_hbm, ext.at[0:NJ]), (dir_hbm, dir_buf),
+            )
         )
     ]
     for copy in small:
@@ -63,7 +76,7 @@
         copy = pltpu.make_async_copy(a_hbm.at[rows], a_buf.at[rows], sems.at[b])
         copy.start()
         copies.append(copy)
-    for copy in small[0:3]:
+    for copy in small[0:4]:
         copy.wait()
     values = spline_values(phase_buf[...])
     row = lax.broadcasted_iota(jnp.int32, (16, SEG), 0)
@@ -77,14 +90,21 @@
     design[NJ:JP] = jnp.zeros((1, NS), F32)
 
     def build(j, carry):
-        high, low = split(basis[...] * design[pl.ds(j, 1), :])
-        rows = pl.ds(pl.multiple_of(j * 16, 16), 16)
-        ghi_ref[rows, :] = high
-        glo_ref[rows, :] = low
+        for part in range(2):
+            spline = basis[part * 8 : part * 8 + 8, :]
+            product = jnp.concatenate(
+                [spline * design[pl.ds(2 * j + k, 1), :] for k in range(2)], axis=0
+            )
+            high, low = split(product)
+            rows = pl.ds(pl.multiple_of(part * GROWS + j * 16, 16), 16)
+            ghi_ref[rows, :] = high
+            glo_ref[rows, :] = low
         return carry
 
-    lax.fori_loop(0, JP, build, 0)
-    small[3].wait()
+    lax.fori_loop(0, JP // 2, build, 0)
+    ext[NJ:JP] = jnp.zeros((1, 8, MEM), F32)
+    out_ref[...] = core_product(ext, ghi_ref, glo_ref, 0)
+    small[4].wait()
     for b, copy in enumerate(copies):
         lo, hi = FORWARD_CUTS[b], FORWARD_CUTS[b + 1]
         high, low = split(dir_buf[:, lo:hi])
@@ -96,19 +116,15 @@
             acc[...] = part
         else:
             acc[...] += part
-    out_ref[...] = acc[0:MEM] + acc[MEM:]
-
-
-def core_forward_kernel(lith_ref, cdir_ref, halo_ref, ghi_ref, glo_ref, out_ref, ext):
-    ext[0:NJ, 0:8, :] = cdir_ref[...]
+    out_ref[...] += acc[0:MEM] + acc[MEM:]
+
+
+def core_forward_kernel(lith_ref, halo_ref, ghi_ref, glo_ref, out_ref, ext):
     last = jnp.logical_and(lax.axis_index("plane") == 15, lax.axis_index("core") == 1)
-    ext[0:NJ, 8:16, :] = halo_ref[...] * jnp.where(last, 0.0, 1.0)
-    ext[NJ:JP] = jnp.zeros((1, 16, MEM), F32)
-    high, low = split(jnp.transpose(ext[...].reshape(JP * 16, MEM)))
-    both = jnp.concatenate([high, low], axis=0)
-    wide = jnp.dot(both, ghi_ref[...], preferred_element_type=F32)
-    value = wide[0:MEM] + wide[MEM:] + jnp.dot(high, glo_ref[...], preferred_element_type=F32)
-    out_ref[...] = (value + lith_ref[...]).reshape(8, 8, NS)
+    ext[0:NJ] = halo_ref[...] * jnp.where(last, 0.0, 1.0)
+    ext[NJ:JP] = jnp.zeros((1, 8, MEM), F32)
+    value = core_product(ext, ghi_ref, glo_ref, GROWS) + lith_ref[...]
+    out_ref[...] = value.reshape(8, 8, NS)
 
 
 def sum_kernel(parts_ref, out_ref):
@@ -119,8 +135,9 @@
         out_ref[k] = total
 
 
-def core_back_kernel(
-    field_ref, weight_ref, ghi_ref, glo_ref, count_ref, pair_ref, local_ref, halo_ref, curve_ref
+def back_kernel(
+    field_ref, weight_ref, ghi_ref, glo_ref, a_ref, count_ref,
+    own_ref, other_ref, local_ref, halo_ref, curve_ref, pair, lhs,
 ):
     lane = lax.broadcasted_iota(jnp.int32, (1, SEG), 1)
     curve = jnp.zeros((MEM, SEG), F32)
@@ -131,48 +148,53 @@
         residual = field * weight
         curve = curve + residual * field
         high, low = split(residual)
-        pair_ref[0:MEM, cols] = high
-        pair_ref[MEM:, cols] = low
+        pair[0:MEM, cols] = high
+        pair[MEM:, cols] = low
     curve_ref[...] = curve
-    wide = lax.dot_general(ghi_ref[...], pair_ref[...], TRANS_B, preferred_element_type=F32)
-    low = lax.dot_general(
-        glo_ref[...], pair_ref[0:MEM], TRANS_B, preferred_element_type=F32
-    )
-    grad = (wide[:, 0:MEM] + wide[:, MEM:] + low).reshape(JP, 16, MEM)
-    local_ref[...] = grad[0:NJ, 0:8, :]
-    halo_ref[...] = jnp.concatenate([grad[0 : JP // 2, 8:16, :], grad[JP // 2 :, 8:16, :]], axis=2)
-
-
-def back_kernel(pair_ref, a_ref, own_ref, other_ref, lhs):
     half = MEM // 2
     core = lax.axis_index("core")
     mine = pl.multiple_of(core * half, half)
     theirs = pl.multiple_of((1 - core) * half, half)
     for k, start in enumerate((mine, theirs, MEM + mine, MEM + theirs)):
-        lhs[k * half : (k + 1) * half] = pair_ref[pl.ds(pl.multiple_of(start, half), half), :]
+        lhs[k * half : (k + 1) * half] = pair[pl.ds(pl.multiple_of(start, half), half), :]
+
+    def product(rows):
+        part = lax.dot_general(lhs[...], a_ref[rows], TRANS_B, preferred_element_type=F32)
+        part = part[0:MEM] + part[MEM:]
+        return part[0:half], part[half:]
+
     for y in range(4):
-        cols = columns_of(y)
-        count = cols.stop - cols.start
-        part = lax.dot_general(lhs[...], a_ref[cols], TRANS_B, preferred_element_type=F32)
-        part = part[0:MEM] + part[MEM:]
-        own_ref[:, y, :, 0:count] = part[0:half].reshape(4, 8, count)
-        other_ref[:, y, :, 0:count] = part[half:].reshape(4, 8, count)
-    for out in (own_ref, other_ref):
-        out[:, 3, :, NL - 3 * WIDE :] = jnp.zeros((4, 8, 4 * WIDE - NL), F32)
+        for out, part in zip((own_ref, other_ref), product(slice(y * FULL, (y + 1) * FULL))):
+            out[:, y, :, 0:FULL] = part.reshape(4, 8, FULL)
+    for out, part in zip((own_ref, other_ref), product(slice(4 * FULL, NL))):
+        for y in range(4):
+            tail = part[:, y // 2 * SEG : (y // 2 + 1) * SEG]
+            out[:, y, :, FULL:] = tail.reshape(4, 8, SEG)
+    wide = lax.dot_general(ghi_ref[...], pair[...], TRANS_B, preferred_element_type=F32)
+    low = lax.dot_general(glo_ref[...], pair[0:MEM], TRANS_B, preferred_element_type=F32)
+    grad = (wide[:, 0:MEM] + wide[:, MEM:] + low).reshape(2, JP, 8, MEM)
+    local_ref[...] = grad[0, 0:NJ]
+    packed = jnp.concatenate([grad[1, 0 : JP // 2], grad[1, JP // 2 :]], axis=2)
+    for j in range(JP // 2):
+        halo_ref[j * 5 : j * 5 + 5, :] = packed[j, 0:5, :]
+    halo_ref[JP // 2 * 5 :, :] = jnp.zeros((HALO - JP // 2 * 5, 128), F32)
 
 
 def add_kernel(
-    a_ref, b_ref, tile_ref, local_ref, halo_ref, cdir_ref, cres_ref, cdamp_ref, out_ref, tile_out_ref, cimage_ref
+    own_ref, got_ref, tile_ref, local_ref, halo_ref, cdir_ref, cres_ref, cdamp_ref,
+    out_ref, tile_out_ref, cimage_ref,
 ):
-    out_ref[...] = a_ref[...] + b_ref[...]
+    out_ref[...] = own_ref[...] + got_ref[...]
     cross = jnp.zeros((8, MEM), F32)
     norm = jnp.zeros((8, MEM), F32)
     first = jnp.logical_and(lax.axis_index("plane") == 0, lax.axis_index("core") == 0)
-    later = jnp.where(first, 0.0, 1.0)
+    row = lax.broadcasted_iota(jnp.int32, (8, 128), 0)
+    inside = jnp.where(row < 5, jnp.where(first, 0.0, 1.0), 0.0)
     for j in range(NJ):
-        packed = halo_ref[j % (JP // 2)]
+        place = j % (JP // 2) * 5
+        packed = halo_ref[place : place + 8, :] * inside
         halo = packed[:, 0:MEM] if j < JP // 2 else packed[:, MEM:]
-        core_image = local_ref[j] + later * halo + cdamp_ref[j] * cdir_ref[j]
+        core_image = local_ref[j] + halo + cdamp_ref[j] * cdir_ref[j]
         cimage_ref[j] = core_image
         cross = cross + cres_ref[j] * core_image
         norm = norm + core_image * core_image
@@ -184,10 +206,6 @@
 
 def turned(row):
     return jnp.transpose(jnp.broadcast_to(row, (128, 128)))
-
-
-def columns_of(y):
-    return slice(y * WIDE, min((y + 1) * WIDE, NL))
 
 
 def out_copies(pairs, sems):
@@ -253,14 +271,19 @@
     square[...] = jnp.zeros((2, MEM, 128), F32)
     plane = lax.axis_index("plane")
     rows = pl.ds(pl.multiple_of((lax.axis_index("core") * 4 + plane // 4) * 8, 8), 8)
+    lane = lax.broadcasted_iota(jnp.int32, (8, SEG), 1)
+    mine = lane // HALF == lax.rem(plane, 2)
 
     def finish(y):
-        cols = columns_of(y)
-        count = cols.stop - cols.start
-        value = image[:, 0:count] + damp_rows(damp_ref, cols) * dir_ref[rows, cols]
-        image[:, 0:count] = value
-        square[0, rows, :] = folded(value * res_ref[rows, cols])
-        square[1, rows, :] = folded(value * value)
+        cols = slice(y * FULL, (y + 1) * FULL)
+        tail = slice(4 * FULL + y // 2 * SEG, 4 * FULL + (y // 2 + 1) * SEG)
+        value = image[:, 0:FULL] + damp_rows(damp_ref, cols) * dir_ref[rows, cols]
+        rest = image[:, FULL:] + damp_rows(damp_ref, tail) * dir_ref[rows, tail]
+        rest = jnp.where(mine, rest, 0.0)
+        image[:, 0:FULL] = value
+        image[:, FULL:] = rest
+        square[0, rows, :] = folded(value * res_ref[rows, cols]) + rest * res_ref[rows, tail]
+        square[1, rows, :] = folded(value * value) + rest * rest
 
     for y in range(4):
         pl.when(lax.rem(plane, 4) == y)(lambda y=y: finish(y))
@@ -273,15 +296,20 @@
             member_row(square[1]),
         ]
     )
+    tile = jnp.concatenate([tile[:, 0:HALF], tile[:, 0:HALF]], axis=1)
+    rest = jnp.where(mine, image[:, FULL:], tile)
     for k in range(16):
-        out_ref[k, :, 0:WIDE] = image[...]
-        out_ref[k, :, WIDE:] = tile
+        out_ref[k, :, 0:FULL] = image[:, 0:FULL]
+        out_ref[k, :, FULL:] = rest
 
 
 def plane_sum_kernel(whole_ref, out_ref):
-    tile = whole_ref[0]
-    for k in range(1, 16):
-        tile = tile + whole_ref[k]
+    even, odd = whole_ref[0], whole_ref[1]
+    for k in range(2, 16, 2):
+        even = even + whole_ref[k]
+        odd = odd + whole_ref[k + 1]
+    tile = odd[:, 0:HALF] + even[:, HALF:]
+    tile = jnp.concatenate([tile, jnp.zeros((8, SEG - HALF), F32)], axis=1)
     for k in range(16):
         out_ref[k] = tile
 
@@ -299,21 +327,36 @@
     before = tile[0:1]
     step = before / tile[1:2]
     ratio = (before + step * (step * tile[3:4] - 2.0 * tile[2:3])) / before
+    for j in range(NJ):
+        csol_buf[j] = csol_ref[j] + step * cdir_ref[j]
+        new_res = cres_ref[j] - step * cimage_ref[j]
+        cres_buf[j] = new_res
+        cdir_buf[j] = new_res + ratio * cdir_ref[j]
+    waits = out_copies(
+        [(csol_buf, csol_hbm), (cres_buf, cres_hbm), (cdir_buf, cdir_hbm)], core_sems
+    )
     blank = jnp.zeros((1, 128 - MEM), F32)
     step_col[...] = turned(jnp.concatenate([step, blank], axis=1))
     ratio_col[...] = turned(jnp.concatenate([ratio, blank], axis=1))
-    waits = []
-    for y in range(4):
-        cols = columns_of(y)
+    lane = lax.broadcasted_iota(jnp.int32, (8, SEG), 1)
+    for y in range(5):
+        cols = slice(y * FULL, min((y + 1) * FULL, NL))
         count = (cols.stop - cols.start) // SEG
         for k in range(8):
             ref, part = (own_ref, core) if k < 4 else (got_ref, 1 - core)
             rows = pl.ds(pl.multiple_of(part * 32 + (k % 4) * 8, 8), 8)
+            if y < 4:
+                image = ref[k % 4, y, :, 0:FULL]
+            else:
+                tails = [ref[k % 4, t, :, FULL:] for t in range(4)]
+                image = jnp.concatenate(
+                    [jnp.where(lane < HALF, tails[t], tails[t + 1]) for t in (0, 2)], axis=1
+                )
             scale = jnp.concatenate([step_col[rows, :]] * count, axis=1)
             other = jnp.concatenate([ratio_col[rows, :]] * count, axis=1)
             direction = dir_ref[rows, cols]
             sol_buf[rows, cols] = sol_ref[rows, cols] + scale * direction
-            new_res = res_ref[rows, cols] - scale * ref[k % 4, y, :, 0 : count * SEG]
+            new_res = res_ref[rows, cols] - scale * image
             res_buf[rows, cols] = new_res
             dir_buf[rows, cols] = new_res + other * direction
         waits += out_copies(
@@ -323,14 +366,6 @@
             ],
             sems.at[y],
         )
-    for j in range(NJ):
-        csol_buf[j] = csol_ref[j] + step * cdir_ref[j]
-        new_res = cres_ref[j] - step * cimage_ref[j]
-        cres_buf[j] = new_res
-        cdir_buf[j] = new_res + ratio * cdir_ref[j]
-    waits += out_copies(
-        [(csol_buf, csol_hbm), (cres_buf, cres_hbm), (cdir_buf, cdir_hbm)], core_sems
-    )
     for copy in waits:
         copy.wait()
 
@@ -362,7 +397,7 @@
             struct((JP * 16, NS), BF16),
             struct((JP * 16, NS), BF16),
         ),
-        in_specs=[HB] * 5,
+        in_specs=[HB] * 6,
         out_specs=(VM,) * 4,
         scratch_shapes=[
             pltpu.VMEM((MEM, NL), F32),
@@ -371,25 +406,26 @@
             pltpu.VMEM((NJ, NS), BF16),
             pltpu.VMEM((8, SEG), F32),
             pltpu.SMEM((8,), jnp.int32),
+            pltpu.VMEM((JP, 8, MEM), F32),
             pltpu.VMEM((16, NS), F32),
             pltpu.VMEM((JP, NS), F32),
-            pltpu.SemaphoreType.DMA((4,)),
+            pltpu.SemaphoreType.DMA((5,)),
             pltpu.SemaphoreType.DMA((len(FORWARD_CUTS) - 1,)),
         ],
         compiler_params=params(24),
         cost_estimate=product_cost,
         name="forward",
-    )(pin(lith_direction), pin(design_lith), pin(design_core), pin(phase), pin(knot_index))
+    )(pin(lith_direction), pin(design_lith), pin(design_core), pin(phase), pin(knot_index), pin(cdir))
 
     partial = pl.pallas_call(
         core_forward_kernel,
         out_shape=struct((8, 8, NS)),
-        in_specs=[VM] * 5,
+        in_specs=[VM] * 4,
         out_specs=VM,
-        scratch_shapes=[pltpu.VMEM((JP, 16, MEM), F32)],
+        scratch_shapes=[pltpu.VMEM((JP, 8, MEM), F32)],
         compiler_params=params(12),
         name="core_forward",
-    )(lith, cdir, upper, ghi, glo)
+    )(lith, upper, ghi, glo)
 
     parts = lax.all_to_all(partial, "coef", 0, 0)
     total = pl.pallas_call(
@@ -402,33 +438,19 @@
     )(parts)
     field = lax.all_to_all(total, "coef", 0, 0)
 
-    pair, local, halo, curve = pl.pallas_call(
-        core_back_kernel,
-        out_shape=(
-            struct((2 * MEM, NS), BF16),
-            struct((NJ, 8, MEM)),
-            struct((JP // 2, 8, 2 * MEM)),
-            struct((MEM, SEG)),
-        ),
-        in_specs=[VM] * 4 + [SM],
-        out_specs=(VM,) * 4,
-        compiler_params=params(16),
-        name="core_back",
-    )(field, weight, ghi, glo, counts)
-    lower = lax.ppermute(halo, segments, [(t, (t + 1) % tm) for t in range(tm)])
-
     chunks = struct((4, 4, 8, WIDE))
     core_struct = struct((NJ, 8, MEM))
-    own, other = pl.pallas_call(
+    own, other, local, halo, curve = pl.pallas_call(
         back_kernel,
-        out_shape=(chunks, chunks),
-        in_specs=[VM, VM],
-        out_specs=(VM, VM),
-        scratch_shapes=[pltpu.VMEM((2 * MEM, NS), BF16)],
-        compiler_params=params(12),
+        out_shape=(chunks, chunks, core_struct, struct((HALO, 128)), struct((MEM, SEG))),
+        in_specs=[VM] * 5 + [SM],
+        out_specs=(VM,) * 5,
+        scratch_shapes=[pltpu.VMEM((2 * MEM, NS), BF16), pltpu.VMEM((2 * MEM, NS), BF16)],
+        compiler_params=params(16),
         cost_estimate=product_cost,
         name="back",
-    )(pair, design)
+    )(field, weight, ghi, glo, design, counts)
+    lower = lax.ppermute(halo, segments, [(t, (t + 1) % tm) for t in range(tm)])
     got = lax.ppermute(other, "core", swap)
     known = pl.pallas_call(
         known_sums_kernel,
@@ -451,7 +473,7 @@
     pieces = lax.all_to_all(terms.reshape(16, 8, WIDE), "plane", 0, 0)
     sent = pl.pallas_call(
         image_kernel,
-        out_shape=struct((16, 8, SENT)),
+        out_shape=struct((16, 8, WIDE)),
         in_specs=[VM] * 6,
         out_specs=VM,
         scratch_shapes=[pltpu.VMEM((8, WIDE), F32), pltpu.VMEM((2, MEM, 128), F32)],
@@ -459,18 +481,18 @@
         name="image",
     )(pieces, curve, lith_direction, lith_residual, damp, known)
     whole = lax.all_to_all(sent, "plane", 0, 0)
-    rest = lax.ppermute(whole, "core", swap).reshape(4, 4, 8, SENT)
+    rest = lax.ppermute(whole, "core", swap).reshape(4, 4, 8, WIDE)
     sums = pl.pallas_call(
         plane_sum_kernel,
         grid=(1,),
         out_shape=struct((16, 8, 128)),
-        in_specs=[pl.BlockSpec((16, 8, 128), lambda i: (0, 0, WIDE // 128))],
+        in_specs=[pl.BlockSpec((16, 8, 128), lambda i: (0, 0, FULL // 128))],
         out_specs=pl.BlockSpec((16, 8, 128), lambda i: (0, 0, 0)),
         compiler_params=params(8),
         name="plane_sum",
     )(whole)
     sums = lax.all_to_all(sums, ("core", "coef"), 0, 0)
-    whole = whole.reshape(4, 4, 8, SENT)
+    whole = whole.reshape(4, 4, 8, WIDE)
 
     lith_struct = struct((MEM, NL))
     new_sol, new_res, new_dir, new_csol, new_cres, new_cdir = pl.pallas_call(
@@ -481,14 +503,14 @@
         scratch_shapes=[pltpu.VMEM((MEM, NL), F32)] * 3
         + [pltpu.VMEM((NJ, 8, MEM), F32)] * 3
         + [pltpu.VMEM((128, 128), F32)] * 2
-        + [pltpu.SemaphoreType.DMA((3,)), pltpu.SemaphoreType.DMA((4, 3))],
+        + [pltpu.SemaphoreType.DMA((3,)), pltpu.SemaphoreType.DMA((5, 3))],
         compiler_params=params(20),
         name="update",
     )(
         whole, rest, sums, lith_solution, lith_residual, lith_direction, cimage, csol, cres, cdir,
     )
-    back = lambda v: jnp.transpose(v, (2, 0, 1))
-    return new_sol, new_res, new_dir, back(new_csol), back(new_cres), back(new_cdir)
+    first = lambda v: jnp.transpose(v, (2, 0, 1))
+    return new_sol, new_res, new_dir, first(new_csol), first(new_cres), first(new_cdir)
 
 
 def solution(mesh):

time: 99.6 us -> 98.7 us (level)
    pallas_call x3 -> x2, Pallas kernels: 4.93 us -> 4.79 us  [the longest x1 4.52 us: shards(): pl.pallas_call(back_kernel, out_shape=(chunks, chunks, core_struct, struc...]
  transfers between devices with their start and end apart: 4 -> 4, of which waited for: 1 -> 1; matrix products, arithmetic and copies ran while one was open for 0% -> 0% of each run, Pallas kernels for 6% -> 7%
where the time goes in v4:
time: 98.7 us; the launch traced here: 98.4 us
  blocking collectives  67.1 us (68%)
  starting transfers between devices  15 us (15%)
  Pallas kernels  14.9 us (15%)
    all_to_all x1, blocking collectives, shards(): pieces = lax.all_to_all(terms.reshape(16, 8, WIDE), 'plane', 0, 0)  17.4 us
    all_to_all x1, blocking collectives, shards(): parts = lax.all_to_all(partial, 'coef', 0, 0)  15.6 us
    all_to_all x1, blocking collectives, shards(): whole = lax.all_to_all(sent, 'plane', 0, 0)  12.8 us
    all_to_all x1, blocking collectives, shards(): field = lax.all_to_all(total, 'coef', 0, 0)  11.7 us
    all_to_all x1, blocking collectives, shards(): sums = lax.all_to_all(sums, ('core', 'coef'), 0, 0)  9.61 us
    ppermute x1, starting transfers between devices, shards(): got = lax.ppermute(other, 'core', swap)  7.3 us
    pallas_call x1, Pallas kernels, shards(): pl.pallas_call(forward_kernel, out_shape=(struct((MEM, NS)), pltpu.VMEM((...  5.48 us
    pallas_call x1, Pallas kernels, shards(): pl.pallas_call(back_kernel, out_shape=(chunks, chunks, core_struct, struc...  4.52 us
  transfers between devices with their start and end apart: 4, of which 1 were waited for; matrix products, arithmetic and copies ran while one was open for 0% of the time, Pallas kernels for 7%

profile of v4, /device:TPU:1, one launch (start us, length us, event | category | flops | bytes accessed | tf_op | source)
XLA Modules:
  0.0 98.4 jit_solution(3488522399768847491)
XLA Ops:
  0.6 3.3 %collective-permute-start = (f32[55,8,64]{2,1,0:T(8,128)}, f32[55,8,64]{2,1,0:T(8,128)S(1)}, u32[]{:S(2)}, u32[]{:S(2)}) collective-permute-start(f32[55,8,64]{2,1,0:T(8,128)} %bitcast.13), channel_id=1, source_target_pairs={{0,248},{8,0},{16,8},{24,16},{32,24},{40,32},{48,40},{56,48},{64,5... | collective-permute-start | bytes 337928 | tf_op jit(solution)/shard_map/ppermute | solution.py:386
  4.0 5.5 %forward.1 = (f32[64,1024]{1,0:T(8,128)S(1)}, bf16[4352,1024]{1,0:T(8,128)(2,1)S(1)}, bf16[896,1024]{1,0:T(8,128)(2,1)S(1)}, bf16[896,1024]{1,0:T(8,128)(2,1)S(1)}) custom-call(f32[64,4352]{1,0:T(8,128)} %dir_ref.5, bf16[4352,1024]{1,0:T(8,128)(2,1)} %a_hbm.1, bf16[55,1024]{1,0:T(8,128)(2,1)} %design_hbm.1, f32[8,128]{1,0:T(8,128)} %bitcast.30, s32[8]{0:T(128)} %knot_hbm.1, ...), custom_call_target="tpu_custom_call" | custom-call | flops 4563402752 | bytes 12582912 | tf_op jit(solution)/shard_map/forward/pallas_call | solution.py:392
  9.4 0.0 collective-permute-done.halo_ref
  9.4 0.5 core_forward.1
  9.9 0.0 copy-start.8
  9.9 0.0 copy-start.9
  10.0 15.6 %all_to_all.25.parts_ref = f32[8,8,1024]{2,1,0:T(8,128)S(1)} all-to-all(f32[8,8,1024]{2,1,0:T(8,128)S(1)} %core_forward.1), channel_id=1, replica_groups=mesh['plane'=16,'core'=2,'coef'=8] {'coef'}, dimensions={0} | all-to-all | bytes 524288 | tf_op jit(solution)/shard_map/all_to_all | solution.py:430
  25.6 11.7 %all_to_all.26.field_ref = f32[8,8,1024]{2,1,0:T(8,128)S(1)} all-to-all(f32[8,8,1024]{2,1,0:T(8,128)S(1)} %field_sum.1), channel_id=1, replica_groups=mesh['plane'=16,'core'=2,'coef'=8] {'coef'}, dimensions={0} | all-to-all | bytes 524288 | tf_op jit(solution)/shard_map/all_to_all | solution.py:439
  37.3 0.0 copy-done.8
  37.3 0.0 copy-done.9
  37.3 0.0 copy-start
  37.3 0.0 copy-start.1
  37.3 0.0 copy-start.2
  37.3 0.0 copy-start.3
  37.4 0.0 copy-start.6
  37.4 0.0 copy-start.7
  37.4 4.5 %back.1 = (f32[4,4,8,1152]{3,2,1,0:T(8,128)S(1)}, f32[4,4,8,1152]{3,2,1,0:T(8,128)S(1)}, f32[55,8,64]{2,1,0:T(8,128)S(1)}, f32[144,128]{1,0:T(8,128)S(1)}, f32[64,128]{1,0:T(8,128)S(1)}) custom-call(f32[8,8,1024]{2,1,0:T(8,128)S(1)} %all_to_all.26.field_ref, f32[8,128]{1,0:T(8,128)S(1)} %bitcast.26, bf16[896,1024]{1,0:T(8,128)(2,1)S(1)} %get-tuple-element.25.ghi_ref, ...), custom_call_target="tpu_custom_call" | custom-call | flops 4563402752 | bytes 12582912 | tf_op jit(solution)/shard_map/back/pallas_call | solution.py:443
  41.9 7.3 %collective-permute-start.1 = (f32[4,4,8,1152]{3,2,1,0:T(8,128)S(1)}, f32[4,4,8,1152]{3,2,1,0:T(8,128)S(1)}, u32[]{:S(2)}, u32[]{:S(2)}) collective-permute-start(f32[4,4,8,1152]{3,2,1,0:T(8,128)S(1)} %get-tuple-element.29), channel_id=1, source_target_pairs={{0,8},{8,0},{1,9},{9,1},{2,10},{10,2},{3,11},{11,3},{4,12},{12,4},... | collective-permute-start | bytes 1769480 | tf_op jit(solution)/shard_map/ppermute | solution.py:454
  49.2 0.6 collective-permute-start.2
  49.8 0.0 copy-done
  49.8 0.0 copy-done.1
  49.8 0.0 copy-done.2
  49.8 0.0 copy-done.3
  49.8 0.0 copy-done.6
  49.8 0.0 copy-done.7
  49.8 0.9 known_sums.1.tile_ref
  50.7 0.5 collective-permute-done.2.halo_ref
  51.2 0.0 collective-permute-done.1.got_ref
  51.2 0.7 add_halves.1
  51.9 17.4 %all_to_all.27.parts_ref = f32[16,8,1152]{2,1,0:T(8,128)S(1)} all-to-all(f32[16,8,1152]{2,1,0:T(8,128)S(1)} %bitcast.21), channel_id=1, replica_groups=mesh['plane'=16,'core'=2,'coef'=8] {'plane'}, dimensions={0} | all-to-all | bytes 1179648 | tf_op jit(solution)/shard_map/all_to_all | solution.py:473
  69.3 0.3 image.1
  69.5 0.0 copy-start.4
  69.6 0.0 copy-start.5
  69.6 12.8 %all_to_all.28.whole_ref = f32[16,8,1152]{2,1,0:T(8,128)S(1)} all-to-all(f32[16,8,1152]{2,1,0:T(8,128)S(1)} %image.1), channel_id=1, replica_groups=mesh['plane'=16,'core'=2,'coef'=8] {'plane'}, dimensions={0} | all-to-all | bytes 1179648 | tf_op jit(solution)/shard_map/all_to_all | solution.py:483
  82.4 3.8 %collective-permute-start.3 = (f32[16,8,1152]{2,1,0:T(8,128)S(1)}, f32[16,8,1152]{2,1,0:T(8,128)S(1)}, u32[]{:S(2)}, u32[]{:S(2)}) collective-permute-start(f32[16,8,1152]{2,1,0:T(8,128)S(1)} %all_to_all.28.whole_ref), channel_id=1, source_target_pairs={{0,8},{8,0},{1,9},{9,1},{2,10},{10,2},{3,11},{11,3},{4,12},{12,4},... | collective-permute-start | bytes 1769480 | tf_op jit(solution)/shard_map/ppermute | solution.py:484
  86.2 0.1 plane_sum.1
  86.2 9.6 %all_to_all.29.sums_ref = f32[16,8,128]{2,1,0:T(8,128)S(1)} all-to-all(f32[16,8,128]{2,1,0:T(8,128)S(1)} %plane_sum.1), channel_id=1, replica_groups=mesh['plane'=16,'core'=2,'coef'=8] {'core','coef'}, dimensions={0} | all-to-all | bytes 131072 | tf_op jit(solution)/shard_map/all_to_all | solution.py:494
  95.8 0.0 collective-permute-done.3
  95.9 0.0 copy-done.4
  95.9 0.0 copy-done.5
  95.9 2.5 %update.1 = (f32[64,4352]{1,0:T(8,128)}, f32[64,4352]{1,0:T(8,128)}, f32[64,4352]{1,0:T(8,128)}, f32[55,8,64]{2,1,0:T(8,128)}, f32[55,8,64]{2,1,0:T(8,128)}, /*index=5*/f32[55,8,64]{2,1,0:T(8,128)}) custom-call(f32[4,4,8,1152]{3,2,1,0:T(8,128)S(1)} %bitcast.12, f32[4,4,8,1152]{3,2,1,0:T(8,128)S(1)} %bitcast.22, f32[16,8,128]{2,1,0:T(8,128)S(1)} %all_to_all.29.sums_ref, ...), custom_call_target="tpu_custom_call" | custom-call | tf_op jit(solution)/shard_map/update/pallas_call | solution.py:498
  (1 shorter events, 0.0 us)
Async XLA Ops:
  0.6 8.8 %collective-permute-start = (f32[55,8,64]{2,1,0:T(8,128)}, f32[55,8,64]{2,1,0:T(8,128)S(1)}, u32[]{:S(2)}, u32[]{:S(2)}) collective-permute-start(f32[55,8,64]{2,1,0:T(8,128)} %bitcast.13), channel_id=1, source_target_pairs={{0,248},{8,0},{16,8},{24,16},{32,24},{40,32},{48,40},{56,48},{64,5... | collective-permute-start | bytes 337928 | tf_op jit(solution)/shard_map/ppermute | solution.py:386
  9.9 27.4 %copy-start.8 = (f32[1024]{0:T(1024)S(1)}, f32[1024]{0:T(1024)}, u32[]{:S(2)}) copy-start(f32[1024]{0:T(1024)} %param.17) | copy-start | bytes 12292
  9.9 27.4 %copy-start.9 = (s32[8]{0:T(128)S(1)}, s32[8]{0:T(128)}, u32[]{:S(2)}) copy-start(s32[8]{0:T(128)} %count_ref.1) | copy-start | bytes 100
  37.3 12.5 %copy-start = (f32[64,4352]{1,0:T(8,128)S(1)}, f32[64,4352]{1,0:T(8,128)}, u32[]{:S(2)}) copy-start(f32[64,4352]{1,0:T(8,128)} %dir_ref.5) | copy-start | bytes 3342340
  37.3 12.5 %copy-start.1 = (f32[64,4352]{1,0:T(8,128)S(1)}, f32[64,4352]{1,0:T(8,128)}, u32[]{:S(2)}) copy-start(f32[64,4352]{1,0:T(8,128)} %res_ref.5) | copy-start | bytes 3342340
  37.3 12.5 %copy-start.2 = (f32[64,55,8]{0,2,1:T(8,128)S(1)}, f32[64,55,8]{0,2,1:T(8,128)}, u32[]{:S(2)}) copy-start(f32[64,55,8]{0,2,1:T(8,128)} %param.27) | copy-start | bytes 337924
  37.3 12.4 %copy-start.3 = (f32[64,55,8]{0,2,1:T(8,128)S(1)}, f32[64,55,8]{0,2,1:T(8,128)}, u32[]{:S(2)}) copy-start(f32[64,55,8]{0,2,1:T(8,128)} %param.26) | copy-start | bytes 337924
  37.4 12.4 %copy-start.6 = (f32[4352]{0:T(1024)S(1)}, f32[4352]{0:T(1024)}, u32[]{:S(2)}) copy-start(f32[4352]{0:T(1024)} %param.20) | copy-start | bytes 52228
  37.4 12.4 %copy-start.7 = (f32[55]{0:T(128)S(1)}, f32[55]{0:T(128)}, u32[]{:S(2)}) copy-start(f32[55]{0:T(128)} %cdamp_ref.3) | copy-start | bytes 664
  41.9 9.3 %collective-permute-start.1 = (f32[4,4,8,1152]{3,2,1,0:T(8,128)S(1)}, f32[4,4,8,1152]{3,2,1,0:T(8,128)S(1)}, u32[]{:S(2)}, u32[]{:S(2)}) collective-permute-start(f32[4,4,8,1152]{3,2,1,0:T(8,128)S(1)} %get-tuple-element.29), channel_id=1, source_target_pairs={{0,8},{8,0},{1,9},{9,1},{2,10},{10,2},{3,11},{11,3},{4,12},{12,4},... | collective-permute-start | bytes 1769480 | tf_op jit(solution)/shard_map/ppermute | solution.py:454
  49.2 2.0 %collective-permute-start.2 = (f32[144,128]{1,0:T(8,128)S(1)}, f32[144,128]{1,0:T(8,128)S(1)}, u32[]{:S(2)}, u32[]{:S(2)}) collective-permute-start(f32[144,128]{1,0:T(8,128)S(1)} %get-tuple-element.31), channel_id=1, source_target_pairs={{0,8},{8,16},{16,24},{24,32},{32,40},{40,48},{48,56},{56,64},{64,7... | collective-permute-start | bytes 221192 | tf_op jit(solution)/shard_map/ppermute | solution.py:453
  69.5 26.3 %copy-start.4 = (f32[64,4352]{1,0:T(8,128)S(1)}, f32[64,4352]{1,0:T(8,128)}, u32[]{:S(2)}) copy-start(f32[64,4352]{1,0:T(8,128)} %sol_ref.1) | copy-start | bytes 3342340
  69.6 26.3 %copy-start.5 = (f32[64,55,8]{0,2,1:T(8,128)S(1)}, f32[64,55,8]{0,2,1:T(8,128)}, u32[]{:S(2)}) copy-start(f32[64,55,8]{0,2,1:T(8,128)} %param.25) | copy-start | bytes 337924
  82.4 13.5 %collective-permute-start.3 = (f32[16,8,1152]{2,1,0:T(8,128)S(1)}, f32[16,8,1152]{2,1,0:T(8,128)S(1)}, u32[]{:S(2)}, u32[]{:S(2)}) collective-permute-start(f32[16,8,1152]{2,1,0:T(8,128)S(1)} %all_to_all.28.whole_ref), channel_id=1, source_target_pairs={{0,8},{8,0},{1,9},{9,1},{2,10},{10,2},{3,11},{11,3},{4,12},{12,4},... | collective-permute-start | bytes 1769480 | tf_op jit(solution)/shard_map/ppermute | solution.py:484

commit v5 on v4

--- a/solution.py
+++ b/solution.py
@@ -56,14 +56,14 @@
 
 
 def forward_kernel(
-    dir_hbm, a_hbm, design_hbm, phase_hbm, knot_hbm, cdir_hbm, out_ref, a_buf, ghi_ref, glo_ref,
-    dir_buf, lhs, acc, design_buf, phase_buf, knot_buf, ext, basis, design, small_sems, sems,
+    dir_hbm, a_hbm, design_ref, phase_hbm, knot_hbm, cdir_hbm, out_ref, a_buf, ghi_ref, glo_ref,
+    dir_buf, lhs, acc, phase_buf, knot_buf, ext, basis, design, small_sems, sems,
 ):
     small = [
         pltpu.make_async_copy(src, dst, small_sems.at[k])
         for k, (src, dst) in enumerate(
             (
-                (phase_hbm, phase_buf), (knot_hbm, knot_buf), (design_hbm, design_buf),
+                (phase_hbm, phase_buf), (knot_hbm, knot_buf),
                 (cdir_hbm, ext.at[0:NJ]), (dir_hbm, dir_buf),
             )
         )
@@ -76,7 +76,7 @@
         copy = pltpu.make_async_copy(a_hbm.at[rows], a_buf.at[rows], sems.at[b])
         copy.start()
         copies.append(copy)
-    for copy in small[0:4]:
+    for copy in small[0:3]:
         copy.wait()
     values = spline_values(phase_buf[...])
     row = lax.broadcasted_iota(jnp.int32, (16, SEG), 0)
@@ -86,7 +86,7 @@
         for k in range(6):
             block = block + jnp.where(row == first + k, values[k][g : g + 1, :], 0.0)
         basis[:, g * SEG : (g + 1) * SEG] = block
-    design[0:NJ] = design_buf[...].astype(F32)
+    design[0:NJ] = design_ref[...].astype(F32)
     design[NJ:JP] = jnp.zeros((1, NS), F32)
 
     def build(j, carry):
@@ -104,7 +104,7 @@
     lax.fori_loop(0, JP // 2, build, 0)
     ext[NJ:JP] = jnp.zeros((1, 8, MEM), F32)
     out_ref[...] = core_product(ext, ghi_ref, glo_ref, 0)
-    small[4].wait()
+    small[3].wait()
     for b, copy in enumerate(copies):
         lo, hi = FORWARD_CUTS[b], FORWARD_CUTS[b + 1]
         high, low = split(dir_buf[:, lo:hi])
@@ -397,25 +397,24 @@
             struct((JP * 16, NS), BF16),
             struct((JP * 16, NS), BF16),
         ),
-        in_specs=[HB] * 6,
+        in_specs=[HB, HB, VM, HB, HB, HB],
         out_specs=(VM,) * 4,
         scratch_shapes=[
             pltpu.VMEM((MEM, NL), F32),
             pltpu.VMEM((2 * MEM, NL), BF16),
             pltpu.VMEM((2 * MEM, NS), F32),
-            pltpu.VMEM((NJ, NS), BF16),
             pltpu.VMEM((8, SEG), F32),
             pltpu.SMEM((8,), jnp.int32),
             pltpu.VMEM((JP, 8, MEM), F32),
             pltpu.VMEM((16, NS), F32),
             pltpu.VMEM((JP, NS), F32),
-            pltpu.SemaphoreType.DMA((5,)),
+            pltpu.SemaphoreType.DMA((4,)),
             pltpu.SemaphoreType.DMA((len(FORWARD_CUTS) - 1,)),
         ],
         compiler_params=params(24),
         cost_estimate=product_cost,
         name="forward",
-    )(pin(lith_direction), pin(design_lith), pin(design_core), pin(phase), pin(knot_index), pin(cdir))
+    )(pin(lith_direction), pin(design_lith), design_core, pin(phase), pin(knot_index), pin(cdir))
 
     partial = pl.pallas_call(
         core_forward_kernel,

time: 98.7 us -> 99.6 us (level)
  transfers between devices with their start and end apart: 4 -> 4, of which waited for: 1 -> 1; matrix products, arithmetic and copies ran while one was open for 0% -> 0% of each run, Pallas kernels for 7% -> 6%
where the time goes in v5:
time: 99.6 us; the launch traced here: 99.3 us
  blocking collectives  67.1 us (67%)
  starting transfers between devices  15 us (15%)
  Pallas kernels  14.9 us (15%)
    all_to_all x1, blocking collectives, shards(): pieces = lax.all_to_all(terms.reshape(16, 8, WIDE), 'plane', 0, 0)  17.4 us
    all_to_all x1, blocking collectives, shards(): parts = lax.all_to_all(partial, 'coef', 0, 0)  15.6 us
    all_to_all x1, blocking collectives, shards(): whole = lax.all_to_all(sent, 'plane', 0, 0)  12.8 us
    all_to_all x1, blocking collectives, shards(): field = lax.all_to_all(total, 'coef', 0, 0)  11.7 us
    all_to_all x1, blocking collectives, shards(): sums = lax.all_to_all(sums, ('core', 'coef'), 0, 0)  9.61 us
    ppermute x1, starting transfers between devices, shards(): got = lax.ppermute(other, 'core', swap)  7.3 us
    pallas_call x1, Pallas kernels, shards(): pl.pallas_call(forward_kernel, out_shape=(struct((MEM, NS)), pltpu.VMEM((...  5.43 us
    pallas_call x1, Pallas kernels, shards(): pl.pallas_call(back_kernel, out_shape=(chunks, chunks, core_struct, struc...  4.51 us
  transfers between devices with their start and end apart: 4, of which 1 were waited for; matrix products, arithmetic and copies ran while one was open for 0% of the time, Pallas kernels for 6%

profile of v5, /device:TPU:1, one launch (start us, length us, event | category | flops | bytes accessed | tf_op | source)
XLA Modules:
  0.0 99.3 jit_solution(11070286076606625035)
XLA Ops:
  0.6 3.3 %collective-permute-start = (f32[55,8,64]{2,1,0:T(8,128)}, f32[55,8,64]{2,1,0:T(8,128)S(1)}, u32[]{:S(2)}, u32[]{:S(2)}) collective-permute-start(f32[55,8,64]{2,1,0:T(8,128)} %bitcast.13), channel_id=1, source_target_pairs={{0,248},{8,0},{16,8},{24,16},{32,24},{40,32},{48,40},{56,48},{64,5... | collective-permute-start | bytes 337928 | tf_op jit(solution)/shard_map/ppermute | solution.py:386
  4.0 0.0 copy-start.8
  4.0 0.9 copy-done.8
  4.8 5.4 %forward.1 = (f32[64,1024]{1,0:T(8,128)S(1)}, bf16[4352,1024]{1,0:T(8,128)(2,1)S(1)}, bf16[896,1024]{1,0:T(8,128)(2,1)S(1)}, bf16[896,1024]{1,0:T(8,128)(2,1)S(1)}) custom-call(f32[64,4352]{1,0:T(8,128)} %dir_ref.5, bf16[4352,1024]{1,0:T(8,128)(2,1)} %a_hbm.1, bf16[55,1024]{1,0:T(8,128)(2,1)S(1)} %copy-done.8, f32[8,128]{1,0:T(8,128)} %bitcast.30, ...), custom_call_target="tpu_custom_call" | custom-call | flops 4563402752 | bytes 12582912 | tf_op jit(solution)/shard_map/forward/pallas_call | solution.py:392
  10.3 0.0 collective-permute-done.halo_ref
  10.3 0.5 core_forward.1
  10.8 0.0 copy-start.9
  10.8 0.0 copy-start.10
  10.8 15.6 %all_to_all.25.parts_ref = f32[8,8,1024]{2,1,0:T(8,128)S(1)} all-to-all(f32[8,8,1024]{2,1,0:T(8,128)S(1)} %core_forward.1), channel_id=1, replica_groups=mesh['plane'=16,'core'=2,'coef'=8] {'coef'}, dimensions={0} | all-to-all | bytes 524288 | tf_op jit(solution)/shard_map/all_to_all | solution.py:429
  26.4 11.7 %all_to_all.26.field_ref = f32[8,8,1024]{2,1,0:T(8,128)S(1)} all-to-all(f32[8,8,1024]{2,1,0:T(8,128)S(1)} %field_sum.1), channel_id=1, replica_groups=mesh['plane'=16,'core'=2,'coef'=8] {'coef'}, dimensions={0} | all-to-all | bytes 524288 | tf_op jit(solution)/shard_map/all_to_all | solution.py:438
  38.2 0.0 copy-done.9
  38.2 0.0 copy-done.10
  38.2 0.0 copy-start
  38.2 0.0 copy-start.1
  38.2 0.0 copy-start.2
  38.2 0.0 copy-start.3
  38.2 0.0 copy-start.6
  38.2 0.0 copy-start.7
  38.2 4.5 %back.1 = (f32[4,4,8,1152]{3,2,1,0:T(8,128)S(1)}, f32[4,4,8,1152]{3,2,1,0:T(8,128)S(1)}, f32[55,8,64]{2,1,0:T(8,128)S(1)}, f32[144,128]{1,0:T(8,128)S(1)}, f32[64,128]{1,0:T(8,128)S(1)}) custom-call(f32[8,8,1024]{2,1,0:T(8,128)S(1)} %all_to_all.26.field_ref, f32[8,128]{1,0:T(8,128)S(1)} %bitcast.26, bf16[896,1024]{1,0:T(8,128)(2,1)S(1)} %get-tuple-element.25.ghi_ref, ...), custom_call_target="tpu_custom_call" | custom-call | flops 4563402752 | bytes 12582912 | tf_op jit(solution)/shard_map/back/pallas_call | solution.py:442
  42.8 7.3 %collective-permute-start.1 = (f32[4,4,8,1152]{3,2,1,0:T(8,128)S(1)}, f32[4,4,8,1152]{3,2,1,0:T(8,128)S(1)}, u32[]{:S(2)}, u32[]{:S(2)}) collective-permute-start(f32[4,4,8,1152]{3,2,1,0:T(8,128)S(1)} %get-tuple-element.29), channel_id=1, source_target_pairs={{0,8},{8,0},{1,9},{9,1},{2,10},{10,2},{3,11},{11,3},{4,12},{12,4},... | collective-permute-start | bytes 1769480 | tf_op jit(solution)/shard_map/ppermute | solution.py:453
  50.1 0.6 collective-permute-start.2
  50.7 0.0 copy-done
  50.7 0.0 copy-done.1
  50.7 0.0 copy-done.2
  50.7 0.0 copy-done.3
  50.7 0.0 copy-done.6
  50.7 0.0 copy-done.7
  50.7 0.9 known_sums.1.tile_ref
  51.5 0.5 collective-permute-done.2.halo_ref
  52.1 0.0 collective-permute-done.1.got_ref
  52.1 0.7 add_halves.1
  52.8 17.4 %all_to_all.27.parts_ref = f32[16,8,1152]{2,1,0:T(8,128)S(1)} all-to-all(f32[16,8,1152]{2,1,0:T(8,128)S(1)} %bitcast.21), channel_id=1, replica_groups=mesh['plane'=16,'core'=2,'coef'=8] {'plane'}, dimensions={0} | all-to-all | bytes 1179648 | tf_op jit(solution)/shard_map/all_to_all | solution.py:472
  70.2 0.3 image.1
  70.5 0.0 copy-start.4
  70.5 0.0 copy-start.5
  70.5 12.8 %all_to_all.28.whole_ref = f32[16,8,1152]{2,1,0:T(8,128)S(1)} all-to-all(f32[16,8,1152]{2,1,0:T(8,128)S(1)} %image.1), channel_id=1, replica_groups=mesh['plane'=16,'core'=2,'coef'=8] {'plane'}, dimensions={0} | all-to-all | bytes 1179648 | tf_op jit(solution)/shard_map/all_to_all | solution.py:482
  83.3 3.8 %collective-permute-start.3 = (f32[16,8,1152]{2,1,0:T(8,128)S(1)}, f32[16,8,1152]{2,1,0:T(8,128)S(1)}, u32[]{:S(2)}, u32[]{:S(2)}) collective-permute-start(f32[16,8,1152]{2,1,0:T(8,128)S(1)} %all_to_all.28.whole_ref), channel_id=1, source_target_pairs={{0,8},{8,0},{1,9},{9,1},{2,10},{10,2},{3,11},{11,3},{4,12},{12,4},... | collective-permute-start | bytes 1769480 | tf_op jit(solution)/shard_map/ppermute | solution.py:483
  87.1 0.1 plane_sum.1
  87.1 9.6 %all_to_all.29.sums_ref = f32[16,8,128]{2,1,0:T(8,128)S(1)} all-to-all(f32[16,8,128]{2,1,0:T(8,128)S(1)} %plane_sum.1), channel_id=1, replica_groups=mesh['plane'=16,'core'=2,'coef'=8] {'core','coef'}, dimensions={0} | all-to-all | bytes 131072 | tf_op jit(solution)/shard_map/all_to_all | solution.py:493
  96.8 0.0 collective-permute-done.3
  96.8 0.0 copy-done.4
  96.8 0.0 copy-done.5
  96.8 2.5 %update.1 = (f32[64,4352]{1,0:T(8,128)}, f32[64,4352]{1,0:T(8,128)}, f32[64,4352]{1,0:T(8,128)}, f32[55,8,64]{2,1,0:T(8,128)}, f32[55,8,64]{2,1,0:T(8,128)}, /*index=5*/f32[55,8,64]{2,1,0:T(8,128)}) custom-call(f32[4,4,8,1152]{3,2,1,0:T(8,128)S(1)} %bitcast.12, f32[4,4,8,1152]{3,2,1,0:T(8,128)S(1)} %bitcast.22, f32[16,8,128]{2,1,0:T(8,128)S(1)} %all_to_all.29.sums_ref, ...), custom_call_target="tpu_custom_call" | custom-call | tf_op jit(solution)/shard_map/update/pallas_call | solution.py:497
  (1 shorter events, 0.0 us)
Async XLA Ops:
  0.6 9.7 %collective-permute-start = (f32[55,8,64]{2,1,0:T(8,128)}, f32[55,8,64]{2,1,0:T(8,128)S(1)}, u32[]{:S(2)}, u32[]{:S(2)}) collective-permute-start(f32[55,8,64]{2,1,0:T(8,128)} %bitcast.13), channel_id=1, source_target_pairs={{0,248},{8,0},{16,8},{24,16},{32,24},{40,32},{48,40},{56,48},{64,5... | collective-permute-start | bytes 337928 | tf_op jit(solution)/shard_map/ppermute | solution.py:386
  4.0 0.9 copy-start.8
  10.8 27.4 %copy-start.9 = (f32[1024]{0:T(1024)S(1)}, f32[1024]{0:T(1024)}, u32[]{:S(2)}) copy-start(f32[1024]{0:T(1024)} %param.17) | copy-start | bytes 12292
  10.8 27.4 %copy-start.10 = (s32[8]{0:T(128)S(1)}, s32[8]{0:T(128)}, u32[]{:S(2)}) copy-start(s32[8]{0:T(128)} %count_ref.1) | copy-start | bytes 100
  38.2 12.5 %copy-start = (f32[64,4352]{1,0:T(8,128)S(1)}, f32[64,4352]{1,0:T(8,128)}, u32[]{:S(2)}) copy-start(f32[64,4352]{1,0:T(8,128)} %dir_ref.5) | copy-start | bytes 3342340
  38.2 12.5 %copy-start.1 = (f32[64,4352]{1,0:T(8,128)S(1)}, f32[64,4352]{1,0:T(8,128)}, u32[]{:S(2)}) copy-start(f32[64,4352]{1,0:T(8,128)} %res_ref.5) | copy-start | bytes 3342340
  38.2 12.5 %copy-start.2 = (f32[64,55,8]{0,2,1:T(8,128)S(1)}, f32[64,55,8]{0,2,1:T(8,128)}, u32[]{:S(2)}) copy-start(f32[64,55,8]{0,2,1:T(8,128)} %param.27) | copy-start | bytes 337924
  38.2 12.5 %copy-start.3 = (f32[64,55,8]{0,2,1:T(8,128)S(1)}, f32[64,55,8]{0,2,1:T(8,128)}, u32[]{:S(2)}) copy-start(f32[64,55,8]{0,2,1:T(8,128)} %param.26) | copy-start | bytes 337924
  38.2 12.5 %copy-start.6 = (f32[4352]{0:T(1024)S(1)}, f32[4352]{0:T(1024)}, u32[]{:S(2)}) copy-start(f32[4352]{0:T(1024)} %param.20) | copy-start | bytes 52228
  38.2 12.5 %copy-start.7 = (f32[55]{0:T(128)S(1)}, f32[55]{0:T(128)}, u32[]{:S(2)}) copy-start(f32[55]{0:T(128)} %cdamp_ref.3) | copy-start | bytes 664
  42.8 9.3 %collective-permute-start.1 = (f32[4,4,8,1152]{3,2,1,0:T(8,128)S(1)}, f32[4,4,8,1152]{3,2,1,0:T(8,128)S(1)}, u32[]{:S(2)}, u32[]{:S(2)}) collective-permute-start(f32[4,4,8,1152]{3,2,1,0:T(8,128)S(1)} %get-tuple-element.29), channel_id=1, source_target_pairs={{0,8},{8,0},{1,9},{9,1},{2,10},{10,2},{3,11},{11,3},{4,12},{12,4},... | collective-permute-start | bytes 1769480 | tf_op jit(solution)/shard_map/ppermute | solution.py:453
  50.1 2.0 %collective-permute-start.2 = (f32[144,128]{1,0:T(8,128)S(1)}, f32[144,128]{1,0:T(8,128)S(1)}, u32[]{:S(2)}, u32[]{:S(2)}) collective-permute-start(f32[144,128]{1,0:T(8,128)S(1)} %get-tuple-element.31), channel_id=1, source_target_pairs={{0,8},{8,16},{16,24},{24,32},{32,40},{40,48},{48,56},{56,64},{64,7... | collective-permute-start | bytes 221192 | tf_op jit(solution)/shard_map/ppermute | solution.py:452
  70.5 26.3 %copy-start.4 = (f32[64,4352]{1,0:T(8,128)S(1)}, f32[64,4352]{1,0:T(8,128)}, u32[]{:S(2)}) copy-start(f32[64,4352]{1,0:T(8,128)} %sol_ref.1) | copy-start | bytes 3342340
  70.5 26.3 %copy-start.5 = (f32[64,55,8]{0,2,1:T(8,128)S(1)}, f32[64,55,8]{0,2,1:T(8,128)}, u32[]{:S(2)}) copy-start(f32[64,55,8]{0,2,1:T(8,128)} %param.25) | copy-start | bytes 337924
  83.3 13.5 %collective-permute-start.3 = (f32[16,8,1152]{2,1,0:T(8,128)S(1)}, f32[16,8,1152]{2,1,0:T(8,128)S(1)}, u32[]{:S(2)}, u32[]{:S(2)}) collective-permute-start(f32[16,8,1152]{2,1,0:T(8,128)S(1)} %all_to_all.28.whole_ref), channel_id=1, source_target_pairs={{0,8},{8,0},{1,9},{9,1},{2,10},{10,2},{3,11},{11,3},{4,12},{12,4},... | collective-permute-start | bytes 1769480 | tf_op jit(solution)/shard_map/ppermute | solution.py:483

commit v6 on v5

--- a/solution.py
+++ b/solution.py
@@ -14,7 +14,7 @@
 VM = pl.BlockSpec(memory_space=pltpu.VMEM)
 SM = pl.BlockSpec(memory_space=pltpu.SMEM)
 HB = pl.BlockSpec(memory_space=pltpu.HBM)
-FORWARD_CUTS = (0, 512, 1280, 2304, 3328, 4352)
+FORWARD_CUTS = (0, 768, 1792, 2816, 3840, 4352)
 TRANS_B = (((1,), (1,)), ((), ()))
 
 

time: 99.6 us -> 99.6 us (level)
  transfers between devices with their start and end apart: 4 -> 4, of which waited for: 1 -> 1; matrix products, arithmetic and copies ran while one was open for 0% -> 0% of each run, Pallas kernels for 6% -> 7%
where the time goes in v6:
time: 99.6 us; the launch traced here: 99.3 us
  blocking collectives  66.9 us (67%)
  Pallas kernels  15.2 us (15%)
  starting transfers between devices  15 us (15%)
    all_to_all x1, blocking collectives, shards(): pieces = lax.all_to_all(terms.reshape(16, 8, WIDE), 'plane', 0, 0)  17.1 us
    all_to_all x1, blocking collectives, shards(): parts = lax.all_to_all(partial, 'coef', 0, 0)  15.6 us
    all_to_all x1, blocking collectives, shards(): whole = lax.all_to_all(sent, 'plane', 0, 0)  12.8 us
    all_to_all x1, blocking collectives, shards(): field = lax.all_to_all(total, 'coef', 0, 0)  11.7 us
    all_to_all x1, blocking collectives, shards(): sums = lax.all_to_all(sums, ('core', 'coef'), 0, 0)  9.61 us
    ppermute x1, starting transfers between devices, shards(): got = lax.ppermute(other, 'core', swap)  7.29 us
    pallas_call x1, Pallas kernels, shards(): pl.pallas_call(forward_kernel, out_shape=(struct((MEM, NS)), pltpu.VMEM((...  5.74 us
    pallas_call x1, Pallas kernels, shards(): pl.pallas_call(back_kernel, out_shape=(chunks, chunks, core_struct, struc...  4.52 us
  transfers between devices with their start and end apart: 4, of which 1 were waited for; matrix products, arithmetic and copies ran while one was open for 0% of the time, Pallas kernels for 7%

profile of v6, /device:TPU:1, one launch (start us, length us, event | category | flops | bytes accessed | tf_op | source)
XLA Modules:
  0.0 99.3 jit_solution(11248257837864170441)
XLA Ops:
  0.6 3.3 %collective-permute-start = (f32[55,8,64]{2,1,0:T(8,128)}, f32[55,8,64]{2,1,0:T(8,128)S(1)}, u32[]{:S(2)}, u32[]{:S(2)}) collective-permute-start(f32[55,8,64]{2,1,0:T(8,128)} %bitcast.13), channel_id=1, source_target_pairs={{0,248},{8,0},{16,8},{24,16},{32,24},{40,32},{48,40},{56,48},{64,5... | collective-permute-start | bytes 337928 | tf_op jit(solution)/shard_map/ppermute | solution.py:386
  4.0 0.0 copy-start.8
  4.0 0.9 copy-done.8
  4.8 5.7 %forward.1 = (f32[64,1024]{1,0:T(8,128)S(1)}, bf16[4352,1024]{1,0:T(8,128)(2,1)S(1)}, bf16[896,1024]{1,0:T(8,128)(2,1)S(1)}, bf16[896,1024]{1,0:T(8,128)(2,1)S(1)}) custom-call(f32[64,4352]{1,0:T(8,128)} %dir_ref.5, bf16[4352,1024]{1,0:T(8,128)(2,1)} %a_hbm.1, bf16[55,1024]{1,0:T(8,128)(2,1)S(1)} %copy-done.8, f32[8,128]{1,0:T(8,128)} %bitcast.30, ...), custom_call_target="tpu_custom_call" | custom-call | flops 4563402752 | bytes 12582912 | tf_op jit(solution)/shard_map/forward/pallas_call | solution.py:392
  10.6 0.0 collective-permute-done.halo_ref
  10.6 0.5 core_forward.1
  11.1 0.0 copy-start.9
  11.1 0.0 copy-start.10
  11.1 15.6 %all_to_all.25.parts_ref = f32[8,8,1024]{2,1,0:T(8,128)S(1)} all-to-all(f32[8,8,1024]{2,1,0:T(8,128)S(1)} %core_forward.1), channel_id=1, replica_groups=mesh['plane'=16,'core'=2,'coef'=8] {'coef'}, dimensions={0} | all-to-all | bytes 524288 | tf_op jit(solution)/shard_map/all_to_all | solution.py:429
  26.8 11.7 %all_to_all.26.field_ref = f32[8,8,1024]{2,1,0:T(8,128)S(1)} all-to-all(f32[8,8,1024]{2,1,0:T(8,128)S(1)} %field_sum.1), channel_id=1, replica_groups=mesh['plane'=16,'core'=2,'coef'=8] {'coef'}, dimensions={0} | all-to-all | bytes 524288 | tf_op jit(solution)/shard_map/all_to_all | solution.py:438
  38.5 0.0 copy-done.9
  38.5 0.0 copy-done.10
  38.5 0.0 copy-start
  38.5 0.0 copy-start.1
  38.5 0.0 copy-start.2
  38.5 0.0 copy-start.3
  38.5 0.0 copy-start.6
  38.5 0.0 copy-start.7
  38.6 4.5 %back.1 = (f32[4,4,8,1152]{3,2,1,0:T(8,128)S(1)}, f32[4,4,8,1152]{3,2,1,0:T(8,128)S(1)}, f32[55,8,64]{2,1,0:T(8,128)S(1)}, f32[144,128]{1,0:T(8,128)S(1)}, f32[64,128]{1,0:T(8,128)S(1)}) custom-call(f32[8,8,1024]{2,1,0:T(8,128)S(1)} %all_to_all.26.field_ref, f32[8,128]{1,0:T(8,128)S(1)} %bitcast.26, bf16[896,1024]{1,0:T(8,128)(2,1)S(1)} %get-tuple-element.25.ghi_ref, ...), custom_call_target="tpu_custom_call" | custom-call | flops 4563402752 | bytes 12582912 | tf_op jit(solution)/shard_map/back/pallas_call | solution.py:442
  43.1 7.3 %collective-permute-start.1 = (f32[4,4,8,1152]{3,2,1,0:T(8,128)S(1)}, f32[4,4,8,1152]{3,2,1,0:T(8,128)S(1)}, u32[]{:S(2)}, u32[]{:S(2)}) collective-permute-start(f32[4,4,8,1152]{3,2,1,0:T(8,128)S(1)} %get-tuple-element.29), channel_id=1, source_target_pairs={{0,8},{8,0},{1,9},{9,1},{2,10},{10,2},{3,11},{11,3},{4,12},{12,4},... | collective-permute-start | bytes 1769480 | tf_op jit(solution)/shard_map/ppermute | solution.py:453
  50.4 0.6 collective-permute-start.2
  51.0 0.0 copy-done
  51.0 0.0 copy-done.1
  51.0 0.0 copy-done.2
  51.0 0.0 copy-done.3
  51.0 0.0 copy-done.6
  51.0 0.0 copy-done.7
  51.0 0.9 known_sums.1.tile_ref
  51.9 0.5 collective-permute-done.2.halo_ref
  52.4 0.0 collective-permute-done.1.got_ref
  52.4 0.7 add_halves.1
  53.1 17.1 %all_to_all.27.parts_ref = f32[16,8,1152]{2,1,0:T(8,128)S(1)} all-to-all(f32[16,8,1152]{2,1,0:T(8,128)S(1)} %bitcast.21), channel_id=1, replica_groups=mesh['plane'=16,'core'=2,'coef'=8] {'plane'}, dimensions={0} | all-to-all | bytes 1179648 | tf_op jit(solution)/shard_map/all_to_all | solution.py:472
  70.2 0.3 image.1
  70.5 0.0 copy-start.4
  70.5 0.0 copy-start.5
  70.5 12.8 %all_to_all.28.whole_ref = f32[16,8,1152]{2,1,0:T(8,128)S(1)} all-to-all(f32[16,8,1152]{2,1,0:T(8,128)S(1)} %image.1), channel_id=1, replica_groups=mesh['plane'=16,'core'=2,'coef'=8] {'plane'}, dimensions={0} | all-to-all | bytes 1179648 | tf_op jit(solution)/shard_map/all_to_all | solution.py:482
  83.3 3.8 %collective-permute-start.3 = (f32[16,8,1152]{2,1,0:T(8,128)S(1)}, f32[16,8,1152]{2,1,0:T(8,128)S(1)}, u32[]{:S(2)}, u32[]{:S(2)}) collective-permute-start(f32[16,8,1152]{2,1,0:T(8,128)S(1)} %all_to_all.28.whole_ref), channel_id=1, source_target_pairs={{0,8},{8,0},{1,9},{9,1},{2,10},{10,2},{3,11},{11,3},{4,12},{12,4},... | collective-permute-start | bytes 1769480 | tf_op jit(solution)/shard_map/ppermute | solution.py:483
  87.1 0.1 plane_sum.1
  87.2 9.6 %all_to_all.29.sums_ref = f32[16,8,128]{2,1,0:T(8,128)S(1)} all-to-all(f32[16,8,128]{2,1,0:T(8,128)S(1)} %plane_sum.1), channel_id=1, replica_groups=mesh['plane'=16,'core'=2,'coef'=8] {'core','coef'}, dimensions={0} | all-to-all | bytes 131072 | tf_op jit(solution)/shard_map/all_to_all | solution.py:493
  96.8 0.0 collective-permute-done.3
  96.8 0.0 copy-done.4
  96.8 0.0 copy-done.5
  96.8 2.5 %update.1 = (f32[64,4352]{1,0:T(8,128)}, f32[64,4352]{1,0:T(8,128)}, f32[64,4352]{1,0:T(8,128)}, f32[55,8,64]{2,1,0:T(8,128)}, f32[55,8,64]{2,1,0:T(8,128)}, /*index=5*/f32[55,8,64]{2,1,0:T(8,128)}) custom-call(f32[4,4,8,1152]{3,2,1,0:T(8,128)S(1)} %bitcast.12, f32[4,4,8,1152]{3,2,1,0:T(8,128)S(1)} %bitcast.22, f32[16,8,128]{2,1,0:T(8,128)S(1)} %all_to_all.29.sums_ref, ...), custom_call_target="tpu_custom_call" | custom-call | tf_op jit(solution)/shard_map/update/pallas_call | solution.py:497
  (1 shorter events, 0.0 us)
Async XLA Ops:
  0.6 10.0 %collective-permute-start = (f32[55,8,64]{2,1,0:T(8,128)}, f32[55,8,64]{2,1,0:T(8,128)S(1)}, u32[]{:S(2)}, u32[]{:S(2)}) collective-permute-start(f32[55,8,64]{2,1,0:T(8,128)} %bitcast.13), channel_id=1, source_target_pairs={{0,248},{8,0},{16,8},{24,16},{32,24},{40,32},{48,40},{56,48},{64,5... | collective-permute-start | bytes 337928 | tf_op jit(solution)/shard_map/ppermute | solution.py:386
  4.0 0.9 copy-start.8
  11.1 27.4 %copy-start.9 = (f32[1024]{0:T(1024)S(1)}, f32[1024]{0:T(1024)}, u32[]{:S(2)}) copy-start(f32[1024]{0:T(1024)} %param.17) | copy-start | bytes 12292
  11.1 27.4 %copy-start.10 = (s32[8]{0:T(128)S(1)}, s32[8]{0:T(128)}, u32[]{:S(2)}) copy-start(s32[8]{0:T(128)} %count_ref.1) | copy-start | bytes 100
  38.5 12.5 %copy-start = (f32[64,4352]{1,0:T(8,128)S(1)}, f32[64,4352]{1,0:T(8,128)}, u32[]{:S(2)}) copy-start(f32[64,4352]{1,0:T(8,128)} %dir_ref.5) | copy-start | bytes 3342340
  38.5 12.5 %copy-start.1 = (f32[64,4352]{1,0:T(8,128)S(1)}, f32[64,4352]{1,0:T(8,128)}, u32[]{:S(2)}) copy-start(f32[64,4352]{1,0:T(8,128)} %res_ref.5) | copy-start | bytes 3342340
  38.5 12.5 %copy-start.2 = (f32[64,55,8]{0,2,1:T(8,128)S(1)}, f32[64,55,8]{0,2,1:T(8,128)}, u32[]{:S(2)}) copy-start(f32[64,55,8]{0,2,1:T(8,128)} %param.27) | copy-start | bytes 337924
  38.5 12.4 %copy-start.3 = (f32[64,55,8]{0,2,1:T(8,128)S(1)}, f32[64,55,8]{0,2,1:T(8,128)}, u32[]{:S(2)}) copy-start(f32[64,55,8]{0,2,1:T(8,128)} %param.26) | copy-start | bytes 337924
  38.5 12.4 %copy-start.6 = (f32[4352]{0:T(1024)S(1)}, f32[4352]{0:T(1024)}, u32[]{:S(2)}) copy-start(f32[4352]{0:T(1024)} %param.20) | copy-start | bytes 52228
  38.5 12.4 %copy-start.7 = (f32[55]{0:T(128)S(1)}, f32[55]{0:T(128)}, u32[]{:S(2)}) copy-start(f32[55]{0:T(128)} %cdamp_ref.3) | copy-start | bytes 664
  43.1 9.3 %collective-permute-start.1 = (f32[4,4,8,1152]{3,2,1,0:T(8,128)S(1)}, f32[4,4,8,1152]{3,2,1,0:T(8,128)S(1)}, u32[]{:S(2)}, u32[]{:S(2)}) collective-permute-start(f32[4,4,8,1152]{3,2,1,0:T(8,128)S(1)} %get-tuple-element.29), channel_id=1, source_target_pairs={{0,8},{8,0},{1,9},{9,1},{2,10},{10,2},{3,11},{11,3},{4,12},{12,4},... | collective-permute-start | bytes 1769480 | tf_op jit(solution)/shard_map/ppermute | solution.py:453
  50.4 2.0 %collective-permute-start.2 = (f32[144,128]{1,0:T(8,128)S(1)}, f32[144,128]{1,0:T(8,128)S(1)}, u32[]{:S(2)}, u32[]{:S(2)}) collective-permute-start(f32[144,128]{1,0:T(8,128)S(1)} %get-tuple-element.31), channel_id=1, source_target_pairs={{0,8},{8,16},{16,24},{24,32},{32,40},{40,48},{48,56},{56,64},{64,7... | collective-permute-start | bytes 221192 | tf_op jit(solution)/shard_map/ppermute | solution.py:452
  70.5 26.3 %copy-start.4 = (f32[64,4352]{1,0:T(8,128)S(1)}, f32[64,4352]{1,0:T(8,128)}, u32[]{:S(2)}) copy-start(f32[64,4352]{1,0:T(8,128)} %sol_ref.1) | copy-start | bytes 3342340
  70.5 26.3 %copy-start.5 = (f32[64,55,8]{0,2,1:T(8,128)S(1)}, f32[64,55,8]{0,2,1:T(8,128)}, u32[]{:S(2)}) copy-start(f32[64,55,8]{0,2,1:T(8,128)} %param.25) | copy-start | bytes 337924
  83.3 13.5 %collective-permute-start.3 = (f32[16,8,1152]{2,1,0:T(8,128)S(1)}, f32[16,8,1152]{2,1,0:T(8,128)S(1)}, u32[]{:S(2)}, u32[]{:S(2)}) collective-permute-start(f32[16,8,1152]{2,1,0:T(8,128)S(1)} %all_to_all.28.whole_ref), channel_id=1, source_target_pairs={{0,8},{8,0},{1,9},{9,1},{2,10},{10,2},{3,11},{11,3},{4,12},{12,4},... | collective-permute-start | bytes 1769480 | tf_op jit(solution)/shard_map/ppermute | solution.py:483
